TPU v7x, 32 devices: a whole 2x2x4 slice. The times are simulated.
32 devices in a mesh: groups: 2 (over y), vox: 4 (over z), chan: 2 (over x), frm: 2 (over core).
Axes of the slice: x: 2, y: 2, z: 4, core: 2. Of those that a mesh axis runs over, the one named last changes fastest.
Arguments:
- echo_data: bfloat16 [8, 2, 1024, 2, 512], P(('groups', 'vox'), 'chan', None, None, 'frm'), parts along dimension 0, may hold values from -36 to 36
- tile_weights: bfloat16 [4, 2, 64, 128, 128], P('vox', 'chan'), may hold values from -0.0625 to 0.0625
- tile_target: int32 [4, 2, 64], P('vox', 'chan'), may hold values from 0 to 1
- tile_offset: int32 [4, 2, 64], P('vox', 'chan'), may hold values from 0 to 896
- tile_count: int32 [4, 2], P('vox', 'chan'), may hold values from 8 to 64, as said below
- grid_map: int32 [4, 256], P('vox'), may hold values from 0 to 255, each once within a row
- psf_kernel: float32 [5, 5], replicated, may hold values from -1.25 to 1.25
Outputs:
- psf_image: float32 [64, 32, 512], P(('groups', 'vox'), 'chan', 'frm'), parts along dimension 0
There are 2 independent parts, one for each index of `groups`. A program takes and returns all parts, laid end to end along the dimension named above; an argument that names none is the same for every part. Nothing has to cross between parts.
Inputs may be any that keep to these rules, and one draw needn't show every extreme that they name: `tile_count`: in each voxel block exactly one channel group uses all 64 slots; the others use far fewer. `grid_map`: each block's row is a permutation of 0 to 255.
All inputs are finite; a program needn't handle non-finite values.
Results may differ from a plain program's by a relative error of at most 0.014.
Values may be sent and summed in bfloat16 or wider, within the bound.
No kernel may reach another device: no remote copies, remote signals or barrier semaphores. Data moves between devices by JAX's collectives and lax.ppermute only.
A program may use at most 64 MiB of HBM per device.

v0:
```python
import jax
import jax.numpy as jnp
from jax import lax
from jax.sharding import PartitionSpec as P

TBATCH = 8
LAT_DEV = 8


POLY_COEFFS = (1.0, -0.6, 0.15, -0.03)


def with_halo(shard, sides, width):
    for axis, dim in sides:
        devices, length = (lax.axis_size(axis), shard.shape[dim])
        up = [(i, (i + 1) % devices) for i in range(devices - 1)]
        down = [(j, i) for i, j in up]
        last = lax.slice_in_dim(shard, length - width, length, axis=dim)
        leading = lax.slice_in_dim(shard, 0, width, axis=dim)
        before = lax.ppermute(last, axis, up)
        after = lax.ppermute(leading, axis, down)
        shard = jnp.concatenate([before, shard, after], axis=dim)
    return shard


def complex_times(left_real, left_imag, right_real, right_imag):
    level = lax.Precision.HIGH
    real_part = jnp.dot(
        left_real, right_real, precision=level, preferred_element_type=jnp.float32
    ) - jnp.dot(left_imag, right_imag, precision=level, preferred_element_type=jnp.float32)
    imag_part = jnp.dot(
        left_real, right_imag, precision=level, preferred_element_type=jnp.float32
    ) + jnp.dot(left_imag, right_real, precision=level, preferred_element_type=jnp.float32)
    return (real_part, imag_part)


def tile_pass(flat_echo, weights, tile_goal, tile_start, live_total, tiles_out):
    tile_size = weights.shape[-1]
    col_count = flat_echo.shape[-1]
    slot_count = weights.shape[0]
    lane_ids = jnp.arange(TBATCH, dtype=jnp.int32)
    target_ids = jnp.arange(tiles_out, dtype=jnp.int32)
    zero_index = jnp.zeros((), jnp.int32)

    def cut_rows(offset_id):
        return lax.dynamic_slice(flat_echo, (offset_id, zero_index), (tile_size, col_count))

    def one_turn(turn_index, totals):
        where_at = turn_index * TBATCH + lane_ids
        live_lane = where_at < live_total
        chosen = jnp.minimum(where_at, slot_count - 1)
        picked = weights[chosen]
        samples = jax.vmap(cut_rows)(tile_start[chosen])
        product = jnp.einsum("krs,ksc->krc", picked, samples, preferred_element_type=jnp.float32)
        placing = ((tile_goal[chosen][:, None] == target_ids[None, :]) & live_lane[:, None]).astype(
            jnp.float32
        )
        return totals + jnp.einsum("kt,krc->trc", placing, product)

    start_totals = jnp.zeros((tiles_out, tile_size, col_count), jnp.float32)
    turn_count = (live_total + TBATCH - 1) // TBATCH
    return lax.fori_loop(0, turn_count, one_turn, start_totals)


def shards(echo_data, tile_weights, tile_target, tile_offset, tile_count, grid_map, psf_kernel):
    row_count = echo_data.shape[2]
    half_frames = echo_data.shape[4]
    tile_size = tile_weights.shape[-1]
    slot_count = tile_weights.shape[2]
    voxels = grid_map.shape[1]
    tiles_out = voxels // tile_size
    flat_echo = echo_data.reshape(row_count, 2 * half_frames)
    weights = tile_weights.reshape(slot_count, tile_size, tile_size)
    tile_sums = tile_pass(
        flat_echo,
        weights,
        tile_target.reshape(-1),
        tile_offset.reshape(-1),
        tile_count[0, 0],
        tiles_out,
    )
    arranged = jnp.take(tile_sums.reshape(voxels, 2, half_frames), grid_map[0], axis=0)
    arranged = arranged.reshape(LAT_DEV, voxels // LAT_DEV, 2, half_frames)
    beamformed = lax.psum_scatter(arranged, "chan", scatter_dimension=1, tiled=True).astype(
        jnp.bfloat16
    )
    lat_count = beamformed.shape[0]
    depth_count = beamformed.shape[1]
    cell_count = lat_count * depth_count
    own_frames = beamformed.reshape(cell_count, 2, half_frames)
    all_frames = lax.all_gather(own_frames, "frm", axis=2, tiled=True)
    frames = all_frames.shape[2]
    own_flat = own_frames.reshape(cell_count, 2 * half_frames)
    all_flat = all_frames.reshape(cell_count, 2 * frames)
    gram_block = lax.dot_general(
        own_flat, all_flat, (((0,), (0,)), ((), ())), preferred_element_type=jnp.float32
    )
    gram_real = gram_block[:half_frames, :frames] + gram_block[half_frames:, frames:]
    gram_imag = gram_block[:half_frames, frames:] - gram_block[half_frames:, :frames]
    frame_start = lax.axis_index("frm") * half_frames
    echo_real = all_frames[:, 0, :].astype(jnp.float32)
    echo_imag = all_frames[:, 1, :].astype(jnp.float32)
    energy = jnp.sum(echo_real * echo_real + echo_imag * echo_imag)
    gram_real, gram_imag, trace_value = lax.psum((gram_real, gram_imag, energy), ("vox", "chan"))
    factor = frames / trace_value
    norm_real = factor * gram_real
    norm_imag = factor * gram_imag
    full_real, full_imag = (
        lax.all_gather(norm_real, "frm", axis=0, tiled=True),
        lax.all_gather(norm_imag, "frm", axis=0, tiled=True),
    )
    identity = jnp.eye(frames, dtype=jnp.float32)
    poly_real = POLY_COEFFS[3] * full_real + POLY_COEFFS[2] * identity
    poly_imag = POLY_COEFFS[3] * full_imag
    poly_real, poly_imag = complex_times(poly_real, poly_imag, full_real, full_imag)
    poly_real = poly_real + POLY_COEFFS[1] * identity
    cols_real = lax.dynamic_slice_in_dim(full_real, frame_start, half_frames, 1)
    cols_imag = lax.dynamic_slice_in_dim(full_imag, frame_start, half_frames, 1)
    filter_real, filter_imag = complex_times(poly_real, poly_imag, cols_real, cols_imag)
    filter_real = filter_real + POLY_COEFFS[0] * lax.dynamic_slice_in_dim(
        identity, frame_start, half_frames, 1
    )
    out_real, out_imag = complex_times(echo_real, echo_imag, filter_real, filter_imag)
    envelope = jnp.sqrt(out_real * out_real + out_imag * out_imag + 1e-06)
    envelope = envelope.reshape(lat_count, depth_count, half_frames)
    padded = with_halo(envelope, (("vox", 0), ("chan", 1)), 2)
    psf_image = jnp.zeros_like(envelope)
    for shift_a in range(5):
        for shift_b in range(5):
            psf_image = (
                psf_image
                + psf_kernel[shift_a, shift_b]
                * padded[shift_a : shift_a + lat_count, shift_b : shift_b + depth_count]
            )
    return psf_image


def solution(mesh):
    in_specs = (
        P(("groups", "vox"), "chan", None, None, "frm"),
        P("vox", "chan", None, None, None),
        P("vox", "chan", None),
        P("vox", "chan", None),
        P("vox", "chan"),
        P("vox", None),
        P(),
    )
    out_specs = P(("groups", "vox"), "chan", "frm")
    return jax.shard_map(shards, mesh=mesh, in_specs=in_specs, out_specs=out_specs, check_vma=False)
```

profile of v0, /device:TPU:0, one launch (start us, length us, event | category | flops | bytes accessed | tf_op | source)
XLA Modules:
  0.0 306.3 jit_solution(13649038592146255879)
XLA Ops:
  11.6 120.6 %while.15 = (s32[]{:T(128)}, f32[2,128,512]{2,0,1:T(2,128)S(1)}, s32[]{:T(128)}, s32[64]{0:T(128)S(1)}, s32[]{:T(128)}, /*index=5*/bf16[64,128,128]{2,1,0:T(8,12...) while((s32[]{:T(128)}, f32[2,128,512]{2,0,1:T(2,128)S(1)}, ...), condition=%wide.region_1.2_spmd.clone, body=%wide.region_0.1_spmd.clone.sunk | while | flops 136447088 | bytes 5247770 | solution.py:62
  13.6 2.2 gather_fusion
  15.8 9.3 %while.16 = (s32[]{:T(128)}, bf16[1024,512]{1,0:T(8,128)(2,1)S(1)}, s32[8,2]{0,1:T(2,128)S(1)}, bf16[8,128,512]{2,1,0:T(8,128)(2,1)S(1)}, s32[]{:T(128)}) while((s32[]{:T(128)}, bf16[1024,512]{1,0:T(8,128)(2,1)S(1)}, s32[8,2]{0,1:T(2,128)S(1)}, bf16[8,128,512]{2,1,0:T(8,128)(2,1)S(1)}, s32[]{:T(128)}) %tuple.64), condition=%wide.while_cond, body=%wide.while_body.sunk | while | flops 2 | bytes 262249 | solution.py:46
  28.7 2.2 gather_fusion
  30.9 9.3 %while.16 = (s32[]{:T(128)}, bf16[1024,512]{1,0:T(8,128)(2,1)S(1)}, s32[8,2]{0,1:T(2,128)S(1)}, bf16[8,128,512]{2,1,0:T(8,128)(2,1)S(1)}, s32[]{:T(128)}) while((s32[]{:T(128)}, bf16[1024,512]{1,0:T(8,128)(2,1)S(1)}, s32[8,2]{0,1:T(2,128)S(1)}, bf16[8,128,512]{2,1,0:T(8,128)(2,1)S(1)}, s32[]{:T(128)}) %tuple.64), condition=%wide.while_cond, body=%wide.while_body.sunk | while | flops 2 | bytes 262249 | solution.py:46
  43.8 2.2 gather_fusion
  46.0 9.3 %while.16 = (s32[]{:T(128)}, bf16[1024,512]{1,0:T(8,128)(2,1)S(1)}, s32[8,2]{0,1:T(2,128)S(1)}, bf16[8,128,512]{2,1,0:T(8,128)(2,1)S(1)}, s32[]{:T(128)}) while((s32[]{:T(128)}, bf16[1024,512]{1,0:T(8,128)(2,1)S(1)}, s32[8,2]{0,1:T(2,128)S(1)}, bf16[8,128,512]{2,1,0:T(8,128)(2,1)S(1)}, s32[]{:T(128)}) %tuple.64), condition=%wide.while_cond, body=%wide.while_body.sunk | while | flops 2 | bytes 262249 | solution.py:46
  58.8 2.2 gather_fusion
  61.0 9.3 %while.16 = (s32[]{:T(128)}, bf16[1024,512]{1,0:T(8,128)(2,1)S(1)}, s32[8,2]{0,1:T(2,128)S(1)}, bf16[8,128,512]{2,1,0:T(8,128)(2,1)S(1)}, s32[]{:T(128)}) while((s32[]{:T(128)}, bf16[1024,512]{1,0:T(8,128)(2,1)S(1)}, s32[8,2]{0,1:T(2,128)S(1)}, bf16[8,128,512]{2,1,0:T(8,128)(2,1)S(1)}, s32[]{:T(128)}) %tuple.64), condition=%wide.while_cond, body=%wide.while_body.sunk | while | flops 2 | bytes 262249 | solution.py:46
  76.1 9.3 %while.16 = (s32[]{:T(128)}, bf16[1024,512]{1,0:T(8,128)(2,1)S(1)}, s32[8,2]{0,1:T(2,128)S(1)}, bf16[8,128,512]{2,1,0:T(8,128)(2,1)S(1)}, s32[]{:T(128)}) while((s32[]{:T(128)}, bf16[1024,512]{1,0:T(8,128)(2,1)S(1)}, s32[8,2]{0,1:T(2,128)S(1)}, bf16[8,128,512]{2,1,0:T(8,128)(2,1)S(1)}, s32[]{:T(128)}) %tuple.64), condition=%wide.while_cond, body=%wide.while_body.sunk | while | flops 2 | bytes 262249 | solution.py:46
  91.2 9.3 %while.16 = (s32[]{:T(128)}, bf16[1024,512]{1,0:T(8,128)(2,1)S(1)}, s32[8,2]{0,1:T(2,128)S(1)}, bf16[8,128,512]{2,1,0:T(8,128)(2,1)S(1)}, s32[]{:T(128)}) while((s32[]{:T(128)}, bf16[1024,512]{1,0:T(8,128)(2,1)S(1)}, s32[8,2]{0,1:T(2,128)S(1)}, bf16[8,128,512]{2,1,0:T(8,128)(2,1)S(1)}, s32[]{:T(128)}) %tuple.64), condition=%wide.while_cond, body=%wide.while_body.sunk | while | flops 2 | bytes 262249 | solution.py:46
  106.3 9.3 %while.16 = (s32[]{:T(128)}, bf16[1024,512]{1,0:T(8,128)(2,1)S(1)}, s32[8,2]{0,1:T(2,128)S(1)}, bf16[8,128,512]{2,1,0:T(8,128)(2,1)S(1)}, s32[]{:T(128)}) while((s32[]{:T(128)}, bf16[1024,512]{1,0:T(8,128)(2,1)S(1)}, s32[8,2]{0,1:T(2,128)S(1)}, bf16[8,128,512]{2,1,0:T(8,128)(2,1)S(1)}, s32[]{:T(128)}) %tuple.64), condition=%wide.while_cond, body=%wide.while_body.sunk | while | flops 2 | bytes 262249 | solution.py:46
  121.3 9.3 %while.16 = (s32[]{:T(128)}, bf16[1024,512]{1,0:T(8,128)(2,1)S(1)}, s32[8,2]{0,1:T(2,128)S(1)}, bf16[8,128,512]{2,1,0:T(8,128)(2,1)S(1)}, s32[]{:T(128)}) while((s32[]{:T(128)}, bf16[1024,512]{1,0:T(8,128)(2,1)S(1)}, s32[8,2]{0,1:T(2,128)S(1)}, bf16[8,128,512]{2,1,0:T(8,128)(2,1)S(1)}, s32[]{:T(128)}) %tuple.64), condition=%wide.while_cond, body=%wide.while_body.sunk | while | flops 2 | bytes 262249 | solution.py:46
  135.1 17.3 %reduce-scatter.2.cloned.1.call-done = f32[8,16,2,256]{3,0,2,1:T(8,128)} async-done(((f32[8,32,2,256]{3,0,2,1:T(8,128)}), f32[8,16,2,256]{3,0,2,1:T(8,128)}) %reduce-scatter.2.cloned.1.call-update) | async-done | bytes 262160 | tf_op jit(solution)/shard_map/reduce_scatter | solution.py:84
  158.2 21.4 %psum.21 = f32[]{:T(128)} all-reduce(f32[]{:T(128)} %add_reduce_fusion), channel_id=1, replica_groups=mesh['groups'=2,'vox'=4,'chan'=2,'frm'=2] {'vox','chan'}, use_global_device_ids=true, to_apply=%region_4.5 | all-reduce | flops 1 | bytes 8 | tf_op jit(solution)/shard_map/psum | solution.py:104
  180.3 55.9 %all-reduce.4.cloned.1.call-done = (f32[256,512]{1,0:T(8,128)}, f32[256,512]{1,0:T(8,128)}) async-done(((f32[256,512]{1,0:T(8,128)}, f32[256,512]{1,0:T(8,128)}), (f32[256,512]{1,0:T(8,128)}, f32[256,512]{1,0:T(8,128)})) %all-reduce.4.cloned.1.call-update) | async-done | bytes 1048592 | tf_op jit(solution)/shard_map/psum | solution.py:104
  240.4 6.3 %all-gather.3.cloned.1.call-done = f32[512,512]{1,0:T(8,128)} async-done(((f32[256,512]{1,0:T(8,128)}), f32[512,512]{1,0:T(8,128)}) %all-gather.3.cloned.1.call-update) | async-done | bytes 1048592 | tf_op jit(solution)/shard_map/all_gather | solution.py:109
  246.7 2.7 fusion.38
  249.4 8.9 %all-gather.5.cloned.1.call-done = f32[512,512]{1,0:T(8,128)} async-done(((f32[256,512]{1,0:T(8,128)}), f32[512,512]{1,0:T(8,128)}) %all-gather.5.cloned.1.call-update) | async-done | bytes 1048592 | tf_op jit(solution)/shard_map/all_gather | solution.py:110
  258.4 2.3 fusion.37
  267.6 4.5 %collective-permute-start = (f32[2,16,256]{2,1,0:T(8,128)S(1)}, f32[2,16,256]{2,1,0:T(8,128)S(1)}, u32[]{:S(2)}, u32[]{:S(2)}) collective-permute-start(f32[2,16,256]{2,1,0:T(8,128)S(1)} %bitcast.114), channel_id=1, source_target_pairs={{0,4},{4,8},{8,12},{1,5},{5,9},{9,13},{2,6},{6,10},{10,14},{3,7},{... | collective-permute-start | bytes 98312 | tf_op jit(solution)/shard_map/ppermute | solution.py:20
  273.7 3.6 %collective-permute-start.2 = (f32[12,2,256]{2,1,0:T(2,128)S(1)}, f32[12,2,256]{2,1,0:T(2,128)S(1)}, u32[]{:S(2)}, u32[]{:S(2)}) collective-permute-start(f32[12,2,256]{2,1,0:T(2,128)S(1)} %get-tuple-element.118), channel_id=1, source_target_pairs={{0,2},{1,3},{4,6},{5,7},{8,10},{9,11},{12,14},{13,15},{16,18},{17,... | collective-permute-start | bytes 73736 | tf_op jit(solution)/shard_map/ppermute | solution.py:20
  279.3 3.7 %collective-permute-done.3 = f32[12,2,256]{2,1,0:T(2,128)S(1)} collective-permute-done((f32[12,2,256]{2,1,0:T(2,128)S(1)}, f32[12,2,256]{2,1,0:T(2,128)S(1)}, u32[]{:S(2)}, u32[]{:S(2)}) %collective-permute-start.3) | collective-permute-done | bytes 24608 | tf_op jit(solution)/shard_map/ppermute | solution.py:21
  283.1 16.6 %fusion.62 = f32[8,16,256]{2,1,0:T(8,128)} fusion(f32[8,16,256]{2,1,0:T(8,128)S(1)} %bitcast.106, f32[2,16,256]{2,1,0:T(8,128)S(1)} %collective-permute-done.1, f32[2,16,256]{2,1,0:T(8,128)S(1)} %collective-permute-done, f32[12,18,256]{2,1,0:T(8,128)S(1)} %get-tuple-element.117, f32[12,18,256]{2,1,0:T(8,128)S(1)} %get-tuple-element.116, f32[]{:T(128)} %bitcast.38, ...), kind=kLoop, calls=%fused_computation.80 | loop fusion | flops 1736704 | bytes 2949220 | tf_op jit(solution)/shard_map/add | solution.py:131
  (339 shorter events, 137.1 us)
Async XLA Ops:
  6.5 5.0 %copy-start.1 = (s32[1,1,64]{2,1,0:T(1,128)S(1)}, s32[1,1,64]{2,1,0:T(1,128)}, u32[]{:S(2)}) copy-start(s32[1,1,64]{2,1,0:T(1,128)} %param.12) | copy-start | bytes 772
  6.5 5.1 %copy-start = (s32[1,1,64]{2,1,0:T(1,128)S(1)}, s32[1,1,64]{2,1,0:T(1,128)}, u32[]{:S(2)}) copy-start(s32[1,1,64]{2,1,0:T(1,128)} %param.11) | copy-start | bytes 772
  6.5 145.9 %reduce-scatter.2.cloned.1.call-start = ((), (), s32[]{:S(2)}) async-start(), calls=%async_computation.1 | async-start | bytes 786432 | tf_op jit(solution)/shard_map/reduce_scatter | solution.py:84
  135.1 101.2 %all-reduce.4.cloned.1.call-start = ((), (), s32[]{:S(2)}) async-start(), calls=%async_computation.4 | async-start | bytes 2097152 | tf_op jit(solution)/shard_map/psum | solution.py:104
  157.5 89.3 %all-gather.3.cloned.1.call-start = ((), (), s32[]{:S(2)}) async-start(), calls=%async_computation.2 | async-start | bytes 1572864 | tf_op jit(solution)/shard_map/all_gather | solution.py:109
  238.2 20.2 %all-gather.5.cloned.1.call-start = ((), (), s32[]{:S(2)}) async-start(), calls=%async_computation.3 | async-start | bytes 1572864 | tf_op jit(solution)/shard_map/all_gather | solution.py:110
  246.7 11.6 %copy-start.2 = (f32[512,512]{1,0:T(8,128)S(1)}, f32[512,512]{1,0:T(8,128)}, u32[]{:S(2)}) copy-start(f32[512,512]{1,0:T(8,128)} %all-gather.3.cloned.1.call-done) | copy-start | bytes 3145732
  258.4 2.3 copy-start.3
  265.5 6.7 %copy-start.4 = (f32[5,5]{1,0:T(8,128)S(1)}, f32[5,5]{1,0:T(8,128)}, u32[]{:S(2)}) copy-start(f32[5,5]{1,0:T(8,128)} %param.15) | copy-start | bytes 304
  266.3 6.6 %collective-permute-start.1 = (f32[2,16,256]{2,1,0:T(8,128)S(1)}, f32[2,16,256]{2,1,0:T(8,128)S(1)}, u32[]{:S(2)}, u32[]{:S(2)}) collective-permute-start(f32[2,16,256]{2,1,0:T(8,128)S(1)} %bitcast.115), channel_id=1, source_target_pairs={{4,0},{8,4},{12,8},{5,1},{9,5},{13,9},{6,2},{10,6},{14,10},{7,3},{... | collective-permute-start | bytes 98312 | tf_op jit(solution)/shard_map/ppermute | solution.py:21
  267.6 6.1 %collective-permute-start = (f32[2,16,256]{2,1,0:T(8,128)S(1)}, f32[2,16,256]{2,1,0:T(8,128)S(1)}, u32[]{:S(2)}, u32[]{:S(2)}) collective-permute-start(f32[2,16,256]{2,1,0:T(8,128)S(1)} %bitcast.114), channel_id=1, source_target_pairs={{0,4},{4,8},{8,12},{1,5},{5,9},{9,13},{2,6},{6,10},{10,14},{3,7},{... | collective-permute-start | bytes 98312 | tf_op jit(solution)/shard_map/ppermute | solution.py:20
  273.7 5.6 %collective-permute-start.2 = (f32[12,2,256]{2,1,0:T(2,128)S(1)}, f32[12,2,256]{2,1,0:T(2,128)S(1)}, u32[]{:S(2)}, u32[]{:S(2)}) collective-permute-start(f32[12,2,256]{2,1,0:T(2,128)S(1)} %get-tuple-element.118), channel_id=1, source_target_pairs={{0,2},{1,3},{4,6},{5,7},{8,10},{9,11},{12,14},{13,15},{16,18},{17,... | collective-permute-start | bytes 73736 | tf_op jit(solution)/shard_map/ppermute | solution.py:20
  277.4 5.7 %collective-permute-start.3 = (f32[12,2,256]{2,1,0:T(2,128)S(1)}, f32[12,2,256]{2,1,0:T(2,128)S(1)}, u32[]{:S(2)}, u32[]{:S(2)}) collective-permute-start(f32[12,2,256]{2,1,0:T(2,128)S(1)} %get-tuple-element.119), channel_id=1, source_target_pairs={{2,0},{3,1},{6,4},{7,5},{10,8},{11,9},{14,12},{15,13},{18,16},{19,... | collective-permute-start | bytes 73736 | tf_op jit(solution)/shard_map/ppermute | solution.py:21
Sparse Core Ops, SparseCore 0:
  135.2 17.2 reduce-scatter.1
  157.6 78.6 all-reduce.3
  238.3 8.4 all-gather.2
  248.1 10.1 all-gather.4
where the time goes:
time: 307 us; the launch traced here: 306 us
  local copies, waits for them, and re-layouts  107 us (35%)
  waiting for transfers between devices  93.2 us (30%)
  other arithmetic  31.9 us (10%)
  blocking collectives  23.4 us (8%)
  matrix products  23.2 us (8%)
  between operations  14.8 us (5%)
  starting transfers between devices  11.1 us (4%)
    gather x192, local copies, waits for them, and re-layouts  73 us
    psum x1, waiting for transfers between devices, shards(): lax.psum((gram_real, gram_imag, energy), ('vox', 'chan'))  55.9 us
    psum x1, blocking collectives, shards(): lax.psum((gram_real, gram_imag, energy), ('vox', 'chan'))  21.4 us
    gather x8, local copies, waits for them, and re-layouts, one_turn(): picked = weights[chosen]  17.5 us
    reduce_scatter x1, waiting for transfers between devices, shards(): lax.psum_scatter(arranged, 'chan', scatter_dimension=1, tiled=True)  17.3 us
    add x1, other arithmetic, shards(): psf_image + psf_kernel[shift_a, shift_b] * padded[shift_a:shift_a + lat_c...  16.6 us
    all_gather x1, waiting for transfers between devices, shards(): lax.all_gather(norm_imag, 'frm', axis=0, tiled=True)  8.93 us
    dot_general x8, matrix products, one_turn(): return totals + jnp.einsum('kt,krc->trc', placing, product)  8.92 us
  transfers between devices with their start and end apart: 8, of which 6 were waited for; matrix products, arithmetic and copies ran while one was open for 2% of the time, Pallas kernels for 0%

commit v1 on v0

v1 whole, which is shorter than its diff:
```python
import functools

import jax
import jax.numpy as jnp
from jax import lax
from jax.experimental import pallas as pl
from jax.experimental.pallas import tpu as pltpu
from jax.sharding import PartitionSpec as P

POLY_COEFFS = (1.0, -0.6, 0.15, -0.03)
HALO = 2
BATCH = 4
EDGE = 4
VMEM_LIMIT = 56 * 2**20
F32 = jnp.float32
BF16 = jnp.bfloat16


def split(x):
    high = x.astype(BF16)
    return high, (x - high.astype(F32)).astype(BF16)


def dot(a, b, dims=((1,), (0,))):
    return lax.dot_general(a, b, (dims, ((), ())), preferred_element_type=F32)


def das_kernel(
    count, target, offset, echo, weights, grid_map, own_out, send_out, dense, arranged, *, chans, lat
):
    slots, tile = weights.shape[0], weights.shape[1]
    voxels = grid_map.shape[1]
    tiles_out = voxels // tile
    spans = echo.shape[0] // tile
    live = count[0]
    dense[...] = jnp.zeros_like(dense)
    lanes = lax.broadcasted_iota(jnp.int32, (tile, tile), 1)

    def one_batch(turn, carry):
        for lane in range(BATCH):
            at = turn * BATCH + lane
            slot = jnp.minimum(at, slots - 1)
            goal = jnp.where(at < live, target[slot], tiles_out)
            first = offset[slot]
            span, shift = first // tile, first % tile
            turned = pltpu.roll(weights[slot].astype(F32), shift, 1)
            dense[goal, span] += jnp.where(lanes >= shift, turned, 0.0)
            dense[goal, span + 1] += jnp.where(lanes < shift, turned, 0.0)
        return carry

    lax.fori_loop(0, (live + BATCH - 1) // BATCH, one_batch, 0)

    rows = []
    for t in range(tiles_out):
        rows.append(jnp.concatenate([dense[t, s] for s in range(spans)], axis=1))
    high, low = split(jnp.concatenate(rows, axis=0))
    data = echo[...]
    sums = dot(high, data) + dot(low, data)
    voxel_ids = lax.broadcasted_iota(jnp.int32, (voxels, voxels), 0)
    placing = (voxel_ids == grid_map[...]).astype(F32).astype(BF16)
    high, low = split(sums)
    arranged[...] = dot(placing, high, ((0,), (0,))) + dot(placing, low, ((0,), (0,)))
    depth = voxels // lat
    width = depth // chans
    mine = lax.axis_index("chan")
    for a in range(lat):
        for step in range(chans):
            first = pl.multiple_of(a * depth + (mine ^ step) * width, 8)
            rows = arranged[pl.ds(first, width), :]
            if step == 0:
                own_out[a * width : (a + 1) * width, :] = rows
            else:
                send_out[step - 1, a * width : (a + 1) * width, :] = rows.astype(BF16)


def gram_parts(a, b):
    con = ((0,), (0,))
    return [dot(a, a, con), dot(a, b, con), dot(b, b, con)]


def gram_kernel(*refs):
    out = refs[-1]
    count = (len(refs) - 1) // 2
    a = jnp.concatenate([r[...] for r in refs[:count]], axis=0)
    b = jnp.concatenate([r[...] for r in refs[count : 2 * count]], axis=0)
    for i, t in enumerate(gram_parts(a, b)):
        out[i] = t


def filter_kernel(psf, gram, *refs, fresh, inner, chans, lat, width, vox_total, frames):
    total_blocks = (len(refs) - 5) // 2
    mine = refs[:total_blocks]
    other = refs[total_blocks : 2 * total_blocks]
    out, stack_a, stack_b, mat_high, mat_low = refs[2 * total_blocks :]
    n = lat * width
    half = mine[0].shape[1]
    hf = half // 2
    vox = lax.axis_index("vox")
    chan = lax.axis_index("chan")
    for i in range(total_blocks):
        stack_a[i] = mine[i][...]
        stack_b[i] = other[i][...]
    parts = [gram[i] for i in range(3)]
    if fresh:
        first = total_blocks - fresh
        a = stack_a[first:].reshape(fresh * n, half)
        b = stack_b[first:].reshape(fresh * n, half)
        parts = [p + t for p, t in zip(parts, gram_parts(a, b))]

    def diag_sum(t):
        r = lax.broadcasted_iota(jnp.int32, t.shape, 0)
        c = lax.broadcasted_iota(jnp.int32, t.shape, 1)
        return jnp.sum(jnp.where(r == c, t, 0.0))

    factor = frames / (diag_sum(parts[0]) + diag_sum(parts[2]))
    for i, t in enumerate(parts):
        real = factor * (t[:hf, :hf] + t[hf:, hf:])
        imag = factor * (t[:hf, hf:] - t[hf:, :hf])
        real_high, real_low = split(real)
        imag_high, imag_low = split(imag)
        for ref, re, im in ((mat_high, real_high, imag_high), (mat_low, real_low, imag_low)):
            ref[i, :hf, :hf] = re
            ref[i, hf:, hf:] = re
            ref[i, :hf, hf:] = im
            ref[i, hf:, :hf] = -im

    def place(v):
        away = vox ^ v
        return jnp.where(away >= inner // 2, inner // 2 + (away ^ (inner - 1)), away)

    edge = HALO * width
    if vox_total > inner:
        above, below = inner * chans, (inner + 1) * chans
    else:
        above = place(jnp.maximum(vox - 1, 0)) * chans
        below = place(jnp.minimum(vox + 1, vox_total - 1)) * chans

    def column(stack, away):
        return jnp.concatenate(
            [
                stack[above + away, n - edge :, :],
                stack[away],
                stack[below + away, :edge, :],
            ],
            axis=0,
        )

    rows = (lat + 2 * HALO) * width
    lat_all = lat + 2 * HALO
    pr = lax.broadcasted_iota(jnp.int32, (lat_all * EDGE, rows), 0)
    pc = lax.broadcasted_iota(jnp.int32, (lat_all * EDGE, rows), 1)
    x_rows = [[column(stack_a, 0)], [column(stack_b, 0)]]
    sides = [-1, 1] if chans > 2 else [0]
    side_start = []
    for side in sides:
        if side == 0:
            away = 1
            start = jnp.where(chan == 0, 0, width - EDGE)
            base = jnp.where(chan == 0, width, 0) + start
        else:
            near = jnp.clip(chan + side, 0, chans - 1)
            away = chan ^ near
            start = 0 if side == 1 else width - EDGE
            base = near * width + start
            base = jnp.where(near == chan, -(10**6), base)
        pick = ((pr // EDGE == pc // width) & (pc % width == start + pr % EDGE)).astype(F32).astype(BF16)
        for which, stack in enumerate((stack_a, stack_b)):
            x_rows[which].append(dot(pick, column(stack, away)).astype(BF16))
        side_start.append(base)
    xa, xb = (jnp.concatenate(x, axis=0) for x in x_rows)

    def times(za, zb, last):
        m = [(mat_high[i], mat_low[i]) for i in range(3)]
        (ah, al), (bh, bl) = split(za), split(zb)
        back = ((1,), (1,))

        def product(h, l, mat, dims):
            return dot(h, mat[0], dims) + dot(l, mat[0], dims) + dot(h, mat[1], dims)

        fwd = ((1,), (0,))
        new_a = product(ah, al, m[0], fwd) + product(bh, bl, m[1], back)
        if last:
            return new_a, None
        return new_a, product(ah, al, m[1], fwd) + product(bh, bl, m[2], fwd)

    fa, fb = xa.astype(F32), xb.astype(F32)
    za, zb = POLY_COEFFS[3] * fa, POLY_COEFFS[3] * fb
    for degree in (2, 1, 0):
        za, zb = times(za, zb, degree == 0)
        za = za + POLY_COEFFS[degree] * fa
        if degree:
            zb = zb + POLY_COEFFS[degree] * fb
    env = jnp.sqrt(za[:, :hf] * za[:, :hf] + za[:, hf:] * za[:, hf:] + 1e-06)

    total = env.shape[0]
    outs = lax.broadcasted_iota(jnp.int32, (n, total), 0)
    ins = lax.broadcasted_iota(jnp.int32, (n, total), 1)
    lat_in = ins // width
    dep_in = chan * width + ins % width
    for s, base in enumerate(side_start):
        local = ins - rows - s * lat_all * EDGE
        here = local >= 0
        lat_in = jnp.where(here, local // EDGE, lat_in)
        dep_in = jnp.where(here, base + local % EDGE, dep_in)
    tap_a = lat_in - outs // width
    tap_b = dep_in - (chan * width + outs % width) + HALO
    lat_grid = vox * lat + lat_in - HALO
    inside = (lat_grid >= 0) & (lat_grid < vox_total * lat)
    tap = jnp.where(
        inside & (tap_a >= 0) & (tap_a < 5) & (tap_b >= 0) & (tap_b < 5), tap_a * 5 + tap_b, -1
    )
    mix = jnp.zeros((n, total), F32)
    for i in range(5):
        for j in range(5):
            mix = jnp.where(tap == i * 5 + j, psf[i, j], mix)
    mh, ml = split(mix)
    eh, el = split(env)
    out[...] = dot(mh, eh) + dot(ml, eh) + dot(mh, el)


def shards(mesh, echo_data, tile_weights, tile_target, tile_offset, tile_count, grid_map, psf_kernel):
    rows, hf = echo_data.shape[2], echo_data.shape[4]
    slots, tile = tile_weights.shape[2], tile_weights.shape[3]
    voxels = grid_map.shape[1]
    chans, vox_total, frms = mesh.shape["chan"], mesh.shape["vox"], mesh.shape["frm"]
    lat = 8
    width = voxels // lat // chans
    n = lat * width
    smem = pl.BlockSpec(memory_space=pltpu.SMEM)
    vmem = pl.BlockSpec(memory_space=pltpu.VMEM)
    echo = echo_data.reshape(rows, 2 * hf)
    own, sent = pl.pallas_call(
        functools.partial(das_kernel, chans=chans, lat=lat),
        out_shape=(
            jax.ShapeDtypeStruct((n, 2 * hf), F32),
            jax.ShapeDtypeStruct((chans - 1, n, 2 * hf), BF16),
        ),
        in_specs=[smem, smem, smem, vmem, vmem, vmem],
        out_specs=(vmem, vmem),
        scratch_shapes=[
            pltpu.VMEM((voxels // tile + 1, rows // tile + 1, tile, tile), F32),
            pltpu.VMEM((voxels, 2 * hf), F32),
        ],
        compiler_params=pltpu.CompilerParams(vmem_limit_bytes=VMEM_LIMIT),
    )(
        tile_count.reshape(-1),
        tile_target.reshape(-1),
        tile_offset.reshape(-1),
        echo,
        tile_weights.reshape(slots, tile, tile),
        grid_map,
    )
    inner = min(vox_total, 4)

    def peer(x, dv, dc):
        pairs = [
            (v * chans + c, (v ^ dv) * chans + (c ^ dc))
            for v in range(vox_total)
            for c in range(chans)
        ]
        return lax.ppermute(x, ("vox", "chan"), pairs)

    for step in range(1, chans):
        own = own + peer(sent[step - 1], 0, step).astype(F32)
    own = own.astype(BF16)
    crossed = peer(own, inner - 1, 0)
    near = [(dv, dc) for dv in range(inner // 2) for dc in range(chans)]
    mine = [own] + [peer(own, dv, dc) for dv, dc in near[1:]]
    mine += [crossed] + [peer(crossed, dv, dc) for dv, dc in near[1:]]

    def to_other(x):
        return lax.ppermute(x, "frm", [(f, f ^ 1) for f in range(frms)])

    other = [to_other(x) for x in mine]
    groups = inner * chans
    part = groups // 2

    def gram_of(a, b):
        cost = pl.CostEstimate(
            flops=6 * len(a) * n * (2 * hf) ** 2, bytes_accessed=12 * (2 * hf) ** 2, transcendentals=0
        )
        return pl.pallas_call(
            gram_kernel,
            out_shape=jax.ShapeDtypeStruct((3, 2 * hf, 2 * hf), F32),
            in_specs=[vmem] * (2 * len(a)),
            out_specs=vmem,
            cost_estimate=cost,
            compiler_params=pltpu.CompilerParams(vmem_limit_bytes=VMEM_LIMIT),
        )(*a, *b)

    gram = gram_of(mine[:part], other[:part])
    fresh = groups - part
    if vox_total > inner:
        gram = gram + gram_of(mine[part:], other[part:])
        fresh = 0
        away = inner
        while away < vox_total:
            gram = gram + peer(gram, away, 0)
            away *= 2
        for go in (1, -1):
            pairs = [(v, v + go) for v in range(vox_total) if 0 <= v + go < vox_total]
            mine += [lax.ppermute(x, "vox", pairs) for x in mine[:chans]]
            other += [lax.ppermute(x, "vox", pairs) for x in other[:chans]]
    blocks = len(mine)
    out = pl.pallas_call(
        functools.partial(
            filter_kernel,
            fresh=fresh,
            inner=inner,
            chans=chans,
            lat=lat,
            width=width,
            vox_total=vox_total,
            frames=float(frms * hf),
        ),
        out_shape=jax.ShapeDtypeStruct((n, hf), F32),
        in_specs=[smem, vmem] + [vmem] * (2 * blocks),
        out_specs=vmem,
        scratch_shapes=[
            pltpu.VMEM((blocks, n, 2 * hf), BF16),
            pltpu.VMEM((blocks, n, 2 * hf), BF16),
            pltpu.VMEM((3, 2 * hf, 2 * hf), BF16),
            pltpu.VMEM((3, 2 * hf, 2 * hf), BF16),
        ],
        compiler_params=pltpu.CompilerParams(vmem_limit_bytes=VMEM_LIMIT),
    )(psf_kernel, gram, *mine, *other)
    return out.reshape(lat, width, hf)


def solution(mesh):
    in_specs = (
        P(("groups", "vox"), "chan", None, None, "frm"),
        P("vox", "chan", None, None, None),
        P("vox", "chan", None),
        P("vox", "chan", None),
        P("vox", "chan"),
        P("vox", None),
        P(),
    )
    out_specs = P(("groups", "vox"), "chan", "frm")
    return jax.shard_map(
        functools.partial(shards, mesh),
        mesh=mesh,
        in_specs=in_specs,
        out_specs=out_specs,
        check_vma=False,
    )
```

time: 307 us -> 52.4 us (0.17)
  local copies, waits for them, and re-layouts: 107 us -> 4.99 us
  waiting for transfers between devices: 93.2 us -> 14.2 us
  other arithmetic: 31.9 us -> 0.98 us
  blocking collectives: 23.4 us -> 0 us
  matrix products: 23.2 us -> 0 us
  Pallas kernels: 0 us -> 18.8 us
  between operations: 14.8 us -> 0.8 us
    gather x217 -> x0, local copies, waits for them, and re-layouts: 102 us -> none
    psum x1 -> x0, waiting for transfers between devices: 55.9 us -> none  [shards(): lax.psum((gram_real, gram_imag, energy), ('vox', 'chan'))]
    dot_general x29 -> x0, matrix products: 23.2 us -> none  [the longest x8 8.92 us: one_turn(): return totals + jnp.einsum('kt,krc->trc', placing, product)]
    psum x1 -> x0, blocking collectives: 21.4 us -> none  [shards(): lax.psum((gram_real, gram_imag, energy), ('vox', 'chan'))]
    pallas_call x0 -> x3, Pallas kernels: none -> 18.8 us  [the longest x1 9.13 us: shards(): pl.pallas_call(functools.partial(filter_kernel, fresh=fresh, inner=inner,...]
    reduce_scatter x1 -> x0, waiting for transfers between devices: 17.3 us -> none  [shards(): lax.psum_scatter(arranged, 'chan', scatter_dimension=1, tiled=True)]
    add x1 -> x0, other arithmetic: 16.6 us -> none  [shards(): psf_image + psf_kernel[shift_a, shift_b] * padded[shift_a:shift_a + lat_c...]
    all_gather x2 -> x0, waiting for transfers between devices: 15.3 us -> none  [the longest x1 8.93 us: shards(): lax.all_gather(norm_imag, 'frm', axis=0, tiled=True)]
  transfers between devices with their start and end apart: 8 -> 16, of which waited for: 6 -> 8; matrix products, arithmetic and copies ran while one was open for 2% -> 0% of each run, Pallas kernels for 0% -> 8%
where the time goes in v1:
time: 52.4 us; the launch traced here: 52 us
  Pallas kernels  18.8 us (36%)
  waiting for transfers between devices  14.2 us (27%)
  starting transfers between devices  12.2 us (23%)
  local copies, waits for them, and re-layouts  4.99 us (10%)
  other arithmetic  0.98 us (2%)
  between operations  0.8 us (2%)
    ppermute x8, waiting for transfers between devices, peer(): return lax.ppermute(x, ('vox', 'chan'), pairs)  14.2 us
    ppermute x8, starting transfers between devices, peer(): return lax.ppermute(x, ('vox', 'chan'), pairs)  11.6 us
    pallas_call x1, Pallas kernels, shards(): pl.pallas_call(functools.partial(filter_kernel, fresh=fresh, inner=inner,...  9.13 us
    pallas_call x1, Pallas kernels, shards(): pl.pallas_call(functools.partial(das_kernel, chans=chans, lat=lat), out_s...  5.74 us
    unnamed x33, local copies, waits for them, and re-layouts  4.99 us
    pallas_call x1, Pallas kernels, gram_of(): pl.pallas_call(gram_kernel, out_shape=jax.ShapeDtypeStruct((3, 2 * hf, 2...  3.93 us
  transfers between devices with their start and end apart: 16, of which 8 were waited for; matrix products, arithmetic and copies ran while one was open for 0% of the time, Pallas kernels for 8%

profile of v1, /device:TPU:0, one launch (start us, length us, event | category | flops | bytes accessed | tf_op | source)
XLA Modules:
  0.0 52.0 jit_solution(9015636840210782057)
XLA Ops:
  0.7 2.4 %copy.8 = bf16[128,8,2,256]{3,1,2,0:T(8,128)(2,1)} copy(bf16[128,8,2,256]{3,2,1,0:T(2,128)(2,1)} %bitcast.12) | data formatting | bytes 2097152
  3.1 5.7 %shard_map.73 = (f32[128,512]{1,0:T(8,128)}, bf16[1,128,512]{2,1,0:T(8,128)(2,1)}) custom-call(s32[1]{0:T(128)} %bitcast.9.count, s32[64]{0:T(128)} %bitcast.13, s32[64]{0:T(128)} %bitcast.14, bf16[1024,512]{1,0:T(8,128)(2,1)} %bitcast.10, bf16[64,128,128]{2,1,0:T(8,128)(2,1)} %bitcast.11, s32[1,256]{1,0:T(1,128)} %grid_map.1), custom_call_target="tpu_custom_call" | custom-call | tf_op jit(solution)/shard_map/pallas_call | solution.py:232
  8.8 1.2 %collective-permute-start = (bf16[128,512]{1,0:T(8,128)(2,1)}, bf16[128,512]{1,0:T(8,128)(2,1)S(1)}, u32[]{:S(2)}, u32[]{:S(2)}) collective-permute-start(bf16[128,512]{1,0:T(8,128)(2,1)} %bitcast.15), channel_id=1, source_target_pairs={{0,2},{2,0},{4,6},{6,4},{8,10},{10,8},{12,14},{14,12},{1,3},{3,1},... | collective-permute-start | bytes 393224 | tf_op jit(solution)/shard_map/ppermute | solution.py:261
  10.0 4.9 %collective-permute-done = bf16[128,512]{1,0:T(8,128)(2,1)S(1)} collective-permute-done((bf16[128,512]{1,0:T(8,128)(2,1)}, bf16[128,512]{1,0:T(8,128)(2,1)S(1)}, u32[]{:S(2)}, u32[]{:S(2)}) %collective-permute-start) | collective-permute-done | bytes 131104 | tf_op jit(solution)/shard_map/ppermute | solution.py:261
  14.9 1.0 %add_convert_fusion.refs_0_ = bf16[128,512]{1,0:T(8,128)(2,1)S(1)} fusion(f32[128,512]{1,0:T(8,128)} %get-tuple-element.7, bf16[128,512]{1,0:T(8,128)(2,1)S(1)} %collective-permute-done), kind=kLoop, calls=%fused_computation | loop fusion | flops 196608 | bytes 524288 | tf_op jit(solution)/shard_map/convert_element_type | solution.py:265
  15.9 4.5 %collective-permute-start.8 = (bf16[128,512]{1,0:T(8,128)(2,1)S(1)}, bf16[128,512]{1,0:T(8,128)(2,1)S(1)}, u32[]{:S(2)}, u32[]{:S(2)}) collective-permute-start(bf16[128,512]{1,0:T(8,128)(2,1)S(1)} %add_convert_fusion.refs_0_), channel_id=1, source_target_pairs={{0,12},{2,14},{4,8},{6,10},{8,4},{10,6},{12,0},{14,2},{1,13},{3,15... | collective-permute-start | bytes 393224 | tf_op jit(solution)/shard_map/ppermute | solution.py:261
  20.4 0.5 collective-permute-start.3
  20.9 1.3 %collective-permute-start.2 = (bf16[128,512]{1,0:T(8,128)(2,1)S(1)}, bf16[128,512]{1,0:T(8,128)(2,1)S(1)}, u32[]{:S(2)}, u32[]{:S(2)}) collective-permute-start(bf16[128,512]{1,0:T(8,128)(2,1)S(1)} %add_convert_fusion.refs_0_), channel_id=1, source_target_pairs={{0,4},{2,6},{4,0},{6,2},{8,12},{10,14},{12,8},{14,10},{1,5},{3,7},... | collective-permute-start | bytes 393224 | tf_op jit(solution)/shard_map/ppermute | solution.py:261
  22.1 1.7 %collective-permute-start.1 = (bf16[128,512]{1,0:T(8,128)(2,1)S(1)}, bf16[128,512]{1,0:T(8,128)(2,1)S(1)}, u32[]{:S(2)}, u32[]{:S(2)}) collective-permute-start(bf16[128,512]{1,0:T(8,128)(2,1)S(1)} %add_convert_fusion.refs_0_), channel_id=1, source_target_pairs={{0,2},{2,0},{4,6},{6,4},{8,10},{10,8},{12,14},{14,12},{1,3},{3,1},... | collective-permute-start | bytes 393224 | tf_op jit(solution)/shard_map/ppermute | solution.py:261
  23.9 0.4 collective-permute-done.8.refs_4_
  24.3 2.1 %collective-permute-start.11 = (bf16[128,512]{1,0:T(8,128)(2,1)S(1)}, bf16[128,512]{1,0:T(8,128)(2,1)S(1)}, u32[]{:S(2)}, u32[]{:S(2)}) collective-permute-start(bf16[128,512]{1,0:T(8,128)(2,1)S(1)} %collective-permute-done.8.refs_4_), channel_id=1, source_target_pairs={{0,6},{2,4},{4,2},{6,0},{8,14},{10,12},{12,10},{14,8},{1,7},{3,5},... | collective-permute-start | bytes 393224 | tf_op jit(solution)/shard_map/ppermute | solution.py:261
  26.3 1.3 %collective-permute-done.3.refs_3_ = bf16[128,512]{1,0:T(8,128)(2,1)S(1)} collective-permute-done((bf16[128,512]{1,0:T(8,128)(2,1)S(1)}, bf16[128,512]{1,0:T(8,128)(2,1)S(1)}, u32[]{:S(2)}, u32[]{:S(2)}) %collective-permute-start.3) | collective-permute-done | bytes 131104 | tf_op jit(solution)/shard_map/ppermute | solution.py:261
  28.0 1.9 %collective-permute-done.2.refs_2_ = bf16[128,512]{1,0:T(8,128)(2,1)S(1)} collective-permute-done((bf16[128,512]{1,0:T(8,128)(2,1)S(1)}, bf16[128,512]{1,0:T(8,128)(2,1)S(1)}, u32[]{:S(2)}, u32[]{:S(2)}) %collective-permute-start.2) | collective-permute-done | bytes 131104 | tf_op jit(solution)/shard_map/ppermute | solution.py:261
  29.9 0.6 %collective-permute-done.1.refs_1_ = bf16[128,512]{1,0:T(8,128)(2,1)S(1)} collective-permute-done((bf16[128,512]{1,0:T(8,128)(2,1)S(1)}, bf16[128,512]{1,0:T(8,128)(2,1)S(1)}, u32[]{:S(2)}, u32[]{:S(2)}) %collective-permute-start.1) | collective-permute-done | bytes 131104 | tf_op jit(solution)/shard_map/ppermute | solution.py:261
  30.5 2.8 %collective-permute-done.11.refs_7_ = bf16[128,512]{1,0:T(8,128)(2,1)S(1)} collective-permute-done((bf16[128,512]{1,0:T(8,128)(2,1)S(1)}, bf16[128,512]{1,0:T(8,128)(2,1)S(1)}, u32[]{:S(2)}, u32[]{:S(2)}) %collective-permute-start.11) | collective-permute-done | bytes 131104 | tf_op jit(solution)/shard_map/ppermute | solution.py:261
  33.3 1.5 %collective-permute-done.10.refs_6_ = bf16[128,512]{1,0:T(8,128)(2,1)S(1)} collective-permute-done((bf16[128,512]{1,0:T(8,128)(2,1)S(1)}, bf16[128,512]{1,0:T(8,128)(2,1)S(1)}, u32[]{:S(2)}, u32[]{:S(2)}) %collective-permute-start.10) | collective-permute-done | bytes 131104 | tf_op jit(solution)/shard_map/ppermute | solution.py:261
  34.8 0.9 %collective-permute-done.9.refs_5_ = bf16[128,512]{1,0:T(8,128)(2,1)S(1)} collective-permute-done((bf16[128,512]{1,0:T(8,128)(2,1)S(1)}, bf16[128,512]{1,0:T(8,128)(2,1)S(1)}, u32[]{:S(2)}, u32[]{:S(2)}) %collective-permute-start.9) | collective-permute-done | bytes 131104 | tf_op jit(solution)/shard_map/ppermute | solution.py:261
  35.6 0.5 collective-permute-start.14
  36.3 0.5 copy-done.6
  36.8 0.6 %copy-done.7 = bf16[128,512]{1,0:T(8,128)(2,1)} copy-done((bf16[128,512]{1,0:T(8,128)(2,1)}, bf16[128,512]{1,0:T(8,128)(2,1)S(1)}, u32[]{:S(2)}) %copy-start.7) | copy-done | bytes 131096
  37.5 3.9 %shard_map.74.gram = f32[3,512,512]{2,1,0:T(8,128)} custom-call(bf16[128,512]{1,0:T(8,128)(2,1)} %copy-done, bf16[128,512]{1,0:T(8,128)(2,1)} %copy-done.4, bf16[128,512]{1,0:T(8,128)(2,1)} %copy-done.3, bf16[128,512]{1,0:T(8,128)(2,1)} %copy-done.2, bf16[128,512]{1,0:T(8,128)(2,1)} %copy-done.1, bf16[128,512]{1,0:T(8,128)(2,1)} %copy-done.7, ...), custom_call_target="tpu_custom_call" | custom-call | flops 805306368 | bytes 3145728 | tf_op jit(solution)/shard_map/pallas_call | solution.py:282
  41.5 0.6 %copy-done.12 = bf16[128,512]{1,0:T(8,128)(2,1)} copy-done((bf16[128,512]{1,0:T(8,128)(2,1)}, bf16[128,512]{1,0:T(8,128)(2,1)S(1)}, u32[]{:S(2)}) %copy-start.12) | copy-done | bytes 131096
  42.2 0.7 %copy-done.15 = bf16[128,512]{1,0:T(8,128)(2,1)} copy-done((bf16[128,512]{1,0:T(8,128)(2,1)}, bf16[128,512]{1,0:T(8,128)(2,1)S(1)}, u32[]{:S(2)}) %copy-start.15) | copy-done | bytes 131096
  42.8 9.1 %shard_map.75 = f32[128,256]{1,0:T(8,128)} custom-call(f32[5,5]{1,0:T(8,128)} %psf.1, f32[3,512,512]{2,1,0:T(8,128)} %shard_map.74.gram, bf16[128,512]{1,0:T(8,128)(2,1)} %copy-done, bf16[128,512]{1,0:T(8,128)(2,1)} %copy-done.4, bf16[128,512]{1,0:T(8,128)(2,1)} %copy-done.3, bf16[128,512]{1,0:T(8,128)(2,1)} %copy-done.2, bf16[128,512]{1,0:T(8,128)(2,1)} %copy-done.8, ...), custom_call_target="tpu_custom_call" | custom-call | tf_op jit(solution)/shard_map/pallas_call | solution.py:305
  (45 shorter events, 0.7 us)
Async XLA Ops:
  8.8 6.1 %collective-permute-start = (bf16[128,512]{1,0:T(8,128)(2,1)}, bf16[128,512]{1,0:T(8,128)(2,1)S(1)}, u32[]{:S(2)}, u32[]{:S(2)}) collective-permute-start(bf16[128,512]{1,0:T(8,128)(2,1)} %bitcast.15), channel_id=1, source_target_pairs={{0,2},{2,0},{4,6},{6,4},{8,10},{10,8},{12,14},{14,12},{1,3},{3,1},... | collective-permute-start | bytes 393224 | tf_op jit(solution)/shard_map/ppermute | solution.py:261
  15.9 20.4 %copy-start = (bf16[128,512]{1,0:T(8,128)(2,1)}, bf16[128,512]{1,0:T(8,128)(2,1)S(1)}, u32[]{:S(2)}) copy-start(bf16[128,512]{1,0:T(8,128)(2,1)S(1)} %add_convert_fusion.refs_0_) | copy-start | bytes 393220
  15.9 8.4 %collective-permute-start.8 = (bf16[128,512]{1,0:T(8,128)(2,1)S(1)}, bf16[128,512]{1,0:T(8,128)(2,1)S(1)}, u32[]{:S(2)}, u32[]{:S(2)}) collective-permute-start(bf16[128,512]{1,0:T(8,128)(2,1)S(1)} %add_convert_fusion.refs_0_), channel_id=1, source_target_pairs={{0,12},{2,14},{4,8},{6,10},{8,4},{10,6},{12,0},{14,2},{1,13},{3,15... | collective-permute-start | bytes 393224 | tf_op jit(solution)/shard_map/ppermute | solution.py:261
  20.4 5.9 %collective-permute-start.4 = (bf16[128,512]{1,0:T(8,128)(2,1)S(1)}, bf16[128,512]{1,0:T(8,128)(2,1)S(1)}, u32[]{:S(2)}, u32[]{:S(2)}) collective-permute-start(bf16[128,512]{1,0:T(8,128)(2,1)S(1)} %add_convert_fusion.refs_0_), channel_id=1, source_target_pairs={{0,1},{1,0},{2,3},{3,2},{4,5},{5,4},{6,7},{7,6},{8,9},{9,8},{10,11... | collective-permute-start | bytes 393224 | tf_op jit(solution)/shard_map/ppermute | solution.py:272
  20.4 7.2 %collective-permute-start.3 = (bf16[128,512]{1,0:T(8,128)(2,1)S(1)}, bf16[128,512]{1,0:T(8,128)(2,1)S(1)}, u32[]{:S(2)}, u32[]{:S(2)}) collective-permute-start(bf16[128,512]{1,0:T(8,128)(2,1)S(1)} %add_convert_fusion.refs_0_), channel_id=1, source_target_pairs={{0,6},{2,4},{4,2},{6,0},{8,14},{10,12},{12,10},{14,8},{1,7},{3,5},... | collective-permute-start | bytes 393224 | tf_op jit(solution)/shard_map/ppermute | solution.py:261
  20.9 9.0 %collective-permute-start.2 = (bf16[128,512]{1,0:T(8,128)(2,1)S(1)}, bf16[128,512]{1,0:T(8,128)(2,1)S(1)}, u32[]{:S(2)}, u32[]{:S(2)}) collective-permute-start(bf16[128,512]{1,0:T(8,128)(2,1)S(1)} %add_convert_fusion.refs_0_), channel_id=1, source_target_pairs={{0,4},{2,6},{4,0},{6,2},{8,12},{10,14},{12,8},{14,10},{1,5},{3,7},... | collective-permute-start | bytes 393224 | tf_op jit(solution)/shard_map/ppermute | solution.py:261
  22.1 8.4 %collective-permute-start.1 = (bf16[128,512]{1,0:T(8,128)(2,1)S(1)}, bf16[128,512]{1,0:T(8,128)(2,1)S(1)}, u32[]{:S(2)}, u32[]{:S(2)}) collective-permute-start(bf16[128,512]{1,0:T(8,128)(2,1)S(1)} %add_convert_fusion.refs_0_), channel_id=1, source_target_pairs={{0,2},{2,0},{4,6},{6,4},{8,10},{10,8},{12,14},{14,12},{1,3},{3,1},... | collective-permute-start | bytes 393224 | tf_op jit(solution)/shard_map/ppermute | solution.py:261
  24.2 17.2 %copy-start.8 = (bf16[128,512]{1,0:T(8,128)(2,1)}, bf16[128,512]{1,0:T(8,128)(2,1)S(1)}, u32[]{:S(2)}) copy-start(bf16[128,512]{1,0:T(8,128)(2,1)S(1)} %collective-permute-done.8.refs_4_) | copy-start | bytes 393220
  24.3 9.0 %collective-permute-start.11 = (bf16[128,512]{1,0:T(8,128)(2,1)S(1)}, bf16[128,512]{1,0:T(8,128)(2,1)S(1)}, u32[]{:S(2)}, u32[]{:S(2)}) collective-permute-start(bf16[128,512]{1,0:T(8,128)(2,1)S(1)} %collective-permute-done.8.refs_4_), channel_id=1, source_target_pairs={{0,6},{2,4},{4,2},{6,0},{8,14},{10,12},{12,10},{14,8},{1,7},{3,5},... | collective-permute-start | bytes 393224 | tf_op jit(solution)/shard_map/ppermute | solution.py:261
  26.3 9.9 %copy-start.1 = (bf16[128,512]{1,0:T(8,128)(2,1)}, bf16[128,512]{1,0:T(8,128)(2,1)S(1)}, u32[]{:S(2)}) copy-start(bf16[128,512]{1,0:T(8,128)(2,1)S(1)} %collective-permute-done.4.refs_4_.refs_8_) | copy-start | bytes 393220
  26.3 8.4 %collective-permute-start.10 = (bf16[128,512]{1,0:T(8,128)(2,1)S(1)}, bf16[128,512]{1,0:T(8,128)(2,1)S(1)}, u32[]{:S(2)}, u32[]{:S(2)}) collective-permute-start(bf16[128,512]{1,0:T(8,128)(2,1)S(1)} %collective-permute-done.8.refs_4_), channel_id=1, source_target_pairs={{0,4},{2,6},{4,0},{6,2},{8,12},{10,14},{12,8},{14,10},{1,5},{3,7},... | collective-permute-start | bytes 393224 | tf_op jit(solution)/shard_map/ppermute | solution.py:261
  27.6 8.6 %copy-start.2 = (bf16[128,512]{1,0:T(8,128)(2,1)}, bf16[128,512]{1,0:T(8,128)(2,1)S(1)}, u32[]{:S(2)}) copy-start(bf16[128,512]{1,0:T(8,128)(2,1)S(1)} %collective-permute-done.3.refs_3_) | copy-start | bytes 393220
  27.6 8.0 %collective-permute-start.9 = (bf16[128,512]{1,0:T(8,128)(2,1)S(1)}, bf16[128,512]{1,0:T(8,128)(2,1)S(1)}, u32[]{:S(2)}, u32[]{:S(2)}) collective-permute-start(bf16[128,512]{1,0:T(8,128)(2,1)S(1)} %collective-permute-done.8.refs_4_), channel_id=1, source_target_pairs={{0,2},{2,0},{4,6},{6,4},{8,10},{10,8},{12,14},{14,12},{1,3},{3,1},... | collective-permute-start | bytes 393224 | tf_op jit(solution)/shard_map/ppermute | solution.py:261
  29.9 6.4 %copy-start.3 = (bf16[128,512]{1,0:T(8,128)(2,1)}, bf16[128,512]{1,0:T(8,128)(2,1)S(1)}, u32[]{:S(2)}) copy-start(bf16[128,512]{1,0:T(8,128)(2,1)S(1)} %collective-permute-done.2.refs_2_) | copy-start | bytes 393220
  29.9 5.8 %collective-permute-start.7 = (bf16[128,512]{1,0:T(8,128)(2,1)S(1)}, bf16[128,512]{1,0:T(8,128)(2,1)S(1)}, u32[]{:S(2)}, u32[]{:S(2)}) collective-permute-start(bf16[128,512]{1,0:T(8,128)(2,1)S(1)} %collective-permute-done.3.refs_3_), channel_id=1, source_target_pairs={{0,1},{1,0},{2,3},{3,2},{4,5},{5,4},{6,7},{7,6},{8,9},{9,8},{10,11... | collective-permute-start | bytes 393224 | tf_op jit(solution)/shard_map/ppermute | solution.py:272
  30.5 5.6 %collective-permute-start.6 = (bf16[128,512]{1,0:T(8,128)(2,1)S(1)}, bf16[128,512]{1,0:T(8,128)(2,1)S(1)}, u32[]{:S(2)}, u32[]{:S(2)}) collective-permute-start(bf16[128,512]{1,0:T(8,128)(2,1)S(1)} %collective-permute-done.2.refs_2_), channel_id=1, source_target_pairs={{0,1},{1,0},{2,3},{3,2},{4,5},{5,4},{6,7},{7,6},{8,9},{9,8},{10,11... | collective-permute-start | bytes 393224 | tf_op jit(solution)/shard_map/ppermute | solution.py:272
  33.3 8.2 %copy-start.9 = (bf16[128,512]{1,0:T(8,128)(2,1)}, bf16[128,512]{1,0:T(8,128)(2,1)S(1)}, u32[]{:S(2)}) copy-start(bf16[128,512]{1,0:T(8,128)(2,1)S(1)} %collective-permute-done.11.refs_7_) | copy-start | bytes 393220
  33.3 2.9 %collective-permute-start.5 = (bf16[128,512]{1,0:T(8,128)(2,1)S(1)}, bf16[128,512]{1,0:T(8,128)(2,1)S(1)}, u32[]{:S(2)}, u32[]{:S(2)}) collective-permute-start(bf16[128,512]{1,0:T(8,128)(2,1)S(1)} %collective-permute-done.1.refs_1_), channel_id=1, source_target_pairs={{0,1},{1,0},{2,3},{3,2},{4,5},{5,4},{6,7},{7,6},{8,9},{9,8},{10,11... | collective-permute-start | bytes 393224 | tf_op jit(solution)/shard_map/ppermute | solution.py:272
  34.8 6.7 %copy-start.10 = (bf16[128,512]{1,0:T(8,128)(2,1)}, bf16[128,512]{1,0:T(8,128)(2,1)S(1)}, u32[]{:S(2)}) copy-start(bf16[128,512]{1,0:T(8,128)(2,1)S(1)} %collective-permute-done.10.refs_6_) | copy-start | bytes 393220
  34.8 6.6 %collective-permute-start.12 = (bf16[128,512]{1,0:T(8,128)(2,1)S(1)}, bf16[128,512]{1,0:T(8,128)(2,1)S(1)}, u32[]{:S(2)}, u32[]{:S(2)}) collective-permute-start(bf16[128,512]{1,0:T(8,128)(2,1)S(1)} %collective-permute-done.8.refs_4_), channel_id=1, source_target_pairs={{0,1},{1,0},{2,3},{3,2},{4,5},{5,4},{6,7},{7,6},{8,9},{9,8},{10,11... | collective-permute-start | bytes 393224 | tf_op jit(solution)/shard_map/ppermute | solution.py:272
  35.6 5.8 %copy-start.11 = (bf16[128,512]{1,0:T(8,128)(2,1)}, bf16[128,512]{1,0:T(8,128)(2,1)S(1)}, u32[]{:S(2)}) copy-start(bf16[128,512]{1,0:T(8,128)(2,1)S(1)} %collective-permute-done.9.refs_5_) | copy-start | bytes 393220
  35.6 5.8 %collective-permute-start.15 = (bf16[128,512]{1,0:T(8,128)(2,1)S(1)}, bf16[128,512]{1,0:T(8,128)(2,1)S(1)}, u32[]{:S(2)}, u32[]{:S(2)}) collective-permute-start(bf16[128,512]{1,0:T(8,128)(2,1)S(1)} %collective-permute-done.11.refs_7_), channel_id=1, source_target_pairs={{0,1},{1,0},{2,3},{3,2},{4,5},{5,4},{6,7},{7,6},{8,9},{9,8},{10,11... | collective-permute-start | bytes 393224 | tf_op jit(solution)/shard_map/ppermute | solution.py:272
  35.6 5.8 %collective-permute-start.14 = (bf16[128,512]{1,0:T(8,128)(2,1)S(1)}, bf16[128,512]{1,0:T(8,128)(2,1)S(1)}, u32[]{:S(2)}, u32[]{:S(2)}) collective-permute-start(bf16[128,512]{1,0:T(8,128)(2,1)S(1)} %collective-permute-done.10.refs_6_), channel_id=1, source_target_pairs={{0,1},{1,0},{2,3},{3,2},{4,5},{5,4},{6,7},{7,6},{8,9},{9,8},{10,11... | collective-permute-start | bytes 393224 | tf_op jit(solution)/shard_map/ppermute | solution.py:272
  36.2 5.3 %collective-permute-start.13 = (bf16[128,512]{1,0:T(8,128)(2,1)S(1)}, bf16[128,512]{1,0:T(8,128)(2,1)S(1)}, u32[]{:S(2)}, u32[]{:S(2)}) collective-permute-start(bf16[128,512]{1,0:T(8,128)(2,1)S(1)} %collective-permute-done.9.refs_5_), channel_id=1, source_target_pairs={{0,1},{1,0},{2,3},{3,2},{4,5},{5,4},{6,7},{7,6},{8,9},{9,8},{10,11... | collective-permute-start | bytes 393224 | tf_op jit(solution)/shard_map/ppermute | solution.py:272
  (8 other events, 10.5 us)

commit v2 on v1

--- a/solution.py
+++ b/solution.py
@@ -10,8 +10,9 @@
 POLY_COEFFS = (1.0, -0.6, 0.15, -0.03)
 HALO = 2
 BATCH = 4
+CHUNKS = 4
 EDGE = 4
-VMEM_LIMIT = 56 * 2**20
+VMEM_LIMIT = 24 * 2**20
 F32 = jnp.float32
 BF16 = jnp.bfloat16
 
@@ -26,9 +27,34 @@
 
 
 def das_kernel(
-    count, target, offset, echo, weights, grid_map, own_out, send_out, dense, arranged, *, chans, lat
+    count,
+    target,
+    offset,
+    echo_hbm,
+    weights_hbm,
+    grid_map,
+    own_out,
+    send_out,
+    echo,
+    weights,
+    dense,
+    arranged,
+    sems,
+    *,
+    chans,
+    lat,
 ):
     slots, tile = weights.shape[0], weights.shape[1]
+    chunk = slots // CHUNKS
+    copies = [
+        pltpu.make_async_copy(
+            weights_hbm.at[pl.ds(i * chunk, chunk)], weights.at[pl.ds(i * chunk, chunk)], sems.at[i]
+        )
+        for i in range(CHUNKS)
+    ]
+    copies.append(pltpu.make_async_copy(echo_hbm, echo, sems.at[CHUNKS]))
+    for copy in copies:
+        copy.start()
     voxels = grid_map.shape[1]
     tiles_out = voxels // tile
     spans = echo.shape[0] // tile
@@ -48,13 +74,18 @@
             dense[goal, span + 1] += jnp.where(lanes < shift, turned, 0.0)
         return carry
 
-    lax.fori_loop(0, (live + BATCH - 1) // BATCH, one_batch, 0)
+    turns = (live + BATCH - 1) // BATCH
+    for i in range(CHUNKS):
+        copies[i].wait()
+        last = jnp.minimum(turns, (i + 1) * chunk // BATCH)
+        lax.fori_loop(i * chunk // BATCH, last, one_batch, 0)
+    copies[CHUNKS].wait()
 
     rows = []
     for t in range(tiles_out):
         rows.append(jnp.concatenate([dense[t, s] for s in range(spans)], axis=1))
     high, low = split(jnp.concatenate(rows, axis=0))
-    data = echo[...]
+    data = echo[...].reshape(echo.shape[0], 2 * echo.shape[2])
     sums = dot(high, data) + dot(low, data)
     voxel_ids = lax.broadcasted_iota(jnp.int32, (voxels, voxels), 0)
     placing = (voxel_ids == grid_map[...]).astype(F32).astype(BF16)
@@ -228,20 +259,24 @@
     n = lat * width
     smem = pl.BlockSpec(memory_space=pltpu.SMEM)
     vmem = pl.BlockSpec(memory_space=pltpu.VMEM)
-    echo = echo_data.reshape(rows, 2 * hf)
+    hbm = pl.BlockSpec(memory_space=pl.ANY)
+    echo = echo_data.reshape(rows, 2, hf)
     own, sent = pl.pallas_call(
         functools.partial(das_kernel, chans=chans, lat=lat),
         out_shape=(
-            jax.ShapeDtypeStruct((n, 2 * hf), F32),
-            jax.ShapeDtypeStruct((chans - 1, n, 2 * hf), BF16),
+            pltpu.VMEM((n, 2 * hf), F32),
+            pltpu.VMEM((chans - 1, n, 2 * hf), BF16),
         ),
-        in_specs=[smem, smem, smem, vmem, vmem, vmem],
+        in_specs=[smem, smem, smem, hbm, hbm, vmem],
         out_specs=(vmem, vmem),
         scratch_shapes=[
+            pltpu.VMEM((rows, 2, hf), BF16),
+            pltpu.VMEM((slots, tile, tile), BF16),
             pltpu.VMEM((voxels // tile + 1, rows // tile + 1, tile, tile), F32),
             pltpu.VMEM((voxels, 2 * hf), F32),
+            pltpu.SemaphoreType.DMA((CHUNKS + 1,)),
         ],
-        compiler_params=pltpu.CompilerParams(vmem_limit_bytes=VMEM_LIMIT),
+        compiler_params=pltpu.CompilerParams(vmem_limit_bytes=56 * 2**20),
     )(
         tile_count.reshape(-1),
         tile_target.reshape(-1),
@@ -271,13 +306,13 @@
     def to_other(x):
         return lax.ppermute(x, "frm", [(f, f ^ 1) for f in range(frms)])
 
-    other = [to_other(x) for x in mine]
     groups = inner * chans
     part = groups // 2
+    other = [to_other(x) for x in mine]
 
     def gram_of(a, b):
         cost = pl.CostEstimate(
-            flops=6 * len(a) * n * (2 * hf) ** 2, bytes_accessed=12 * (2 * hf) ** 2, transcendentals=0
+            flops=60 * len(a) * n * (2 * hf) ** 2, bytes_accessed=12 * (2 * hf) ** 2, transcendentals=0
         )
         return pl.pallas_call(
             gram_kernel,

time: 52.4 us -> 41.5 us (0.79)
  Pallas kernels: 18.8 us -> 12.3 us
  starting transfers between devices: 12.2 us -> 17.2 us
  local copies, waits for them, and re-layouts: 4.99 us -> 0.01 us
  waiting for transfers between devices: 14.2 us -> 11 us
  other arithmetic: 0.98 us -> 0.04 us
    unnamed x33 -> x2, local copies, waits for them, and re-layouts: 4.99 us -> 0.01 us
    ppermute x8, starting transfers between devices: 11.6 us -> 16.5 us  [peer(): return lax.ppermute(x, ('vox', 'chan'), pairs)]
    ppermute x8, waiting for transfers between devices: 14.2 us -> 10.8 us  [peer(): return lax.ppermute(x, ('vox', 'chan'), pairs)]
    pallas_call x1, Pallas kernels: 3.93 us -> 1.02 us  [gram_of(): pl.pallas_call(gram_kernel, out_shape=jax.ShapeDtypeStruct((3, 2 * hf, 2...]
    pallas_call x1, Pallas kernels: 9.13 us -> 7.23 us  [shards(): pl.pallas_call(functools.partial(filter_kernel, fresh=fresh, inner=inner,...]
    pallas_call x1, Pallas kernels: 5.74 us -> 4.05 us  [shards(): pl.pallas_call(functools.partial(das_kernel, chans=chans, lat=lat), out_s...]
    convert_element_type x1, other arithmetic: 0.98 us -> 0.04 us  [shards(): own = own.astype(BF16)]
  transfers between devices with their start and end apart: 16 -> 16, of which waited for: 8 -> 9; matrix products, arithmetic and copies ran while one was open for 0% -> 0% of each run, Pallas kernels for 8% -> 2%
where the time goes in v2:
time: 41.5 us; the launch traced here: 41.3 us
  starting transfers between devices  17.2 us (41%)
  Pallas kernels  12.3 us (30%)
  waiting for transfers between devices  11 us (27%)
  between operations  0.71 us (2%)
    ppermute x8, starting transfers between devices, peer(): return lax.ppermute(x, ('vox', 'chan'), pairs)  16.5 us
    ppermute x8, waiting for transfers between devices, peer(): return lax.ppermute(x, ('vox', 'chan'), pairs)  10.8 us
    pallas_call x1, Pallas kernels, shards(): pl.pallas_call(functools.partial(filter_kernel, fresh=fresh, inner=inner,...  7.23 us
    pallas_call x1, Pallas kernels, shards(): pl.pallas_call(functools.partial(das_kernel, chans=chans, lat=lat), out_s...  4.05 us
    pallas_call x1, Pallas kernels, gram_of(): pl.pallas_call(gram_kernel, out_shape=jax.ShapeDtypeStruct((3, 2 * hf, 2...  1.02 us
  transfers between devices with their start and end apart: 16, of which 9 were waited for; matrix products, arithmetic and copies ran while one was open for 0% of the time, Pallas kernels for 2%

profile of v2, /device:TPU:0, one launch (start us, length us, event | category | flops | bytes accessed | tf_op | source)
XLA Modules:
  0.0 41.3 jit_solution(11337144480360985501)
XLA Ops:
  0.7 4.0 %shard_map.73 = (f32[128,512]{1,0:T(8,128)S(1)}, bf16[1,128,512]{2,1,0:T(8,128)(2,1)S(1)}) custom-call(s32[1]{0:T(128)} %bitcast.7.count, s32[64]{0:T(128)} %bitcast.11, s32[64]{0:T(128)} %bitcast.12, bf16[1024,2,256]{2,1,0:T(2,128)(2,1)} %bitcast.10, bf16[64,128,128]{2,1,0:T(8,128)(2,1)} %bitcast.9, s32[1,256]{1,0:T(1,128)} %grid_map.1), custom_call_target="tpu_custom_call" | custom-call | tf_op jit(solution)/shard_map/pallas_call | solution.py:264
  4.7 4.2 %collective-permute-start = (bf16[128,512]{1,0:T(8,128)(2,1)S(1)}, bf16[128,512]{1,0:T(8,128)(2,1)S(1)}, u32[]{:S(2)}, u32[]{:S(2)}) collective-permute-start(bf16[128,512]{1,0:T(8,128)(2,1)S(1)} %bitcast.8), channel_id=1, source_target_pairs={{0,2},{2,0},{4,6},{6,4},{8,10},{10,8},{12,14},{14,12},{1,3},{3,1},... | collective-permute-start | bytes 393224 | tf_op jit(solution)/shard_map/ppermute | solution.py:296
  8.9 3.5 %collective-permute-done = bf16[128,512]{1,0:T(8,128)(2,1)S(1)} collective-permute-done((bf16[128,512]{1,0:T(8,128)(2,1)S(1)}, bf16[128,512]{1,0:T(8,128)(2,1)S(1)}, u32[]{:S(2)}, u32[]{:S(2)}) %collective-permute-start) | collective-permute-done | bytes 131104 | tf_op jit(solution)/shard_map/ppermute | solution.py:296
  12.5 3.7 %collective-permute-start.8 = (bf16[128,512]{1,0:T(8,128)(2,1)S(1)}, bf16[128,512]{1,0:T(8,128)(2,1)S(1)}, u32[]{:S(2)}, u32[]{:S(2)}) collective-permute-start(bf16[128,512]{1,0:T(8,128)(2,1)S(1)} %add_convert_fusion.refs_0_), channel_id=1, source_target_pairs={{0,12},{2,14},{4,8},{6,10},{8,4},{10,6},{12,0},{14,2},{1,13},{3,15... | collective-permute-start | bytes 393224 | tf_op jit(solution)/shard_map/ppermute | solution.py:296
  16.1 0.7 %collective-permute-start.3 = (bf16[128,512]{1,0:T(8,128)(2,1)S(1)}, bf16[128,512]{1,0:T(8,128)(2,1)S(1)}, u32[]{:S(2)}, u32[]{:S(2)}) collective-permute-start(bf16[128,512]{1,0:T(8,128)(2,1)S(1)} %add_convert_fusion.refs_0_), channel_id=1, source_target_pairs={{0,6},{2,4},{4,2},{6,0},{8,14},{10,12},{12,10},{14,8},{1,7},{3,5},... | collective-permute-start | bytes 393224 | tf_op jit(solution)/shard_map/ppermute | solution.py:296
  16.9 2.5 %collective-permute-start.2 = (bf16[128,512]{1,0:T(8,128)(2,1)S(1)}, bf16[128,512]{1,0:T(8,128)(2,1)S(1)}, u32[]{:S(2)}, u32[]{:S(2)}) collective-permute-start(bf16[128,512]{1,0:T(8,128)(2,1)S(1)} %add_convert_fusion.refs_0_), channel_id=1, source_target_pairs={{0,4},{2,6},{4,0},{6,2},{8,12},{10,14},{12,8},{14,10},{1,5},{3,7},... | collective-permute-start | bytes 393224 | tf_op jit(solution)/shard_map/ppermute | solution.py:296
  19.3 0.3 collective-permute-start.1
  19.6 0.1 collective-permute-done.8.refs_4_
  19.8 2.5 %collective-permute-start.11 = (bf16[128,512]{1,0:T(8,128)(2,1)S(1)}, bf16[128,512]{1,0:T(8,128)(2,1)S(1)}, u32[]{:S(2)}, u32[]{:S(2)}) collective-permute-start(bf16[128,512]{1,0:T(8,128)(2,1)S(1)} %collective-permute-done.8.refs_4_), channel_id=1, source_target_pairs={{0,6},{2,4},{4,2},{6,0},{8,14},{10,12},{12,10},{14,8},{1,7},{3,5},... | collective-permute-start | bytes 393224 | tf_op jit(solution)/shard_map/ppermute | solution.py:296
  22.3 1.4 %collective-permute-start.10 = (bf16[128,512]{1,0:T(8,128)(2,1)S(1)}, bf16[128,512]{1,0:T(8,128)(2,1)S(1)}, u32[]{:S(2)}, u32[]{:S(2)}) collective-permute-start(bf16[128,512]{1,0:T(8,128)(2,1)S(1)} %collective-permute-done.8.refs_4_), channel_id=1, source_target_pairs={{0,4},{2,6},{4,0},{6,2},{8,12},{10,14},{12,8},{14,10},{1,5},{3,7},... | collective-permute-start | bytes 393224 | tf_op jit(solution)/shard_map/ppermute | solution.py:296
  23.8 0.2 collective-permute-done.3.refs_3_
  24.0 1.1 %collective-permute-start.9 = (bf16[128,512]{1,0:T(8,128)(2,1)S(1)}, bf16[128,512]{1,0:T(8,128)(2,1)S(1)}, u32[]{:S(2)}, u32[]{:S(2)}) collective-permute-start(bf16[128,512]{1,0:T(8,128)(2,1)S(1)} %collective-permute-done.8.refs_4_), channel_id=1, source_target_pairs={{0,2},{2,0},{4,6},{6,4},{8,10},{10,8},{12,14},{14,12},{1,3},{3,1},... | collective-permute-start | bytes 393224 | tf_op jit(solution)/shard_map/ppermute | solution.py:296
  25.1 1.3 %collective-permute-done.2.refs_2_ = bf16[128,512]{1,0:T(8,128)(2,1)S(1)} collective-permute-done((bf16[128,512]{1,0:T(8,128)(2,1)S(1)}, bf16[128,512]{1,0:T(8,128)(2,1)S(1)}, u32[]{:S(2)}, u32[]{:S(2)}) %collective-permute-start.2) | collective-permute-done | bytes 131104 | tf_op jit(solution)/shard_map/ppermute | solution.py:296
  26.5 0.4 %collective-permute-done.1.refs_1_ = bf16[128,512]{1,0:T(8,128)(2,1)S(1)} collective-permute-done((bf16[128,512]{1,0:T(8,128)(2,1)S(1)}, bf16[128,512]{1,0:T(8,128)(2,1)S(1)}, u32[]{:S(2)}, u32[]{:S(2)}) %collective-permute-start.1) | collective-permute-done | bytes 131104 | tf_op jit(solution)/shard_map/ppermute | solution.py:296
  26.9 0.1 collective-permute-start.6
  27.0 2.7 %collective-permute-done.11.refs_7_ = bf16[128,512]{1,0:T(8,128)(2,1)S(1)} collective-permute-done((bf16[128,512]{1,0:T(8,128)(2,1)S(1)}, bf16[128,512]{1,0:T(8,128)(2,1)S(1)}, u32[]{:S(2)}, u32[]{:S(2)}) %collective-permute-start.11) | collective-permute-done | bytes 131104 | tf_op jit(solution)/shard_map/ppermute | solution.py:296
  29.7 2.1 %collective-permute-done.10.refs_6_ = bf16[128,512]{1,0:T(8,128)(2,1)S(1)} collective-permute-done((bf16[128,512]{1,0:T(8,128)(2,1)S(1)}, bf16[128,512]{1,0:T(8,128)(2,1)S(1)}, u32[]{:S(2)}, u32[]{:S(2)}) %collective-permute-start.10) | collective-permute-done | bytes 131104 | tf_op jit(solution)/shard_map/ppermute | solution.py:296
  31.7 0.4 %collective-permute-done.9.refs_5_ = bf16[128,512]{1,0:T(8,128)(2,1)S(1)} collective-permute-done((bf16[128,512]{1,0:T(8,128)(2,1)S(1)}, bf16[128,512]{1,0:T(8,128)(2,1)S(1)}, u32[]{:S(2)}, u32[]{:S(2)}) %collective-permute-start.9) | collective-permute-done | bytes 131104 | tf_op jit(solution)/shard_map/ppermute | solution.py:296
  32.2 0.1 collective-permute-start.15
  32.3 0.4 %collective-permute-start.14 = (bf16[128,512]{1,0:T(8,128)(2,1)S(1)}, bf16[128,512]{1,0:T(8,128)(2,1)S(1)}, u32[]{:S(2)}, u32[]{:S(2)}) collective-permute-start(bf16[128,512]{1,0:T(8,128)(2,1)S(1)} %collective-permute-done.10.refs_6_), channel_id=1, source_target_pairs={{0,1},{1,0},{2,3},{3,2},{4,5},{5,4},{6,7},{7,6},{8,9},{9,8},{10,11... | collective-permute-start | bytes 393224 | tf_op jit(solution)/shard_map/ppermute | solution.py:307
  32.7 0.1 collective-permute-start.13
  32.8 1.0 %shard_map.74.gram = f32[3,512,512]{2,1,0:T(8,128)S(1)} custom-call(bf16[128,512]{1,0:T(8,128)(2,1)S(1)} %add_convert_fusion.refs_0_, bf16[128,512]{1,0:T(8,128)(2,1)S(1)} %collective-permute-done.1.refs_1_, bf16[128,512]{1,0:T(8,128)(2,1)S(1)} %collective-permute-done.2.refs_2_, bf16[128,512]{1,0:T(8,128)(2,1)S(1)} %collective-permute-done.3.refs_3_, ...), custom_call_target="tpu_custom_call" | custom-call | flops 8053063680 | bytes 3145728 | tf_op jit(solution)/shard_map/pallas_call | solution.py:317
  33.8 0.2 collective-permute-done.13.refs_13_
  34.0 7.2 %shard_map.75 = f32[128,256]{1,0:T(8,128)} custom-call(f32[5,5]{1,0:T(8,128)S(1)} %copy-done, f32[3,512,512]{2,1,0:T(8,128)S(1)} %shard_map.74.gram, bf16[128,512]{1,0:T(8,128)(2,1)S(1)} %add_convert_fusion.refs_0_, bf16[128,512]{1,0:T(8,128)(2,1)S(1)} %collective-permute-done.1.refs_1_, bf16[128,512]{1,0:T(8,128)(2,1)S(1)} %collective-permute-done.2.refs_2_, ...), custom_call_target="tpu_custom_call" | custom-call | tf_op jit(solution)/shard_map/pallas_call | solution.py:340
  (14 shorter events, 0.1 us)
Async XLA Ops:
  4.7 7.7 %collective-permute-start = (bf16[128,512]{1,0:T(8,128)(2,1)S(1)}, bf16[128,512]{1,0:T(8,128)(2,1)S(1)}, u32[]{:S(2)}, u32[]{:S(2)}) collective-permute-start(bf16[128,512]{1,0:T(8,128)(2,1)S(1)} %bitcast.8), channel_id=1, source_target_pairs={{0,2},{2,0},{4,6},{6,4},{8,10},{10,8},{12,14},{14,12},{1,3},{3,1},... | collective-permute-start | bytes 393224 | tf_op jit(solution)/shard_map/ppermute | solution.py:296
  12.5 21.6 %copy-start = (f32[5,5]{1,0:T(8,128)S(1)}, f32[5,5]{1,0:T(8,128)}, u32[]{:S(2)}) copy-start(f32[5,5]{1,0:T(8,128)} %psf.1) | copy-start | bytes 304
  12.5 7.3 %collective-permute-start.8 = (bf16[128,512]{1,0:T(8,128)(2,1)S(1)}, bf16[128,512]{1,0:T(8,128)(2,1)S(1)}, u32[]{:S(2)}, u32[]{:S(2)}) collective-permute-start(bf16[128,512]{1,0:T(8,128)(2,1)S(1)} %add_convert_fusion.refs_0_), channel_id=1, source_target_pairs={{0,12},{2,14},{4,8},{6,10},{8,4},{10,6},{12,0},{14,2},{1,13},{3,15... | collective-permute-start | bytes 393224 | tf_op jit(solution)/shard_map/ppermute | solution.py:296
  16.1 6.2 %collective-permute-start.4 = (bf16[128,512]{1,0:T(8,128)(2,1)S(1)}, bf16[128,512]{1,0:T(8,128)(2,1)S(1)}, u32[]{:S(2)}, u32[]{:S(2)}) collective-permute-start(bf16[128,512]{1,0:T(8,128)(2,1)S(1)} %add_convert_fusion.refs_0_), channel_id=1, source_target_pairs={{0,1},{1,0},{2,3},{3,2},{4,5},{5,4},{6,7},{7,6},{8,9},{9,8},{10,11... | collective-permute-start | bytes 393224 | tf_op jit(solution)/shard_map/ppermute | solution.py:307
  16.1 7.8 %collective-permute-start.3 = (bf16[128,512]{1,0:T(8,128)(2,1)S(1)}, bf16[128,512]{1,0:T(8,128)(2,1)S(1)}, u32[]{:S(2)}, u32[]{:S(2)}) collective-permute-start(bf16[128,512]{1,0:T(8,128)(2,1)S(1)} %add_convert_fusion.refs_0_), channel_id=1, source_target_pairs={{0,6},{2,4},{4,2},{6,0},{8,14},{10,12},{12,10},{14,8},{1,7},{3,5},... | collective-permute-start | bytes 393224 | tf_op jit(solution)/shard_map/ppermute | solution.py:296
  16.9 9.6 %collective-permute-start.2 = (bf16[128,512]{1,0:T(8,128)(2,1)S(1)}, bf16[128,512]{1,0:T(8,128)(2,1)S(1)}, u32[]{:S(2)}, u32[]{:S(2)}) collective-permute-start(bf16[128,512]{1,0:T(8,128)(2,1)S(1)} %add_convert_fusion.refs_0_), channel_id=1, source_target_pairs={{0,4},{2,6},{4,0},{6,2},{8,12},{10,14},{12,8},{14,10},{1,5},{3,7},... | collective-permute-start | bytes 393224 | tf_op jit(solution)/shard_map/ppermute | solution.py:296
  19.3 7.5 %collective-permute-start.1 = (bf16[128,512]{1,0:T(8,128)(2,1)S(1)}, bf16[128,512]{1,0:T(8,128)(2,1)S(1)}, u32[]{:S(2)}, u32[]{:S(2)}) collective-permute-start(bf16[128,512]{1,0:T(8,128)(2,1)S(1)} %add_convert_fusion.refs_0_), channel_id=1, source_target_pairs={{0,2},{2,0},{4,6},{6,4},{8,10},{10,8},{12,14},{14,12},{1,3},{3,1},... | collective-permute-start | bytes 393224 | tf_op jit(solution)/shard_map/ppermute | solution.py:296
  19.8 9.9 %collective-permute-start.11 = (bf16[128,512]{1,0:T(8,128)(2,1)S(1)}, bf16[128,512]{1,0:T(8,128)(2,1)S(1)}, u32[]{:S(2)}, u32[]{:S(2)}) collective-permute-start(bf16[128,512]{1,0:T(8,128)(2,1)S(1)} %collective-permute-done.8.refs_4_), channel_id=1, source_target_pairs={{0,6},{2,4},{4,2},{6,0},{8,14},{10,12},{12,10},{14,8},{1,7},{3,5},... | collective-permute-start | bytes 393224 | tf_op jit(solution)/shard_map/ppermute | solution.py:296
  22.3 9.4 %collective-permute-start.10 = (bf16[128,512]{1,0:T(8,128)(2,1)S(1)}, bf16[128,512]{1,0:T(8,128)(2,1)S(1)}, u32[]{:S(2)}, u32[]{:S(2)}) collective-permute-start(bf16[128,512]{1,0:T(8,128)(2,1)S(1)} %collective-permute-done.8.refs_4_), channel_id=1, source_target_pairs={{0,4},{2,6},{4,0},{6,2},{8,12},{10,14},{12,8},{14,10},{1,5},{3,7},... | collective-permute-start | bytes 393224 | tf_op jit(solution)/shard_map/ppermute | solution.py:296
  24.0 8.2 %collective-permute-start.9 = (bf16[128,512]{1,0:T(8,128)(2,1)S(1)}, bf16[128,512]{1,0:T(8,128)(2,1)S(1)}, u32[]{:S(2)}, u32[]{:S(2)}) collective-permute-start(bf16[128,512]{1,0:T(8,128)(2,1)S(1)} %collective-permute-done.8.refs_4_), channel_id=1, source_target_pairs={{0,2},{2,0},{4,6},{6,4},{8,10},{10,8},{12,14},{14,12},{1,3},{3,1},... | collective-permute-start | bytes 393224 | tf_op jit(solution)/shard_map/ppermute | solution.py:296
  26.5 5.8 %collective-permute-start.7 = (bf16[128,512]{1,0:T(8,128)(2,1)S(1)}, bf16[128,512]{1,0:T(8,128)(2,1)S(1)}, u32[]{:S(2)}, u32[]{:S(2)}) collective-permute-start(bf16[128,512]{1,0:T(8,128)(2,1)S(1)} %collective-permute-done.3.refs_3_), channel_id=1, source_target_pairs={{0,1},{1,0},{2,3},{3,2},{4,5},{5,4},{6,7},{7,6},{8,9},{9,8},{10,11... | collective-permute-start | bytes 393224 | tf_op jit(solution)/shard_map/ppermute | solution.py:307
  26.9 5.8 %collective-permute-start.6 = (bf16[128,512]{1,0:T(8,128)(2,1)S(1)}, bf16[128,512]{1,0:T(8,128)(2,1)S(1)}, u32[]{:S(2)}, u32[]{:S(2)}) collective-permute-start(bf16[128,512]{1,0:T(8,128)(2,1)S(1)} %collective-permute-done.2.refs_2_), channel_id=1, source_target_pairs={{0,1},{1,0},{2,3},{3,2},{4,5},{5,4},{6,7},{7,6},{8,9},{9,8},{10,11... | collective-permute-start | bytes 393224 | tf_op jit(solution)/shard_map/ppermute | solution.py:307
  29.7 3.1 %collective-permute-start.5 = (bf16[128,512]{1,0:T(8,128)(2,1)S(1)}, bf16[128,512]{1,0:T(8,128)(2,1)S(1)}, u32[]{:S(2)}, u32[]{:S(2)}) collective-permute-start(bf16[128,512]{1,0:T(8,128)(2,1)S(1)} %collective-permute-done.1.refs_1_), channel_id=1, source_target_pairs={{0,1},{1,0},{2,3},{3,2},{4,5},{5,4},{6,7},{7,6},{8,9},{9,8},{10,11... | collective-permute-start | bytes 393224 | tf_op jit(solution)/shard_map/ppermute | solution.py:307
  31.7 2.1 %collective-permute-start.12 = (bf16[128,512]{1,0:T(8,128)(2,1)S(1)}, bf16[128,512]{1,0:T(8,128)(2,1)S(1)}, u32[]{:S(2)}, u32[]{:S(2)}) collective-permute-start(bf16[128,512]{1,0:T(8,128)(2,1)S(1)} %collective-permute-done.8.refs_4_), channel_id=1, source_target_pairs={{0,1},{1,0},{2,3},{3,2},{4,5},{5,4},{6,7},{7,6},{8,9},{9,8},{10,11... | collective-permute-start | bytes 393224 | tf_op jit(solution)/shard_map/ppermute | solution.py:307
  32.2 1.6 %collective-permute-start.15 = (bf16[128,512]{1,0:T(8,128)(2,1)S(1)}, bf16[128,512]{1,0:T(8,128)(2,1)S(1)}, u32[]{:S(2)}, u32[]{:S(2)}) collective-permute-start(bf16[128,512]{1,0:T(8,128)(2,1)S(1)} %collective-permute-done.11.refs_7_), channel_id=1, source_target_pairs={{0,1},{1,0},{2,3},{3,2},{4,5},{5,4},{6,7},{7,6},{8,9},{9,8},{10,11... | collective-permute-start | bytes 393224 | tf_op jit(solution)/shard_map/ppermute | solution.py:307
  32.3 1.6 %collective-permute-start.14 = (bf16[128,512]{1,0:T(8,128)(2,1)S(1)}, bf16[128,512]{1,0:T(8,128)(2,1)S(1)}, u32[]{:S(2)}, u32[]{:S(2)}) collective-permute-start(bf16[128,512]{1,0:T(8,128)(2,1)S(1)} %collective-permute-done.10.refs_6_), channel_id=1, source_target_pairs={{0,1},{1,0},{2,3},{3,2},{4,5},{5,4},{6,7},{7,6},{8,9},{9,8},{10,11... | collective-permute-start | bytes 393224 | tf_op jit(solution)/shard_map/ppermute | solution.py:307
  32.7 1.3 %collective-permute-start.13 = (bf16[128,512]{1,0:T(8,128)(2,1)S(1)}, bf16[128,512]{1,0:T(8,128)(2,1)S(1)}, u32[]{:S(2)}, u32[]{:S(2)}) collective-permute-start(bf16[128,512]{1,0:T(8,128)(2,1)S(1)} %collective-permute-done.9.refs_5_), channel_id=1, source_target_pairs={{0,1},{1,0},{2,3},{3,2},{4,5},{5,4},{6,7},{7,6},{8,9},{9,8},{10,11... | collective-permute-start | bytes 393224 | tf_op jit(solution)/shard_map/ppermute | solution.py:307

commit v3 on v2

v3 whole, which is shorter than its diff:
```python
import functools

import jax
import jax.numpy as jnp
from jax import lax
from jax.experimental import pallas as pl
from jax.experimental.pallas import tpu as pltpu
from jax.sharding import PartitionSpec as P

POLY_COEFFS = (1.0, -0.6, 0.15, -0.03)
HALO = 2
BATCH = 4
CHUNKS = 4
EDGE = 2
DIAG = 128
OUTSIDE = -(10**6)
VMEM_LIMIT = 24 * 2**20
F32 = jnp.float32
BF16 = jnp.bfloat16


def split(x):
    high = x.astype(BF16)
    return high, (x - high.astype(F32)).astype(BF16)


def dot(a, b, dims=((1,), (0,))):
    return lax.dot_general(a, b, (dims, ((), ())), preferred_element_type=F32)


def das_kernel(
    count,
    target,
    offset,
    echo_hbm,
    weights_hbm,
    grid_map,
    psf,
    own_out,
    send_out,
    mix_out,
    echo,
    weights,
    dense,
    arranged,
    sems,
    *,
    chans,
    lat,
    vox_total,
):
    slots, tile = weights.shape[0], weights.shape[1]
    chunk = slots // CHUNKS
    copies = [
        pltpu.make_async_copy(
            weights_hbm.at[pl.ds(i * chunk, chunk)], weights.at[pl.ds(i * chunk, chunk)], sems.at[i]
        )
        for i in range(CHUNKS)
    ]
    copies.append(pltpu.make_async_copy(echo_hbm, echo, sems.at[CHUNKS]))
    for copy in copies:
        copy.start()
    voxels = grid_map.shape[1]
    tiles_out = voxels // tile
    spans = echo.shape[0] // tile
    depth = voxels // lat
    width = depth // chans
    mix_out[0], mix_out[1] = correlation(psf, chans, lat, width, vox_total)
    live = count[0]
    dense[...] = jnp.zeros_like(dense)
    lanes = lax.broadcasted_iota(jnp.int32, (tile, tile), 1)

    def one_batch(turn, carry):
        for lane in range(BATCH):
            at = turn * BATCH + lane
            slot = jnp.minimum(at, slots - 1)
            goal = jnp.where(at < live, target[slot], tiles_out)
            first = offset[slot]
            span, shift = first // tile, first % tile
            turned = pltpu.roll(weights[slot].astype(F32), shift, 1)
            dense[goal, span] += jnp.where(lanes >= shift, turned, 0.0)
            dense[goal, span + 1] += jnp.where(lanes < shift, turned, 0.0)
        return carry

    turns = (live + BATCH - 1) // BATCH
    for i in range(CHUNKS):
        copies[i].wait()
        last = jnp.minimum(turns, (i + 1) * chunk // BATCH)
        lax.fori_loop(i * chunk // BATCH, last, one_batch, 0)
    copies[CHUNKS].wait()

    rows = []
    for t in range(tiles_out):
        rows.append(jnp.concatenate([dense[t, s] for s in range(spans)], axis=1))
    high, low = split(jnp.concatenate(rows, axis=0))
    data = echo[...].reshape(echo.shape[0], 2 * echo.shape[2])
    sums = dot(high, data) + dot(low, data)
    voxel_ids = lax.broadcasted_iota(jnp.int32, (voxels, voxels), 0)
    placing = (voxel_ids == grid_map[...]).astype(F32).astype(BF16)
    high, low = split(sums)
    arranged[...] = dot(placing, high, ((0,), (0,))) + dot(placing, low, ((0,), (0,)))
    mine = lax.axis_index("chan")
    for a in range(lat):
        for step in range(chans):
            first = pl.multiple_of(a * depth + (mine ^ step) * width, 8)
            rows = arranged[pl.ds(first, width), :]
            if step == 0:
                own_out[a * width : (a + 1) * width, :] = rows
            else:
                send_out[step - 1, a * width : (a + 1) * width, :] = rows.astype(BF16)


def gram_parts(a, b):
    con = ((0,), (0,))
    return [dot(a, a, con), dot(a, b, con), dot(b, b, con)]


def gram_kernel(*refs):
    out = refs[-1]
    count = (len(refs) - 1) // 2
    a = jnp.concatenate([r[...] for r in refs[:count]], axis=0)
    b = jnp.concatenate([r[...] for r in refs[count : 2 * count]], axis=0)
    for i, t in enumerate(gram_parts(a, b)):
        out[i] = t


def neighbours(chan, chans, width):
    if chans == 1:
        return []
    if chans == 2:
        start = jnp.where(chan == 0, 0, width - EDGE)
        return [(1, start, jnp.where(chan == 0, width, 0) + start)]
    sides = []
    for side in (-1, 1):
        near = jnp.clip(chan + side, 0, chans - 1)
        start = 0 if side == 1 else width - EDGE
        sides.append((chan ^ near, start, jnp.where(near == chan, OUTSIDE, near * width + start)))
    return sides


def correlation(psf, chans, lat, width, vox_total):
    vox = lax.axis_index("vox")
    chan = lax.axis_index("chan")
    n = lat * width
    lat_all = lat + 2 * HALO
    rows = lat_all * width
    sides = neighbours(chan, chans, width)
    total = rows + len(sides) * lat_all * EDGE
    outs = lax.broadcasted_iota(jnp.int32, (n, total), 0)
    ins = lax.broadcasted_iota(jnp.int32, (n, total), 1)
    lat_in = ins // width
    dep_in = chan * width + ins % width
    for s, (_, _, base) in enumerate(sides):
        local = ins - rows - s * lat_all * EDGE
        here = local >= 0
        lat_in = jnp.where(here, local // EDGE, lat_in)
        dep_in = jnp.where(here, base + local % EDGE, dep_in)
    tap_a = lat_in - outs // width
    tap_b = dep_in - (chan * width + outs % width) + HALO
    lat_grid = vox * lat + lat_in - HALO
    inside = (lat_grid >= 0) & (lat_grid < vox_total * lat)
    taps = 2 * HALO + 1
    valid = inside & (tap_a >= 0) & (tap_a < taps) & (tap_b >= 0) & (tap_b < taps)
    tap = jnp.where(valid, tap_a * taps + tap_b, -1)
    mix = jnp.zeros((n, total), F32)
    for i in range(taps):
        for j in range(taps):
            mix = jnp.where(tap == i * taps + j, psf[i, j], mix)
    return split(mix)


def filter_kernel(mix, *refs, fresh, inner, chans, lat, width, vox_total, frames):
    total_blocks = (len(refs) - 3) // 2
    gram = refs[2 * total_blocks] if not fresh else None
    mine = refs[:total_blocks]
    other = refs[total_blocks : 2 * total_blocks]
    out, mat_high, mat_low = refs[-3:]
    n = lat * width
    half = mine[0].shape[1]
    hf = half // 2
    vox = lax.axis_index("vox")
    chan = lax.axis_index("chan")
    if fresh:
        a = jnp.concatenate([r[...] for r in mine[:fresh]], axis=0)
        b = jnp.concatenate([r[...] for r in other[:fresh]], axis=0)
        parts = gram_parts(a, b)
    else:
        parts = [gram[i] for i in range(3)]

    def diag_sum(t):
        r = lax.broadcasted_iota(jnp.int32, (DIAG, DIAG), 0)
        c = lax.broadcasted_iota(jnp.int32, (DIAG, DIAG), 1)
        tiles = [t[i : i + DIAG, i : i + DIAG] for i in range(0, half, DIAG)]
        return jnp.sum(jnp.where(r == c, functools.reduce(jnp.add, tiles), 0.0))

    factor = frames / (diag_sum(parts[0]) + diag_sum(parts[2]))
    for i, t in enumerate(parts):
        real = t[:hf, :hf] + t[hf:, hf:]
        imag = t[:hf, hf:] - t[hf:, :hf]
        real_high, real_low = split(real)
        imag_high, imag_low = split(imag)
        for ref, re, im in ((mat_high, real_high, imag_high), (mat_low, real_low, imag_low)):
            ref[i, :hf, :hf] = re
            ref[i, hf:, hf:] = re
            ref[i, :hf, hf:] = im
            ref[i, hf:, :hf] = -im

    edge = HALO * width

    def border(blocks, v, away, cut):
        if vox_total > inner:
            return blocks[(inner if v < 0 else inner + 1) * chans + away][cut, :]
        distance = vox ^ jnp.clip(vox + v, 0, vox_total - 1)
        rows = blocks[away][cut, :].astype(F32)
        for d in range(1, inner):
            rows = jnp.where(distance == d, blocks[d * chans + away][cut, :].astype(F32), rows)
        return rows.astype(BF16)

    def column(blocks, away):
        return jnp.concatenate(
            [
                border(blocks, -1, away, slice(n - edge, n)),
                blocks[away][...],
                border(blocks, 1, away, slice(0, edge)),
            ],
            axis=0,
        )

    def any_column(blocks, away):
        if isinstance(away, int):
            return column(blocks, away)
        got = column(blocks, 0).astype(F32)
        for d in range(1, chans):
            got = jnp.where(away == d, column(blocks, d).astype(F32), got)
        return got.astype(BF16)

    lat_all = lat + 2 * HALO
    rows = lat_all * width
    pr = lax.broadcasted_iota(jnp.int32, (lat_all * EDGE, rows), 0)
    pc = lax.broadcasted_iota(jnp.int32, (lat_all * EDGE, rows), 1)
    x_rows = [[column(mine, 0)], [column(other, 0)]]
    for away, start, _ in neighbours(chan, chans, width):
        pick = (pr // EDGE == pc // width) & (pc % width == start + pr % EDGE)
        pick = pick.astype(F32).astype(BF16)
        for which, blocks in enumerate((mine, other)):
            x_rows[which].append(dot(pick, any_column(blocks, away)).astype(BF16))
    xa, xb = (jnp.concatenate(x, axis=0) for x in x_rows)

    def product(z, i, back=False):
        high, low = mat_high[i], mat_low[i]
        if len(z) == 1:
            left, right = [z[0]], [high]
        else:
            left, right = [z[0], z[1], z[0]], [high, high, low]
        axis = 1 if back else 0
        return dot(
            jnp.concatenate(left, axis=1), jnp.concatenate(right, axis=axis), ((1,), (axis,))
        )

    c0, c1, c2, c3 = POLY_COEFFS
    fa, fb = xa.astype(F32), xb.astype(F32)
    first = c3 * factor
    za = first * (product([xa], 0) + product([xb], 1, True)) + c2 * fa
    zb = first * (product([xa], 1) + product([xb], 2)) + c2 * fb
    sa, sb = split(za), split(zb)
    za = factor * (product(sa, 0) + product(sb, 1, True)) + c1 * fa
    zb = factor * (product(sa, 1) + product(sb, 2)) + c1 * fb
    sa, sb = split(za), split(zb)
    za = factor * (product(sa, 0) + product(sb, 1, True)) + c0 * fa
    env = jnp.sqrt(za[:, :hf] * za[:, :hf] + za[:, hf:] * za[:, hf:] + 1e-06)
    eh, el = split(env)
    mh, ml = mix[0], mix[1]
    out[...] = dot(mh, eh) + dot(ml, eh) + dot(mh, el)


def shards(mesh, echo_data, tile_weights, tile_target, tile_offset, tile_count, grid_map, psf_kernel):
    rows, hf = echo_data.shape[2], echo_data.shape[4]
    slots, tile = tile_weights.shape[2], tile_weights.shape[3]
    voxels = grid_map.shape[1]
    chans, vox_total, frms = mesh.shape["chan"], mesh.shape["vox"], mesh.shape["frm"]
    lat = 8
    width = voxels // lat // chans
    n = lat * width
    smem = pl.BlockSpec(memory_space=pltpu.SMEM)
    vmem = pl.BlockSpec(memory_space=pltpu.VMEM)
    hbm = pl.BlockSpec(memory_space=pl.ANY)
    echo = echo_data.reshape(rows, 2, hf)
    seen = (lat + 2 * HALO) * (width + min(chans - 1, 2) * EDGE)
    own, sent, mix = pl.pallas_call(
        functools.partial(das_kernel, chans=chans, lat=lat, vox_total=vox_total),
        out_shape=(
            pltpu.VMEM((n, 2 * hf), F32),
            pltpu.VMEM((chans - 1, n, 2 * hf), BF16),
            pltpu.VMEM((2, n, seen), BF16),
        ),
        in_specs=[smem, smem, smem, hbm, hbm, vmem, smem],
        out_specs=(vmem, vmem, vmem),
        scratch_shapes=[
            pltpu.VMEM((rows, 2, hf), BF16),
            pltpu.VMEM((slots, tile, tile), BF16),
            pltpu.VMEM((voxels // tile + 1, rows // tile + 1, tile, tile), F32),
            pltpu.VMEM((voxels, 2 * hf), F32),
            pltpu.SemaphoreType.DMA((CHUNKS + 1,)),
        ],
        compiler_params=pltpu.CompilerParams(vmem_limit_bytes=56 * 2**20),
    )(
        tile_count.reshape(-1),
        tile_target.reshape(-1),
        tile_offset.reshape(-1),
        echo,
        tile_weights.reshape(slots, tile, tile),
        grid_map,
        psf_kernel,
    )
    inner = min(vox_total, 4)

    def peer(x, dv, dc):
        pairs = [
            (v * chans + c, (v ^ dv) * chans + (c ^ dc))
            for v in range(vox_total)
            for c in range(chans)
        ]
        return lax.ppermute(x, ("vox", "chan"), pairs)

    for step in range(1, chans):
        own = own + peer(sent[step - 1], 0, step).astype(F32)
    own = own.astype(BF16)
    crossed = peer(own, inner // 2, 0)
    near = [(dv, dc) for dv in range(inner // 2) for dc in range(chans)]
    mine = [own] + [peer(own, dv, dc) for dv, dc in near[1:]]
    mine += [crossed] + [peer(crossed, dv, dc) for dv, dc in near[1:]]

    def to_other(x):
        return lax.ppermute(x, "frm", [(f, f ^ 1) for f in range(frms)])

    groups = inner * chans
    other = [to_other(x) for x in mine]

    def gram_of(a, b):
        cost = pl.CostEstimate(
            flops=6 * len(a) * n * (2 * hf) ** 2, bytes_accessed=12 * (2 * hf) ** 2, transcendentals=0
        )
        return pl.pallas_call(
            gram_kernel,
            out_shape=jax.ShapeDtypeStruct((3, 2 * hf, 2 * hf), F32),
            in_specs=[vmem] * (2 * len(a)),
            out_specs=vmem,
            cost_estimate=cost,
            compiler_params=pltpu.CompilerParams(vmem_limit_bytes=VMEM_LIMIT),
        )(*a, *b)

    fresh, gram = groups, []
    if vox_total > inner:
        fresh, gram = 0, [gram_of(mine, other)]
        away = inner
        while away < vox_total:
            gram = [gram[0] + peer(gram[0], away, 0)]
            away *= 2
        for go in (1, -1):
            pairs = [(v, v + go) for v in range(vox_total) if 0 <= v + go < vox_total]
            mine += [lax.ppermute(x, "vox", pairs) for x in mine[:chans]]
            other += [lax.ppermute(x, "vox", pairs) for x in other[:chans]]
    blocks = len(mine)
    out = pl.pallas_call(
        functools.partial(
            filter_kernel,
            fresh=fresh,
            inner=inner,
            chans=chans,
            lat=lat,
            width=width,
            vox_total=vox_total,
            frames=float(frms * hf),
        ),
        out_shape=jax.ShapeDtypeStruct((n, hf), F32),
        in_specs=[vmem] * (1 + 2 * blocks + len(gram)),
        out_specs=vmem,
        scratch_shapes=[
            pltpu.VMEM((3, 2 * hf, 2 * hf), BF16),
            pltpu.VMEM((3, 2 * hf, 2 * hf), BF16),
        ],
        compiler_params=pltpu.CompilerParams(vmem_limit_bytes=VMEM_LIMIT),
    )(mix, *mine, *other, *gram)
    return out.reshape(lat, width, hf)


def solution(mesh):
    in_specs = (
        P(("groups", "vox"), "chan", None, None, "frm"),
        P("vox", "chan", None, None, None),
        P("vox", "chan", None),
        P("vox", "chan", None),
        P("vox", "chan"),
        P("vox", None),
        P(),
    )
    out_specs = P(("groups", "vox"), "chan", "frm")
    return jax.shard_map(
        functools.partial(shards, mesh),
        mesh=mesh,
        in_specs=in_specs,
        out_specs=out_specs,
        check_vma=False,
    )
```

time: 41.5 us -> 39.5 us (0.952)
  starting transfers between devices: 17.2 us -> 13.6 us
  waiting for transfers between devices: 11 us -> 13.3 us
  Pallas kernels: 12.3 us -> 11.3 us
    ppermute x8, starting transfers between devices: 16.5 us -> 12.5 us  [peer(): return lax.ppermute(x, ('vox', 'chan'), pairs)]
    ppermute x8, waiting for transfers between devices: 10.8 us -> 12.3 us  [peer(): return lax.ppermute(x, ('vox', 'chan'), pairs)]
    pallas_call x1, Pallas kernels: 7.23 us -> 5.85 us  [shards(): pl.pallas_call(functools.partial(filter_kernel, fresh=fresh, inner=inner,...]
    ppermute x8, waiting for transfers between devices: 0.22 us -> 1.03 us  [to_other(): return lax.ppermute(x, 'frm', [(f, f ^ 1) for f in range(frms)])]
    pallas_call x2 -> x1, Pallas kernels: 5.07 us -> 5.43 us  [shards(): pl.pallas_call(functools.partial(das_kernel, chans=chans, lat=lat, vox_to...]
  transfers between devices with their start and end apart: 16 -> 16, of which waited for: 9 -> 10; matrix products, arithmetic and copies ran while one was open for 0% -> 0% of each run, Pallas kernels for 2% -> 0%
where the time goes in v3:
time: 39.5 us; the launch traced here: 38.9 us
  starting transfers between devices  13.6 us (34%)
  waiting for transfers between devices  13.3 us (34%)
  Pallas kernels  11.3 us (29%)
  between operations  0.68 us (2%)
    ppermute x8, starting transfers between devices, peer(): return lax.ppermute(x, ('vox', 'chan'), pairs)  12.5 us
    ppermute x8, waiting for transfers between devices, peer(): return lax.ppermute(x, ('vox', 'chan'), pairs)  12.3 us
    pallas_call x1, Pallas kernels, shards(): pl.pallas_call(functools.partial(filter_kernel, fresh=fresh, inner=inner,...  5.85 us
    pallas_call x1, Pallas kernels, shards(): pl.pallas_call(functools.partial(das_kernel, chans=chans, lat=lat, vox_to...  5.43 us
    ppermute x8, starting transfers between devices, to_other(): return lax.ppermute(x, 'frm', [(f, f ^ 1) for f in range(frms)])  1.03 us
    ppermute x8, waiting for transfers between devices, to_other(): return lax.ppermute(x, 'frm', [(f, f ^ 1) for f in range(frms)])  1.03 us
  transfers between devices with their start and end apart: 16, of which 10 were waited for; matrix products, arithmetic and copies ran while one was open for 0% of the time, Pallas kernels for 0%

profile of v3, /device:TPU:0, one launch (start us, length us, event | category | flops | bytes accessed | tf_op | source)
XLA Modules:
  0.0 38.9 jit_solution(5343192163817212326)
XLA Ops:
  0.7 5.4 %shard_map.73 = (f32[128,512]{1,0:T(8,128)S(1)}, bf16[1,128,512]{2,1,0:T(8,128)(2,1)S(1)}, bf16[2,128,216]{2,1,0:T(8,128)(2,1)S(1)}) custom-call(s32[1]{0:T(128)} %bitcast.7.count, s32[64]{0:T(128)} %bitcast.11, s32[64]{0:T(128)} %bitcast.12, bf16[1024,2,256]{2,1,0:T(2,128)(2,1)} %bitcast.10, bf16[64,128,128]{2,1,0:T(8,128)(2,1)} %bitcast.9, ...), custom_call_target="tpu_custom_call" | custom-call | tf_op jit(solution)/shard_map/pallas_call | solution.py:289
  6.1 1.8 %collective-permute-start = (bf16[128,512]{1,0:T(8,128)(2,1)S(1)}, bf16[128,512]{1,0:T(8,128)(2,1)S(1)}, u32[]{:S(2)}, u32[]{:S(2)}) collective-permute-start(bf16[128,512]{1,0:T(8,128)(2,1)S(1)} %bitcast.8), channel_id=1, source_target_pairs={{0,2},{2,0},{4,6},{6,4},{8,10},{10,8},{12,14},{14,12},{1,3},{3,1},... | collective-permute-start | bytes 393224 | tf_op jit(solution)/shard_map/ppermute | solution.py:323
  7.9 4.1 %collective-permute-done = bf16[128,512]{1,0:T(8,128)(2,1)S(1)} collective-permute-done((bf16[128,512]{1,0:T(8,128)(2,1)S(1)}, bf16[128,512]{1,0:T(8,128)(2,1)S(1)}, u32[]{:S(2)}, u32[]{:S(2)}) %collective-permute-start) | collective-permute-done | bytes 131104 | tf_op jit(solution)/shard_map/ppermute | solution.py:323
  12.0 3.5 %collective-permute-start.4 = (bf16[128,512]{1,0:T(8,128)(2,1)S(1)}, bf16[128,512]{1,0:T(8,128)(2,1)S(1)}, u32[]{:S(2)}, u32[]{:S(2)}) collective-permute-start(bf16[128,512]{1,0:T(8,128)(2,1)S(1)} %add_convert_fusion.refs_0_), channel_id=1, source_target_pairs={{0,8},{2,10},{4,12},{6,14},{8,0},{10,2},{12,4},{14,6},{1,9},{3,11}... | collective-permute-start | bytes 393224 | tf_op jit(solution)/shard_map/ppermute | solution.py:323
  15.5 0.0 collective-permute-start.8
  15.5 2.5 %collective-permute-start.3 = (bf16[128,512]{1,0:T(8,128)(2,1)S(1)}, bf16[128,512]{1,0:T(8,128)(2,1)S(1)}, u32[]{:S(2)}, u32[]{:S(2)}) collective-permute-start(bf16[128,512]{1,0:T(8,128)(2,1)S(1)} %add_convert_fusion.refs_0_), channel_id=1, source_target_pairs={{0,6},{2,4},{4,2},{6,0},{8,14},{10,12},{12,10},{14,8},{1,7},{3,5},... | collective-permute-start | bytes 393224 | tf_op jit(solution)/shard_map/ppermute | solution.py:323
  18.1 0.0 collective-permute-start.2
  18.1 1.0 %collective-permute-start.1 = (bf16[128,512]{1,0:T(8,128)(2,1)S(1)}, bf16[128,512]{1,0:T(8,128)(2,1)S(1)}, u32[]{:S(2)}, u32[]{:S(2)}) collective-permute-start(bf16[128,512]{1,0:T(8,128)(2,1)S(1)} %add_convert_fusion.refs_0_), channel_id=1, source_target_pairs={{0,2},{2,0},{4,6},{6,4},{8,10},{10,8},{12,14},{14,12},{1,3},{3,1},... | collective-permute-start | bytes 393224 | tf_op jit(solution)/shard_map/ppermute | solution.py:323
  19.0 1.7 %collective-permute-done.4.refs_4_ = bf16[128,512]{1,0:T(8,128)(2,1)S(1)} collective-permute-done((bf16[128,512]{1,0:T(8,128)(2,1)S(1)}, bf16[128,512]{1,0:T(8,128)(2,1)S(1)}, u32[]{:S(2)}, u32[]{:S(2)}) %collective-permute-start.4) | collective-permute-done | bytes 131104 | tf_op jit(solution)/shard_map/ppermute | solution.py:323
  20.7 0.0 collective-permute-start.12
  20.7 1.7 %collective-permute-start.7 = (bf16[128,512]{1,0:T(8,128)(2,1)S(1)}, bf16[128,512]{1,0:T(8,128)(2,1)S(1)}, u32[]{:S(2)}, u32[]{:S(2)}) collective-permute-start(bf16[128,512]{1,0:T(8,128)(2,1)S(1)} %collective-permute-done.4.refs_4_), channel_id=1, source_target_pairs={{0,6},{2,4},{4,2},{6,0},{8,14},{10,12},{12,10},{14,8},{1,7},{3,5},... | collective-permute-start | bytes 393224 | tf_op jit(solution)/shard_map/ppermute | solution.py:323
  22.4 0.9 %collective-permute-done.3.refs_3_ = bf16[128,512]{1,0:T(8,128)(2,1)S(1)} collective-permute-done((bf16[128,512]{1,0:T(8,128)(2,1)S(1)}, bf16[128,512]{1,0:T(8,128)(2,1)S(1)}, u32[]{:S(2)}, u32[]{:S(2)}) %collective-permute-start.3) | collective-permute-done | bytes 131104 | tf_op jit(solution)/shard_map/ppermute | solution.py:323
  23.3 0.8 %collective-permute-start.6 = (bf16[128,512]{1,0:T(8,128)(2,1)S(1)}, bf16[128,512]{1,0:T(8,128)(2,1)S(1)}, u32[]{:S(2)}, u32[]{:S(2)}) collective-permute-start(bf16[128,512]{1,0:T(8,128)(2,1)S(1)} %collective-permute-done.4.refs_4_), channel_id=1, source_target_pairs={{0,4},{2,6},{4,0},{6,2},{8,12},{10,14},{12,8},{14,10},{1,5},{3,7},... | collective-permute-start | bytes 393224 | tf_op jit(solution)/shard_map/ppermute | solution.py:323
  24.1 1.4 %collective-permute-done.2.refs_2_ = bf16[128,512]{1,0:T(8,128)(2,1)S(1)} collective-permute-done((bf16[128,512]{1,0:T(8,128)(2,1)S(1)}, bf16[128,512]{1,0:T(8,128)(2,1)S(1)}, u32[]{:S(2)}, u32[]{:S(2)}) %collective-permute-start.2) | collective-permute-done | bytes 131104 | tf_op jit(solution)/shard_map/ppermute | solution.py:323
  25.4 1.2 %collective-permute-start.5 = (bf16[128,512]{1,0:T(8,128)(2,1)S(1)}, bf16[128,512]{1,0:T(8,128)(2,1)S(1)}, u32[]{:S(2)}, u32[]{:S(2)}) collective-permute-start(bf16[128,512]{1,0:T(8,128)(2,1)S(1)} %collective-permute-done.4.refs_4_), channel_id=1, source_target_pairs={{0,2},{2,0},{4,6},{6,4},{8,10},{10,8},{12,14},{14,12},{1,3},{3,1},... | collective-permute-start | bytes 393224 | tf_op jit(solution)/shard_map/ppermute | solution.py:323
  26.7 0.5 %collective-permute-start.10 = (bf16[128,512]{1,0:T(8,128)(2,1)S(1)}, bf16[128,512]{1,0:T(8,128)(2,1)S(1)}, u32[]{:S(2)}, u32[]{:S(2)}) collective-permute-start(bf16[128,512]{1,0:T(8,128)(2,1)S(1)} %collective-permute-done.2.refs_2_), channel_id=1, source_target_pairs={{0,1},{1,0},{2,3},{3,2},{4,5},{5,4},{6,7},{7,6},{8,9},{9,8},{10,11... | collective-permute-start | bytes 393224 | tf_op jit(solution)/shard_map/ppermute | solution.py:334
  27.2 1.7 %collective-permute-done.7.refs_7_ = bf16[128,512]{1,0:T(8,128)(2,1)S(1)} collective-permute-done((bf16[128,512]{1,0:T(8,128)(2,1)S(1)}, bf16[128,512]{1,0:T(8,128)(2,1)S(1)}, u32[]{:S(2)}, u32[]{:S(2)}) %collective-permute-start.7) | collective-permute-done | bytes 131104 | tf_op jit(solution)/shard_map/ppermute | solution.py:323
  28.9 1.9 %collective-permute-done.6.refs_6_ = bf16[128,512]{1,0:T(8,128)(2,1)S(1)} collective-permute-done((bf16[128,512]{1,0:T(8,128)(2,1)S(1)}, bf16[128,512]{1,0:T(8,128)(2,1)S(1)}, u32[]{:S(2)}, u32[]{:S(2)}) %collective-permute-start.6) | collective-permute-done | bytes 131104 | tf_op jit(solution)/shard_map/ppermute | solution.py:323
  30.8 0.7 %collective-permute-done.5.refs_5_ = bf16[128,512]{1,0:T(8,128)(2,1)S(1)} collective-permute-done((bf16[128,512]{1,0:T(8,128)(2,1)S(1)}, bf16[128,512]{1,0:T(8,128)(2,1)S(1)}, u32[]{:S(2)}, u32[]{:S(2)}) %collective-permute-start.5) | collective-permute-done | bytes 131104 | tf_op jit(solution)/shard_map/ppermute | solution.py:323
  31.5 0.5 %collective-permute-start.13 = (bf16[128,512]{1,0:T(8,128)(2,1)S(1)}, bf16[128,512]{1,0:T(8,128)(2,1)S(1)}, u32[]{:S(2)}, u32[]{:S(2)}) collective-permute-start(bf16[128,512]{1,0:T(8,128)(2,1)S(1)} %collective-permute-done.5.refs_5_), channel_id=1, source_target_pairs={{0,1},{1,0},{2,3},{3,2},{4,5},{5,4},{6,7},{7,6},{8,9},{9,8},{10,11... | collective-permute-start | bytes 393224 | tf_op jit(solution)/shard_map/ppermute | solution.py:334
  32.0 0.2 collective-permute-done.15.refs_15_
  32.2 0.7 %collective-permute-done.14.refs_14_ = bf16[128,512]{1,0:T(8,128)(2,1)S(1)} collective-permute-done((bf16[128,512]{1,0:T(8,128)(2,1)S(1)}, bf16[128,512]{1,0:T(8,128)(2,1)S(1)}, u32[]{:S(2)}, u32[]{:S(2)}) %collective-permute-start.14) | collective-permute-done | bytes 131104 | tf_op jit(solution)/shard_map/ppermute | solution.py:334
  32.9 0.2 collective-permute-done.13.refs_13_
  33.0 5.8 %shard_map.74 = f32[128,256]{1,0:T(8,128)} custom-call(bf16[2,128,216]{2,1,0:T(8,128)(2,1)S(1)} %get-tuple-element.8.mix, bf16[128,512]{1,0:T(8,128)(2,1)S(1)} %add_convert_fusion.refs_0_, bf16[128,512]{1,0:T(8,128)(2,1)S(1)} %collective-permute-done.1.refs_1_, bf16[128,512]{1,0:T(8,128)(2,1)S(1)} %collective-permute-done.2.refs_2_, ...), custom_call_target="tpu_custom_call" | custom-call | tf_op jit(solution)/shard_map/pallas_call | solution.py:364
  (11 shorter events, 0.1 us)
Async XLA Ops:
  6.1 5.9 %collective-permute-start = (bf16[128,512]{1,0:T(8,128)(2,1)S(1)}, bf16[128,512]{1,0:T(8,128)(2,1)S(1)}, u32[]{:S(2)}, u32[]{:S(2)}) collective-permute-start(bf16[128,512]{1,0:T(8,128)(2,1)S(1)} %bitcast.8), channel_id=1, source_target_pairs={{0,2},{2,0},{4,6},{6,4},{8,10},{10,8},{12,14},{14,12},{1,3},{3,1},... | collective-permute-start | bytes 393224 | tf_op jit(solution)/shard_map/ppermute | solution.py:323
  12.0 8.6 %collective-permute-start.4 = (bf16[128,512]{1,0:T(8,128)(2,1)S(1)}, bf16[128,512]{1,0:T(8,128)(2,1)S(1)}, u32[]{:S(2)}, u32[]{:S(2)}) collective-permute-start(bf16[128,512]{1,0:T(8,128)(2,1)S(1)} %add_convert_fusion.refs_0_), channel_id=1, source_target_pairs={{0,8},{2,10},{4,12},{6,14},{8,0},{10,2},{12,4},{14,6},{1,9},{3,11}... | collective-permute-start | bytes 393224 | tf_op jit(solution)/shard_map/ppermute | solution.py:323
  15.5 5.2 %collective-permute-start.8 = (bf16[128,512]{1,0:T(8,128)(2,1)S(1)}, bf16[128,512]{1,0:T(8,128)(2,1)S(1)}, u32[]{:S(2)}, u32[]{:S(2)}) collective-permute-start(bf16[128,512]{1,0:T(8,128)(2,1)S(1)} %add_convert_fusion.refs_0_), channel_id=1, source_target_pairs={{0,1},{1,0},{2,3},{3,2},{4,5},{5,4},{6,7},{7,6},{8,9},{9,8},{10,11... | collective-permute-start | bytes 393224 | tf_op jit(solution)/shard_map/ppermute | solution.py:334
  15.5 7.8 %collective-permute-start.3 = (bf16[128,512]{1,0:T(8,128)(2,1)S(1)}, bf16[128,512]{1,0:T(8,128)(2,1)S(1)}, u32[]{:S(2)}, u32[]{:S(2)}) collective-permute-start(bf16[128,512]{1,0:T(8,128)(2,1)S(1)} %add_convert_fusion.refs_0_), channel_id=1, source_target_pairs={{0,6},{2,4},{4,2},{6,0},{8,14},{10,12},{12,10},{14,8},{1,7},{3,5},... | collective-permute-start | bytes 393224 | tf_op jit(solution)/shard_map/ppermute | solution.py:323
  18.1 7.4 %collective-permute-start.2 = (bf16[128,512]{1,0:T(8,128)(2,1)S(1)}, bf16[128,512]{1,0:T(8,128)(2,1)S(1)}, u32[]{:S(2)}, u32[]{:S(2)}) collective-permute-start(bf16[128,512]{1,0:T(8,128)(2,1)S(1)} %add_convert_fusion.refs_0_), channel_id=1, source_target_pairs={{0,4},{2,6},{4,0},{6,2},{8,12},{10,14},{12,8},{14,10},{1,5},{3,7},... | collective-permute-start | bytes 393224 | tf_op jit(solution)/shard_map/ppermute | solution.py:323
  18.1 8.6 %collective-permute-start.1 = (bf16[128,512]{1,0:T(8,128)(2,1)S(1)}, bf16[128,512]{1,0:T(8,128)(2,1)S(1)}, u32[]{:S(2)}, u32[]{:S(2)}) collective-permute-start(bf16[128,512]{1,0:T(8,128)(2,1)S(1)} %add_convert_fusion.refs_0_), channel_id=1, source_target_pairs={{0,2},{2,0},{4,6},{6,4},{8,10},{10,8},{12,14},{14,12},{1,3},{3,1},... | collective-permute-start | bytes 393224 | tf_op jit(solution)/shard_map/ppermute | solution.py:323
  20.7 6.0 %collective-permute-start.12 = (bf16[128,512]{1,0:T(8,128)(2,1)S(1)}, bf16[128,512]{1,0:T(8,128)(2,1)S(1)}, u32[]{:S(2)}, u32[]{:S(2)}) collective-permute-start(bf16[128,512]{1,0:T(8,128)(2,1)S(1)} %collective-permute-done.4.refs_4_), channel_id=1, source_target_pairs={{0,1},{1,0},{2,3},{3,2},{4,5},{5,4},{6,7},{7,6},{8,9},{9,8},{10,11... | collective-permute-start | bytes 393224 | tf_op jit(solution)/shard_map/ppermute | solution.py:334
  20.7 8.2 %collective-permute-start.7 = (bf16[128,512]{1,0:T(8,128)(2,1)S(1)}, bf16[128,512]{1,0:T(8,128)(2,1)S(1)}, u32[]{:S(2)}, u32[]{:S(2)}) collective-permute-start(bf16[128,512]{1,0:T(8,128)(2,1)S(1)} %collective-permute-done.4.refs_4_), channel_id=1, source_target_pairs={{0,6},{2,4},{4,2},{6,0},{8,14},{10,12},{12,10},{14,8},{1,7},{3,5},... | collective-permute-start | bytes 393224 | tf_op jit(solution)/shard_map/ppermute | solution.py:323
  23.3 7.5 %collective-permute-start.6 = (bf16[128,512]{1,0:T(8,128)(2,1)S(1)}, bf16[128,512]{1,0:T(8,128)(2,1)S(1)}, u32[]{:S(2)}, u32[]{:S(2)}) collective-permute-start(bf16[128,512]{1,0:T(8,128)(2,1)S(1)} %collective-permute-done.4.refs_4_), channel_id=1, source_target_pairs={{0,4},{2,6},{4,0},{6,2},{8,12},{10,14},{12,8},{14,10},{1,5},{3,7},... | collective-permute-start | bytes 393224 | tf_op jit(solution)/shard_map/ppermute | solution.py:323
  25.4 6.1 %collective-permute-start.5 = (bf16[128,512]{1,0:T(8,128)(2,1)S(1)}, bf16[128,512]{1,0:T(8,128)(2,1)S(1)}, u32[]{:S(2)}, u32[]{:S(2)}) collective-permute-start(bf16[128,512]{1,0:T(8,128)(2,1)S(1)} %collective-permute-done.4.refs_4_), channel_id=1, source_target_pairs={{0,2},{2,0},{4,6},{6,4},{8,10},{10,8},{12,14},{14,12},{1,3},{3,1},... | collective-permute-start | bytes 393224 | tf_op jit(solution)/shard_map/ppermute | solution.py:323
  26.7 4.8 %collective-permute-start.11 = (bf16[128,512]{1,0:T(8,128)(2,1)S(1)}, bf16[128,512]{1,0:T(8,128)(2,1)S(1)}, u32[]{:S(2)}, u32[]{:S(2)}) collective-permute-start(bf16[128,512]{1,0:T(8,128)(2,1)S(1)} %collective-permute-done.3.refs_3_), channel_id=1, source_target_pairs={{0,1},{1,0},{2,3},{3,2},{4,5},{5,4},{6,7},{7,6},{8,9},{9,8},{10,11... | collective-permute-start | bytes 393224 | tf_op jit(solution)/shard_map/ppermute | solution.py:334
  26.7 5.3 %collective-permute-start.10 = (bf16[128,512]{1,0:T(8,128)(2,1)S(1)}, bf16[128,512]{1,0:T(8,128)(2,1)S(1)}, u32[]{:S(2)}, u32[]{:S(2)}) collective-permute-start(bf16[128,512]{1,0:T(8,128)(2,1)S(1)} %collective-permute-done.2.refs_2_), channel_id=1, source_target_pairs={{0,1},{1,0},{2,3},{3,2},{4,5},{5,4},{6,7},{7,6},{8,9},{9,8},{10,11... | collective-permute-start | bytes 393224 | tf_op jit(solution)/shard_map/ppermute | solution.py:334
  28.9 3.1 %collective-permute-start.9 = (bf16[128,512]{1,0:T(8,128)(2,1)S(1)}, bf16[128,512]{1,0:T(8,128)(2,1)S(1)}, u32[]{:S(2)}, u32[]{:S(2)}) collective-permute-start(bf16[128,512]{1,0:T(8,128)(2,1)S(1)} %collective-permute-done.1.refs_1_), channel_id=1, source_target_pairs={{0,1},{1,0},{2,3},{3,2},{4,5},{5,4},{6,7},{7,6},{8,9},{9,8},{10,11... | collective-permute-start | bytes 393224 | tf_op jit(solution)/shard_map/ppermute | solution.py:334
  30.8 1.3 %collective-permute-start.15 = (bf16[128,512]{1,0:T(8,128)(2,1)S(1)}, bf16[128,512]{1,0:T(8,128)(2,1)S(1)}, u32[]{:S(2)}, u32[]{:S(2)}) collective-permute-start(bf16[128,512]{1,0:T(8,128)(2,1)S(1)} %collective-permute-done.7.refs_7_), channel_id=1, source_target_pairs={{0,1},{1,0},{2,3},{3,2},{4,5},{5,4},{6,7},{7,6},{8,9},{9,8},{10,11... | collective-permute-start | bytes 393224 | tf_op jit(solution)/shard_map/ppermute | solution.py:334
  31.5 1.3 %collective-permute-start.14 = (bf16[128,512]{1,0:T(8,128)(2,1)S(1)}, bf16[128,512]{1,0:T(8,128)(2,1)S(1)}, u32[]{:S(2)}, u32[]{:S(2)}) collective-permute-start(bf16[128,512]{1,0:T(8,128)(2,1)S(1)} %collective-permute-done.6.refs_6_), channel_id=1, source_target_pairs={{0,1},{1,0},{2,3},{3,2},{4,5},{5,4},{6,7},{7,6},{8,9},{9,8},{10,11... | collective-permute-start | bytes 393224 | tf_op jit(solution)/shard_map/ppermute | solution.py:334
  31.5 1.5 %collective-permute-start.13 = (bf16[128,512]{1,0:T(8,128)(2,1)S(1)}, bf16[128,512]{1,0:T(8,128)(2,1)S(1)}, u32[]{:S(2)}, u32[]{:S(2)}) collective-permute-start(bf16[128,512]{1,0:T(8,128)(2,1)S(1)} %collective-permute-done.5.refs_5_), channel_id=1, source_target_pairs={{0,1},{1,0},{2,3},{3,2},{4,5},{5,4},{6,7},{7,6},{8,9},{9,8},{10,11... | collective-permute-start | bytes 393224 | tf_op jit(solution)/shard_map/ppermute | solution.py:334

commit v4 on v3

--- a/solution.py
+++ b/solution.py
@@ -9,7 +9,7 @@
 
 POLY_COEFFS = (1.0, -0.6, 0.15, -0.03)
 HALO = 2
-BATCH = 4
+BATCH = 8
 CHUNKS = 4
 EDGE = 2
 DIAG = 128
@@ -334,6 +334,9 @@
         return lax.ppermute(x, "frm", [(f, f ^ 1) for f in range(frms)])
 
     groups = inner * chans
+    part = groups // 2
+    tied = lax.optimization_barrier(tuple(mine[1:part] + mine[part + 1 : part + 3]))
+    mine = [mine[0], *tied[: part - 1], mine[part], *tied[part - 1 :], *mine[part + 3 :]]
     other = [to_other(x) for x in mine]
 
     def gram_of(a, b):

time: 39.5 us -> 38.6 us (0.977)
  starting transfers between devices: 13.6 us -> 15.2 us
  Pallas kernels: 11.3 us -> 10.1 us
  waiting for transfers between devices: 13.3 us -> 12.4 us
    ppermute x8, waiting for transfers between devices: 12.3 us -> 11.1 us  [peer(): return lax.ppermute(x, ('vox', 'chan'), pairs)]
    pallas_call x1, Pallas kernels: 5.43 us -> 4.24 us  [shards(): pl.pallas_call(functools.partial(das_kernel, chans=chans, lat=lat, vox_to...]
    ppermute x8, starting transfers between devices: 12.5 us -> 13.6 us  [peer(): return lax.ppermute(x, ('vox', 'chan'), pairs)]
    ppermute x8, starting transfers between devices: 1.03 us -> 1.6 us  [to_other(): return lax.ppermute(x, 'frm', [(f, f ^ 1) for f in range(frms)])]
where the time goes in v4:
time: 38.6 us; the launch traced here: 38.3 us
  starting transfers between devices  15.2 us (39%)
  waiting for transfers between devices  12.4 us (32%)
  Pallas kernels  10.1 us (26%)
  between operations  0.68 us (2%)
    ppermute x8, starting transfers between devices, peer(): return lax.ppermute(x, ('vox', 'chan'), pairs)  13.6 us
    ppermute x8, waiting for transfers between devices, peer(): return lax.ppermute(x, ('vox', 'chan'), pairs)  11.1 us
    pallas_call x1, Pallas kernels, shards(): pl.pallas_call(functools.partial(filter_kernel, fresh=fresh, inner=inner,...  5.85 us
    pallas_call x1, Pallas kernels, shards(): pl.pallas_call(functools.partial(das_kernel, chans=chans, lat=lat, vox_to...  4.24 us
    ppermute x8, starting transfers between devices, to_other(): return lax.ppermute(x, 'frm', [(f, f ^ 1) for f in range(frms)])  1.6 us
    ppermute x8, waiting for transfers between devices, to_other(): return lax.ppermute(x, 'frm', [(f, f ^ 1) for f in range(frms)])  1.28 us
  transfers between devices with their start and end apart: 16, of which 10 were waited for; matrix products, arithmetic and copies ran while one was open for 0% of the time, Pallas kernels for 0%

profile of v4, /device:TPU:0, one launch (start us, length us, event | category | flops | bytes accessed | tf_op | source)
XLA Modules:
  0.0 38.3 jit_solution(12389139183940914349)
XLA Ops:
  0.7 4.2 %shard_map.73 = (f32[128,512]{1,0:T(8,128)S(1)}, bf16[1,128,512]{2,1,0:T(8,128)(2,1)S(1)}, bf16[2,128,216]{2,1,0:T(8,128)(2,1)S(1)}) custom-call(s32[1]{0:T(128)} %bitcast.7.count, s32[64]{0:T(128)} %bitcast.11, s32[64]{0:T(128)} %bitcast.12, bf16[1024,2,256]{2,1,0:T(2,128)(2,1)} %bitcast.10, bf16[64,128,128]{2,1,0:T(8,128)(2,1)} %bitcast.9, ...), custom_call_target="tpu_custom_call" | custom-call | tf_op jit(solution)/shard_map/pallas_call | solution.py:289
  4.9 3.6 %collective-permute-start = (bf16[128,512]{1,0:T(8,128)(2,1)S(1)}, bf16[128,512]{1,0:T(8,128)(2,1)S(1)}, u32[]{:S(2)}, u32[]{:S(2)}) collective-permute-start(bf16[128,512]{1,0:T(8,128)(2,1)S(1)} %bitcast.8), channel_id=1, source_target_pairs={{0,2},{2,0},{4,6},{6,4},{8,10},{10,8},{12,14},{14,12},{1,3},{3,1},... | collective-permute-start | bytes 393224 | tf_op jit(solution)/shard_map/ppermute | solution.py:323
  8.5 3.5 %collective-permute-done = bf16[128,512]{1,0:T(8,128)(2,1)S(1)} collective-permute-done((bf16[128,512]{1,0:T(8,128)(2,1)S(1)}, bf16[128,512]{1,0:T(8,128)(2,1)S(1)}, u32[]{:S(2)}, u32[]{:S(2)}) %collective-permute-start) | collective-permute-done | bytes 131104 | tf_op jit(solution)/shard_map/ppermute | solution.py:323
  12.0 2.7 %collective-permute-start.4 = (bf16[128,512]{1,0:T(8,128)(2,1)S(1)}, bf16[128,512]{1,0:T(8,128)(2,1)S(1)}, u32[]{:S(2)}, u32[]{:S(2)}) collective-permute-start(bf16[128,512]{1,0:T(8,128)(2,1)S(1)} %add_convert_fusion.refs_0_), channel_id=1, source_target_pairs={{0,8},{2,10},{4,12},{6,14},{8,0},{10,2},{12,4},{14,6},{1,9},{3,11}... | collective-permute-start | bytes 393224 | tf_op jit(solution)/shard_map/ppermute | solution.py:323
  14.7 2.2 %collective-permute-start.3 = (bf16[128,512]{1,0:T(8,128)(2,1)S(1)}, bf16[128,512]{1,0:T(8,128)(2,1)S(1)}, u32[]{:S(2)}, u32[]{:S(2)}) collective-permute-start(bf16[128,512]{1,0:T(8,128)(2,1)S(1)} %add_convert_fusion.refs_0_), channel_id=1, source_target_pairs={{0,6},{2,4},{4,2},{6,0},{8,14},{10,12},{12,10},{14,8},{1,7},{3,5},... | collective-permute-start | bytes 393224 | tf_op jit(solution)/shard_map/ppermute | solution.py:323
  16.9 1.0 %collective-permute-start.2 = (bf16[128,512]{1,0:T(8,128)(2,1)S(1)}, bf16[128,512]{1,0:T(8,128)(2,1)S(1)}, u32[]{:S(2)}, u32[]{:S(2)}) collective-permute-start(bf16[128,512]{1,0:T(8,128)(2,1)S(1)} %add_convert_fusion.refs_0_), channel_id=1, source_target_pairs={{0,4},{2,6},{4,0},{6,2},{8,12},{10,14},{12,8},{14,10},{1,5},{3,7},... | collective-permute-start | bytes 393224 | tf_op jit(solution)/shard_map/ppermute | solution.py:323
  17.9 0.3 collective-permute-start.1
  18.2 2.3 %collective-permute-done.4.refs_4_ = bf16[128,512]{1,0:T(8,128)(2,1)S(1)} collective-permute-done((bf16[128,512]{1,0:T(8,128)(2,1)S(1)}, bf16[128,512]{1,0:T(8,128)(2,1)S(1)}, u32[]{:S(2)}, u32[]{:S(2)}) %collective-permute-start.4) | collective-permute-done | bytes 131104 | tf_op jit(solution)/shard_map/ppermute | solution.py:323
  20.5 1.7 %collective-permute-start.7 = (bf16[128,512]{1,0:T(8,128)(2,1)S(1)}, bf16[128,512]{1,0:T(8,128)(2,1)S(1)}, u32[]{:S(2)}, u32[]{:S(2)}) collective-permute-start(bf16[128,512]{1,0:T(8,128)(2,1)S(1)} %collective-permute-done.4.refs_4_), channel_id=1, source_target_pairs={{0,6},{2,4},{4,2},{6,0},{8,14},{10,12},{12,10},{14,8},{1,7},{3,5},... | collective-permute-start | bytes 393224 | tf_op jit(solution)/shard_map/ppermute | solution.py:323
  22.2 0.9 %collective-permute-start.6 = (bf16[128,512]{1,0:T(8,128)(2,1)S(1)}, bf16[128,512]{1,0:T(8,128)(2,1)S(1)}, u32[]{:S(2)}, u32[]{:S(2)}) collective-permute-start(bf16[128,512]{1,0:T(8,128)(2,1)S(1)} %collective-permute-done.4.refs_4_), channel_id=1, source_target_pairs={{0,4},{2,6},{4,0},{6,2},{8,12},{10,14},{12,8},{14,10},{1,5},{3,7},... | collective-permute-start | bytes 393224 | tf_op jit(solution)/shard_map/ppermute | solution.py:323
  23.1 1.2 %collective-permute-start.5 = (bf16[128,512]{1,0:T(8,128)(2,1)S(1)}, bf16[128,512]{1,0:T(8,128)(2,1)S(1)}, u32[]{:S(2)}, u32[]{:S(2)}) collective-permute-start(bf16[128,512]{1,0:T(8,128)(2,1)S(1)} %collective-permute-done.4.refs_4_), channel_id=1, source_target_pairs={{0,2},{2,0},{4,6},{6,4},{8,10},{10,8},{12,14},{14,12},{1,3},{3,1},... | collective-permute-start | bytes 393224 | tf_op jit(solution)/shard_map/ppermute | solution.py:323
  24.3 1.3 %collective-permute-done.2.refs_2_ = bf16[128,512]{1,0:T(8,128)(2,1)S(1)} collective-permute-done((bf16[128,512]{1,0:T(8,128)(2,1)S(1)}, bf16[128,512]{1,0:T(8,128)(2,1)S(1)}, u32[]{:S(2)}, u32[]{:S(2)}) %collective-permute-start.2) | collective-permute-done | bytes 131104 | tf_op jit(solution)/shard_map/ppermute | solution.py:323
  25.7 0.5 %collective-permute-start.12 = (bf16[128,512]{1,0:T(8,128)(2,1)S(1)}, bf16[128,512]{1,0:T(8,128)(2,1)S(1)}, u32[]{:S(2)}, u32[]{:S(2)}) collective-permute-start(bf16[128,512]{1,0:T(8,128)(2,1)S(1)} %collective-permute-done.4.refs_4_), channel_id=1, source_target_pairs={{0,1},{1,0},{2,3},{3,2},{4,5},{5,4},{6,7},{7,6},{8,9},{9,8},{10,11... | collective-permute-start | bytes 393224 | tf_op jit(solution)/shard_map/ppermute | solution.py:334
  26.2 2.4 %collective-permute-done.7.refs_7_ = bf16[128,512]{1,0:T(8,128)(2,1)S(1)} collective-permute-done((bf16[128,512]{1,0:T(8,128)(2,1)S(1)}, bf16[128,512]{1,0:T(8,128)(2,1)S(1)}, u32[]{:S(2)}, u32[]{:S(2)}) %collective-permute-start.7) | collective-permute-done | bytes 131104 | tf_op jit(solution)/shard_map/ppermute | solution.py:323
  28.6 1.5 %collective-permute-done.6.refs_6_ = bf16[128,512]{1,0:T(8,128)(2,1)S(1)} collective-permute-done((bf16[128,512]{1,0:T(8,128)(2,1)S(1)}, bf16[128,512]{1,0:T(8,128)(2,1)S(1)}, u32[]{:S(2)}, u32[]{:S(2)}) %collective-permute-start.6) | collective-permute-done | bytes 131104 | tf_op jit(solution)/shard_map/ppermute | solution.py:323
  30.1 0.5 %collective-permute-start.10 = (bf16[128,512]{1,0:T(8,128)(2,1)S(1)}, bf16[128,512]{1,0:T(8,128)(2,1)S(1)}, u32[]{:S(2)}, u32[]{:S(2)}) collective-permute-start(bf16[128,512]{1,0:T(8,128)(2,1)S(1)} %collective-permute-done.2.refs_2_), channel_id=1, source_target_pairs={{0,1},{1,0},{2,3},{3,2},{4,5},{5,4},{6,7},{7,6},{8,9},{9,8},{10,11... | collective-permute-start | bytes 393224 | tf_op jit(solution)/shard_map/ppermute | solution.py:334
  30.6 0.5 %collective-permute-start.13 = (bf16[128,512]{1,0:T(8,128)(2,1)S(1)}, bf16[128,512]{1,0:T(8,128)(2,1)S(1)}, u32[]{:S(2)}, u32[]{:S(2)}) collective-permute-start(bf16[128,512]{1,0:T(8,128)(2,1)S(1)} %collective-permute-done.5.refs_5_), channel_id=1, source_target_pairs={{0,1},{1,0},{2,3},{3,2},{4,5},{5,4},{6,7},{7,6},{8,9},{9,8},{10,11... | collective-permute-start | bytes 393224 | tf_op jit(solution)/shard_map/ppermute | solution.py:334
  31.1 0.1 collective-permute-start.14
  31.2 0.2 collective-permute-done.9.refs_9_
  31.4 0.2 collective-permute-done.10.refs_10_
  31.6 0.3 collective-permute-done.11.refs_11_
  32.0 0.2 collective-permute-done.13.refs_13_
  32.1 0.3 collective-permute-done.14.refs_14_
  32.5 5.9 %shard_map.74 = f32[128,256]{1,0:T(8,128)} custom-call(bf16[2,128,216]{2,1,0:T(8,128)(2,1)S(1)} %get-tuple-element.13.mix, bf16[128,512]{1,0:T(8,128)(2,1)S(1)} %add_convert_fusion.refs_0_, bf16[128,512]{1,0:T(8,128)(2,1)S(1)} %collective-permute-done.1.refs_1_, bf16[128,512]{1,0:T(8,128)(2,1)S(1)} %collective-permute-done.2.refs_2_, ...), custom_call_target="tpu_custom_call" | custom-call | tf_op jit(solution)/shard_map/pallas_call | solution.py:367
  (11 shorter events, 0.1 us)
Async XLA Ops:
  4.9 7.1 %collective-permute-start = (bf16[128,512]{1,0:T(8,128)(2,1)S(1)}, bf16[128,512]{1,0:T(8,128)(2,1)S(1)}, u32[]{:S(2)}, u32[]{:S(2)}) collective-permute-start(bf16[128,512]{1,0:T(8,128)(2,1)S(1)} %bitcast.8), channel_id=1, source_target_pairs={{0,2},{2,0},{4,6},{6,4},{8,10},{10,8},{12,14},{14,12},{1,3},{3,1},... | collective-permute-start | bytes 393224 | tf_op jit(solution)/shard_map/ppermute | solution.py:323
  12.0 8.5 %collective-permute-start.4 = (bf16[128,512]{1,0:T(8,128)(2,1)S(1)}, bf16[128,512]{1,0:T(8,128)(2,1)S(1)}, u32[]{:S(2)}, u32[]{:S(2)}) collective-permute-start(bf16[128,512]{1,0:T(8,128)(2,1)S(1)} %add_convert_fusion.refs_0_), channel_id=1, source_target_pairs={{0,8},{2,10},{4,12},{6,14},{8,0},{10,2},{12,4},{14,6},{1,9},{3,11}... | collective-permute-start | bytes 393224 | tf_op jit(solution)/shard_map/ppermute | solution.py:323
  14.7 8.4 %collective-permute-start.3 = (bf16[128,512]{1,0:T(8,128)(2,1)S(1)}, bf16[128,512]{1,0:T(8,128)(2,1)S(1)}, u32[]{:S(2)}, u32[]{:S(2)}) collective-permute-start(bf16[128,512]{1,0:T(8,128)(2,1)S(1)} %add_convert_fusion.refs_0_), channel_id=1, source_target_pairs={{0,6},{2,4},{4,2},{6,0},{8,14},{10,12},{12,10},{14,8},{1,7},{3,5},... | collective-permute-start | bytes 393224 | tf_op jit(solution)/shard_map/ppermute | solution.py:323
  16.9 8.8 %collective-permute-start.2 = (bf16[128,512]{1,0:T(8,128)(2,1)S(1)}, bf16[128,512]{1,0:T(8,128)(2,1)S(1)}, u32[]{:S(2)}, u32[]{:S(2)}) collective-permute-start(bf16[128,512]{1,0:T(8,128)(2,1)S(1)} %add_convert_fusion.refs_0_), channel_id=1, source_target_pairs={{0,4},{2,6},{4,0},{6,2},{8,12},{10,14},{12,8},{14,10},{1,5},{3,7},... | collective-permute-start | bytes 393224 | tf_op jit(solution)/shard_map/ppermute | solution.py:323
  17.9 7.8 %collective-permute-start.1 = (bf16[128,512]{1,0:T(8,128)(2,1)S(1)}, bf16[128,512]{1,0:T(8,128)(2,1)S(1)}, u32[]{:S(2)}, u32[]{:S(2)}) collective-permute-start(bf16[128,512]{1,0:T(8,128)(2,1)S(1)} %add_convert_fusion.refs_0_), channel_id=1, source_target_pairs={{0,2},{2,0},{4,6},{6,4},{8,10},{10,8},{12,14},{14,12},{1,3},{3,1},... | collective-permute-start | bytes 393224 | tf_op jit(solution)/shard_map/ppermute | solution.py:323
  20.5 8.1 %collective-permute-start.7 = (bf16[128,512]{1,0:T(8,128)(2,1)S(1)}, bf16[128,512]{1,0:T(8,128)(2,1)S(1)}, u32[]{:S(2)}, u32[]{:S(2)}) collective-permute-start(bf16[128,512]{1,0:T(8,128)(2,1)S(1)} %collective-permute-done.4.refs_4_), channel_id=1, source_target_pairs={{0,6},{2,4},{4,2},{6,0},{8,14},{10,12},{12,10},{14,8},{1,7},{3,5},... | collective-permute-start | bytes 393224 | tf_op jit(solution)/shard_map/ppermute | solution.py:323
  22.2 7.9 %collective-permute-start.6 = (bf16[128,512]{1,0:T(8,128)(2,1)S(1)}, bf16[128,512]{1,0:T(8,128)(2,1)S(1)}, u32[]{:S(2)}, u32[]{:S(2)}) collective-permute-start(bf16[128,512]{1,0:T(8,128)(2,1)S(1)} %collective-permute-done.4.refs_4_), channel_id=1, source_target_pairs={{0,4},{2,6},{4,0},{6,2},{8,12},{10,14},{12,8},{14,10},{1,5},{3,7},... | collective-permute-start | bytes 393224 | tf_op jit(solution)/shard_map/ppermute | solution.py:323
  23.1 7.0 %collective-permute-start.5 = (bf16[128,512]{1,0:T(8,128)(2,1)S(1)}, bf16[128,512]{1,0:T(8,128)(2,1)S(1)}, u32[]{:S(2)}, u32[]{:S(2)}) collective-permute-start(bf16[128,512]{1,0:T(8,128)(2,1)S(1)} %collective-permute-done.4.refs_4_), channel_id=1, source_target_pairs={{0,2},{2,0},{4,6},{6,4},{8,10},{10,8},{12,14},{14,12},{1,3},{3,1},... | collective-permute-start | bytes 393224 | tf_op jit(solution)/shard_map/ppermute | solution.py:323
  25.7 4.9 %collective-permute-start.8 = (bf16[128,512]{1,0:T(8,128)(2,1)S(1)}, bf16[128,512]{1,0:T(8,128)(2,1)S(1)}, u32[]{:S(2)}, u32[]{:S(2)}) collective-permute-start(bf16[128,512]{1,0:T(8,128)(2,1)S(1)} %add_convert_fusion.refs_0_), channel_id=1, source_target_pairs={{0,1},{1,0},{2,3},{3,2},{4,5},{5,4},{6,7},{7,6},{8,9},{9,8},{10,11... | collective-permute-start | bytes 393224 | tf_op jit(solution)/shard_map/ppermute | solution.py:334
  25.7 4.9 %collective-permute-start.12 = (bf16[128,512]{1,0:T(8,128)(2,1)S(1)}, bf16[128,512]{1,0:T(8,128)(2,1)S(1)}, u32[]{:S(2)}, u32[]{:S(2)}) collective-permute-start(bf16[128,512]{1,0:T(8,128)(2,1)S(1)} %collective-permute-done.4.refs_4_), channel_id=1, source_target_pairs={{0,1},{1,0},{2,3},{3,2},{4,5},{5,4},{6,7},{7,6},{8,9},{9,8},{10,11... | collective-permute-start | bytes 393224 | tf_op jit(solution)/shard_map/ppermute | solution.py:334
  28.6 2.5 %collective-permute-start.15 = (bf16[128,512]{1,0:T(8,128)(2,1)S(1)}, bf16[128,512]{1,0:T(8,128)(2,1)S(1)}, u32[]{:S(2)}, u32[]{:S(2)}) collective-permute-start(bf16[128,512]{1,0:T(8,128)(2,1)S(1)} %collective-permute-done.7.refs_7_), channel_id=1, source_target_pairs={{0,1},{1,0},{2,3},{3,2},{4,5},{5,4},{6,7},{7,6},{8,9},{9,8},{10,11... | collective-permute-start | bytes 393224 | tf_op jit(solution)/shard_map/ppermute | solution.py:334
  30.1 1.3 %collective-permute-start.9 = (bf16[128,512]{1,0:T(8,128)(2,1)S(1)}, bf16[128,512]{1,0:T(8,128)(2,1)S(1)}, u32[]{:S(2)}, u32[]{:S(2)}) collective-permute-start(bf16[128,512]{1,0:T(8,128)(2,1)S(1)} %collective-permute-done.1.refs_1_), channel_id=1, source_target_pairs={{0,1},{1,0},{2,3},{3,2},{4,5},{5,4},{6,7},{7,6},{8,9},{9,8},{10,11... | collective-permute-start | bytes 393224 | tf_op jit(solution)/shard_map/ppermute | solution.py:334
  30.1 1.5 %collective-permute-start.10 = (bf16[128,512]{1,0:T(8,128)(2,1)S(1)}, bf16[128,512]{1,0:T(8,128)(2,1)S(1)}, u32[]{:S(2)}, u32[]{:S(2)}) collective-permute-start(bf16[128,512]{1,0:T(8,128)(2,1)S(1)} %collective-permute-done.2.refs_2_), channel_id=1, source_target_pairs={{0,1},{1,0},{2,3},{3,2},{4,5},{5,4},{6,7},{7,6},{8,9},{9,8},{10,11... | collective-permute-start | bytes 393224 | tf_op jit(solution)/shard_map/ppermute | solution.py:334
  30.6 1.3 %collective-permute-start.11 = (bf16[128,512]{1,0:T(8,128)(2,1)S(1)}, bf16[128,512]{1,0:T(8,128)(2,1)S(1)}, u32[]{:S(2)}, u32[]{:S(2)}) collective-permute-start(bf16[128,512]{1,0:T(8,128)(2,1)S(1)} %collective-permute-done.3.refs_3_), channel_id=1, source_target_pairs={{0,1},{1,0},{2,3},{3,2},{4,5},{5,4},{6,7},{7,6},{8,9},{9,8},{10,11... | collective-permute-start | bytes 393224 | tf_op jit(solution)/shard_map/ppermute | solution.py:334
  30.6 1.5 %collective-permute-start.13 = (bf16[128,512]{1,0:T(8,128)(2,1)S(1)}, bf16[128,512]{1,0:T(8,128)(2,1)S(1)}, u32[]{:S(2)}, u32[]{:S(2)}) collective-permute-start(bf16[128,512]{1,0:T(8,128)(2,1)S(1)} %collective-permute-done.5.refs_5_), channel_id=1, source_target_pairs={{0,1},{1,0},{2,3},{3,2},{4,5},{5,4},{6,7},{7,6},{8,9},{9,8},{10,11... | collective-permute-start | bytes 393224 | tf_op jit(solution)/shard_map/ppermute | solution.py:334
  31.1 1.3 %collective-permute-start.14 = (bf16[128,512]{1,0:T(8,128)(2,1)S(1)}, bf16[128,512]{1,0:T(8,128)(2,1)S(1)}, u32[]{:S(2)}, u32[]{:S(2)}) collective-permute-start(bf16[128,512]{1,0:T(8,128)(2,1)S(1)} %collective-permute-done.6.refs_6_), channel_id=1, source_target_pairs={{0,1},{1,0},{2,3},{3,2},{4,5},{5,4},{6,7},{7,6},{8,9},{9,8},{10,11... | collective-permute-start | bytes 393224 | tf_op jit(solution)/shard_map/ppermute | solution.py:334

commit v5 on v4

--- a/solution.py
+++ b/solution.py
@@ -66,7 +66,7 @@
     depth = voxels // lat
     width = depth // chans
     mix_out[0], mix_out[1] = correlation(psf, chans, lat, width, vox_total)
-    live = count[0]
+    live = count[0, 0]
     dense[...] = jnp.zeros_like(dense)
     lanes = lax.broadcasted_iota(jnp.int32, (tile, tile), 1)
 
@@ -107,12 +107,21 @@
             if step == 0:
                 own_out[a * width : (a + 1) * width, :] = rows
             else:
-                send_out[step - 1, a * width : (a + 1) * width, :] = rows.astype(BF16)
+                send_out[step - 1, a * width : (a + 1) * width, :] = rows
 
 
 def gram_parts(a, b):
+    hf = a.shape[1] // 2
     con = ((0,), (0,))
-    return [dot(a, a, con), dot(a, b, con), dot(b, b, con)]
+    a_real, a_imag, b_real, b_imag = a[:, :hf], a[:, hf:], b[:, :hf], b[:, hf:]
+    a_all = jnp.concatenate([a_real, a_imag], axis=0)
+    b_all = jnp.concatenate([b_real, b_imag], axis=0)
+    aa, bb = dot(a_real, a_imag, con), dot(b_real, b_imag, con)
+    return [
+        (dot(a_all, a_all, con), aa - aa.T),
+        (dot(a_all, b_all, con), dot(a_real, b_imag, con) - dot(a_imag, b_real, con)),
+        (dot(b_all, b_all, con), bb - bb.T),
+    ]
 
 
 def gram_kernel(*refs):
@@ -120,8 +129,8 @@
     count = (len(refs) - 1) // 2
     a = jnp.concatenate([r[...] for r in refs[:count]], axis=0)
     b = jnp.concatenate([r[...] for r in refs[count : 2 * count]], axis=0)
-    for i, t in enumerate(gram_parts(a, b)):
-        out[i] = t
+    for i, (real, imag) in enumerate(gram_parts(a, b)):
+        out[i, 0], out[i, 1] = real, imag
 
 
 def neighbours(chan, chans, width):
@@ -185,18 +194,16 @@
         b = jnp.concatenate([r[...] for r in other[:fresh]], axis=0)
         parts = gram_parts(a, b)
     else:
-        parts = [gram[i] for i in range(3)]
+        parts = [(gram[i, 0], gram[i, 1]) for i in range(3)]
 
     def diag_sum(t):
         r = lax.broadcasted_iota(jnp.int32, (DIAG, DIAG), 0)
         c = lax.broadcasted_iota(jnp.int32, (DIAG, DIAG), 1)
-        tiles = [t[i : i + DIAG, i : i + DIAG] for i in range(0, half, DIAG)]
+        tiles = [t[i : i + DIAG, i : i + DIAG] for i in range(0, hf, DIAG)]
         return jnp.sum(jnp.where(r == c, functools.reduce(jnp.add, tiles), 0.0))
 
-    factor = frames / (diag_sum(parts[0]) + diag_sum(parts[2]))
-    for i, t in enumerate(parts):
-        real = t[:hf, :hf] + t[hf:, hf:]
-        imag = t[:hf, hf:] - t[hf:, :hf]
+    factor = frames / (diag_sum(parts[0][0]) + diag_sum(parts[2][0]))
+    for i, (real, imag) in enumerate(parts):
         real_high, real_low = split(real)
         imag_high, imag_low = split(imag)
         for ref, re, im in ((mat_high, real_high, imag_high), (mat_low, real_low, imag_low)):
@@ -290,7 +297,7 @@
         functools.partial(das_kernel, chans=chans, lat=lat, vox_total=vox_total),
         out_shape=(
             pltpu.VMEM((n, 2 * hf), F32),
-            pltpu.VMEM((chans - 1, n, 2 * hf), BF16),
+            pltpu.VMEM((chans - 1, n, 2 * hf), F32),
             pltpu.VMEM((2, n, seen), BF16),
         ),
         in_specs=[smem, smem, smem, hbm, hbm, vmem, smem],
@@ -304,7 +311,7 @@
         ],
         compiler_params=pltpu.CompilerParams(vmem_limit_bytes=56 * 2**20),
     )(
-        tile_count.reshape(-1),
+        tile_count,
         tile_target.reshape(-1),
         tile_offset.reshape(-1),
         echo,
@@ -323,7 +330,7 @@
         return lax.ppermute(x, ("vox", "chan"), pairs)
 
     for step in range(1, chans):
-        own = own + peer(sent[step - 1], 0, step).astype(F32)
+        own = own + peer(sent[step - 1].astype(jnp.float16), 0, step).astype(F32)
     own = own.astype(BF16)
     crossed = peer(own, inner // 2, 0)
     near = [(dv, dc) for dv in range(inner // 2) for dc in range(chans)]
@@ -345,7 +352,7 @@
         )
         return pl.pallas_call(
             gram_kernel,
-            out_shape=jax.ShapeDtypeStruct((3, 2 * hf, 2 * hf), F32),
+            out_shape=jax.ShapeDtypeStruct((3, 2, hf, hf), F32),
             in_specs=[vmem] * (2 * len(a)),
             out_specs=vmem,
             cost_estimate=cost,

time: 38.6 us -> 38 us (0.984); the launches traced: 38.3 us -> 38.1 us
  no operation moved by 1% of the time
where the time goes in v5:
time: 38 us; the launch traced here: 38.1 us
  starting transfers between devices  15.2 us (40%)
  waiting for transfers between devices  12.4 us (33%)
  Pallas kernels  9.86 us (26%)
  between operations  0.69 us (2%)
    ppermute x8, starting transfers between devices, peer(): return lax.ppermute(x, ('vox', 'chan'), pairs)  13.6 us
    ppermute x8, waiting for transfers between devices, peer(): return lax.ppermute(x, ('vox', 'chan'), pairs)  11.1 us
    pallas_call x1, Pallas kernels, shards(): pl.pallas_call(functools.partial(filter_kernel, fresh=fresh, inner=inner,...  5.62 us
    pallas_call x1, Pallas kernels, shards(): pl.pallas_call(functools.partial(das_kernel, chans=chans, lat=lat, vox_to...  4.24 us
    ppermute x8, starting transfers between devices, to_other(): return lax.ppermute(x, 'frm', [(f, f ^ 1) for f in range(frms)])  1.6 us
    ppermute x8, waiting for transfers between devices, to_other(): return lax.ppermute(x, 'frm', [(f, f ^ 1) for f in range(frms)])  1.28 us
  transfers between devices with their start and end apart: 16, of which 10 were waited for; matrix products, arithmetic and copies ran while one was open for 0% of the time, Pallas kernels for 0%

profile of v5, /device:TPU:0, one launch (start us, length us, event | category | flops | bytes accessed | tf_op | source)
XLA Modules:
  0.0 38.1 jit_solution(7024806377184598805)
XLA Ops:
  0.7 4.2 %shard_map.73 = (f32[128,512]{1,0:T(8,128)S(1)}, f32[1,128,512]{2,1,0:T(8,128)S(1)}, bf16[2,128,216]{2,1,0:T(8,128)(2,1)S(1)}) custom-call(s32[1,1]{1,0:T(1,128)S(6)} %copy.8.count, s32[64]{0:T(128)} %bitcast.9, s32[64]{0:T(128)} %bitcast.10, bf16[1024,2,256]{2,1,0:T(2,128)(2,1)} %bitcast.8, bf16[64,128,128]{2,1,0:T(8,128)(2,1)} %bitcast.7, ...), custom_call_target="tpu_custom_call" | custom-call | tf_op jit(solution)/shard_map/pallas_call | solution.py:296
  4.9 3.6 %collective-permute-start = (f16[128,512]{1,0:T(8,128)(2,1)S(1)}, f16[128,512]{1,0:T(8,128)(2,1)S(1)}, u32[]{:S(2)}, u32[]{:S(2)}) collective-permute-start(f16[128,512]{1,0:T(8,128)(2,1)S(1)} %convert_bitcast_fusion), channel_id=1, source_target_pairs={{0,2},{2,0},{4,6},{6,4},{8,10},{10,8},{12,14},{14,12},{1,3},{3,1},... | collective-permute-start | bytes 393224 | tf_op jit(solution)/shard_map/ppermute | solution.py:330
  8.5 3.5 %collective-permute-done = f16[128,512]{1,0:T(8,128)(2,1)S(1)} collective-permute-done((f16[128,512]{1,0:T(8,128)(2,1)S(1)}, f16[128,512]{1,0:T(8,128)(2,1)S(1)}, u32[]{:S(2)}, u32[]{:S(2)}) %collective-permute-start) | collective-permute-done | bytes 131104 | tf_op jit(solution)/shard_map/ppermute | solution.py:330
  12.1 2.7 %collective-permute-start.4 = (bf16[128,512]{1,0:T(8,128)(2,1)S(1)}, bf16[128,512]{1,0:T(8,128)(2,1)S(1)}, u32[]{:S(2)}, u32[]{:S(2)}) collective-permute-start(bf16[128,512]{1,0:T(8,128)(2,1)S(1)} %add_convert_fusion.refs_0_), channel_id=1, source_target_pairs={{0,8},{2,10},{4,12},{6,14},{8,0},{10,2},{12,4},{14,6},{1,9},{3,11}... | collective-permute-start | bytes 393224 | tf_op jit(solution)/shard_map/ppermute | solution.py:330
  14.7 2.8 %collective-permute-start.3 = (bf16[128,512]{1,0:T(8,128)(2,1)S(1)}, bf16[128,512]{1,0:T(8,128)(2,1)S(1)}, u32[]{:S(2)}, u32[]{:S(2)}) collective-permute-start(bf16[128,512]{1,0:T(8,128)(2,1)S(1)} %add_convert_fusion.refs_0_), channel_id=1, source_target_pairs={{0,6},{2,4},{4,2},{6,0},{8,14},{10,12},{12,10},{14,8},{1,7},{3,5},... | collective-permute-start | bytes 393224 | tf_op jit(solution)/shard_map/ppermute | solution.py:330
  17.5 0.4 %collective-permute-start.2 = (bf16[128,512]{1,0:T(8,128)(2,1)S(1)}, bf16[128,512]{1,0:T(8,128)(2,1)S(1)}, u32[]{:S(2)}, u32[]{:S(2)}) collective-permute-start(bf16[128,512]{1,0:T(8,128)(2,1)S(1)} %add_convert_fusion.refs_0_), channel_id=1, source_target_pairs={{0,4},{2,6},{4,0},{6,2},{8,12},{10,14},{12,8},{14,10},{1,5},{3,7},... | collective-permute-start | bytes 393224 | tf_op jit(solution)/shard_map/ppermute | solution.py:330
  17.9 0.3 collective-permute-start.1
  18.2 2.3 %collective-permute-done.4.refs_4_ = bf16[128,512]{1,0:T(8,128)(2,1)S(1)} collective-permute-done((bf16[128,512]{1,0:T(8,128)(2,1)S(1)}, bf16[128,512]{1,0:T(8,128)(2,1)S(1)}, u32[]{:S(2)}, u32[]{:S(2)}) %collective-permute-start.4) | collective-permute-done | bytes 131104 | tf_op jit(solution)/shard_map/ppermute | solution.py:330
  20.5 1.7 %collective-permute-start.7 = (bf16[128,512]{1,0:T(8,128)(2,1)S(1)}, bf16[128,512]{1,0:T(8,128)(2,1)S(1)}, u32[]{:S(2)}, u32[]{:S(2)}) collective-permute-start(bf16[128,512]{1,0:T(8,128)(2,1)S(1)} %collective-permute-done.4.refs_4_), channel_id=1, source_target_pairs={{0,6},{2,4},{4,2},{6,0},{8,14},{10,12},{12,10},{14,8},{1,7},{3,5},... | collective-permute-start | bytes 393224 | tf_op jit(solution)/shard_map/ppermute | solution.py:330
  22.2 0.9 %collective-permute-start.6 = (bf16[128,512]{1,0:T(8,128)(2,1)S(1)}, bf16[128,512]{1,0:T(8,128)(2,1)S(1)}, u32[]{:S(2)}, u32[]{:S(2)}) collective-permute-start(bf16[128,512]{1,0:T(8,128)(2,1)S(1)} %collective-permute-done.4.refs_4_), channel_id=1, source_target_pairs={{0,4},{2,6},{4,0},{6,2},{8,12},{10,14},{12,8},{14,10},{1,5},{3,7},... | collective-permute-start | bytes 393224 | tf_op jit(solution)/shard_map/ppermute | solution.py:330
  23.1 1.2 %collective-permute-start.5 = (bf16[128,512]{1,0:T(8,128)(2,1)S(1)}, bf16[128,512]{1,0:T(8,128)(2,1)S(1)}, u32[]{:S(2)}, u32[]{:S(2)}) collective-permute-start(bf16[128,512]{1,0:T(8,128)(2,1)S(1)} %collective-permute-done.4.refs_4_), channel_id=1, source_target_pairs={{0,2},{2,0},{4,6},{6,4},{8,10},{10,8},{12,14},{14,12},{1,3},{3,1},... | collective-permute-start | bytes 393224 | tf_op jit(solution)/shard_map/ppermute | solution.py:330
  24.4 1.3 %collective-permute-done.2.refs_2_ = bf16[128,512]{1,0:T(8,128)(2,1)S(1)} collective-permute-done((bf16[128,512]{1,0:T(8,128)(2,1)S(1)}, bf16[128,512]{1,0:T(8,128)(2,1)S(1)}, u32[]{:S(2)}, u32[]{:S(2)}) %collective-permute-start.2) | collective-permute-done | bytes 131104 | tf_op jit(solution)/shard_map/ppermute | solution.py:330
  25.7 0.5 %collective-permute-start.12 = (bf16[128,512]{1,0:T(8,128)(2,1)S(1)}, bf16[128,512]{1,0:T(8,128)(2,1)S(1)}, u32[]{:S(2)}, u32[]{:S(2)}) collective-permute-start(bf16[128,512]{1,0:T(8,128)(2,1)S(1)} %collective-permute-done.4.refs_4_), channel_id=1, source_target_pairs={{0,1},{1,0},{2,3},{3,2},{4,5},{5,4},{6,7},{7,6},{8,9},{9,8},{10,11... | collective-permute-start | bytes 393224 | tf_op jit(solution)/shard_map/ppermute | solution.py:341
  26.2 2.4 %collective-permute-done.7.refs_7_ = bf16[128,512]{1,0:T(8,128)(2,1)S(1)} collective-permute-done((bf16[128,512]{1,0:T(8,128)(2,1)S(1)}, bf16[128,512]{1,0:T(8,128)(2,1)S(1)}, u32[]{:S(2)}, u32[]{:S(2)}) %collective-permute-start.7) | collective-permute-done | bytes 131104 | tf_op jit(solution)/shard_map/ppermute | solution.py:330
  28.6 1.5 %collective-permute-done.6.refs_6_ = bf16[128,512]{1,0:T(8,128)(2,1)S(1)} collective-permute-done((bf16[128,512]{1,0:T(8,128)(2,1)S(1)}, bf16[128,512]{1,0:T(8,128)(2,1)S(1)}, u32[]{:S(2)}, u32[]{:S(2)}) %collective-permute-start.6) | collective-permute-done | bytes 131104 | tf_op jit(solution)/shard_map/ppermute | solution.py:330
  30.1 0.5 %collective-permute-start.10 = (bf16[128,512]{1,0:T(8,128)(2,1)S(1)}, bf16[128,512]{1,0:T(8,128)(2,1)S(1)}, u32[]{:S(2)}, u32[]{:S(2)}) collective-permute-start(bf16[128,512]{1,0:T(8,128)(2,1)S(1)} %collective-permute-done.2.refs_2_), channel_id=1, source_target_pairs={{0,1},{1,0},{2,3},{3,2},{4,5},{5,4},{6,7},{7,6},{8,9},{9,8},{10,11... | collective-permute-start | bytes 393224 | tf_op jit(solution)/shard_map/ppermute | solution.py:341
  30.6 0.5 %collective-permute-start.13 = (bf16[128,512]{1,0:T(8,128)(2,1)S(1)}, bf16[128,512]{1,0:T(8,128)(2,1)S(1)}, u32[]{:S(2)}, u32[]{:S(2)}) collective-permute-start(bf16[128,512]{1,0:T(8,128)(2,1)S(1)} %collective-permute-done.5.refs_5_), channel_id=1, source_target_pairs={{0,1},{1,0},{2,3},{3,2},{4,5},{5,4},{6,7},{7,6},{8,9},{9,8},{10,11... | collective-permute-start | bytes 393224 | tf_op jit(solution)/shard_map/ppermute | solution.py:341
  31.2 0.1 collective-permute-start.14
  31.2 0.2 collective-permute-done.9.refs_9_
  31.5 0.2 collective-permute-done.10.refs_10_
  31.7 0.3 collective-permute-done.11.refs_11_
  32.0 0.2 collective-permute-done.13.refs_13_
  32.2 0.3 collective-permute-done.14.refs_14_
  32.5 5.6 %shard_map.74 = f32[128,256]{1,0:T(8,128)} custom-call(bf16[2,128,216]{2,1,0:T(8,128)(2,1)S(1)} %get-tuple-element.13.mix, bf16[128,512]{1,0:T(8,128)(2,1)S(1)} %add_convert_fusion.refs_0_, bf16[128,512]{1,0:T(8,128)(2,1)S(1)} %collective-permute-done.1.refs_1_, bf16[128,512]{1,0:T(8,128)(2,1)S(1)} %collective-permute-done.2.refs_2_, ...), custom_call_target="tpu_custom_call" | custom-call | tf_op jit(solution)/shard_map/pallas_call | solution.py:374
  (12 shorter events, 0.1 us)
Async XLA Ops:
  4.9 7.1 %collective-permute-start = (f16[128,512]{1,0:T(8,128)(2,1)S(1)}, f16[128,512]{1,0:T(8,128)(2,1)S(1)}, u32[]{:S(2)}, u32[]{:S(2)}) collective-permute-start(f16[128,512]{1,0:T(8,128)(2,1)S(1)} %convert_bitcast_fusion), channel_id=1, source_target_pairs={{0,2},{2,0},{4,6},{6,4},{8,10},{10,8},{12,14},{14,12},{1,3},{3,1},... | collective-permute-start | bytes 393224 | tf_op jit(solution)/shard_map/ppermute | solution.py:330
  12.1 8.5 %collective-permute-start.4 = (bf16[128,512]{1,0:T(8,128)(2,1)S(1)}, bf16[128,512]{1,0:T(8,128)(2,1)S(1)}, u32[]{:S(2)}, u32[]{:S(2)}) collective-permute-start(bf16[128,512]{1,0:T(8,128)(2,1)S(1)} %add_convert_fusion.refs_0_), channel_id=1, source_target_pairs={{0,8},{2,10},{4,12},{6,14},{8,0},{10,2},{12,4},{14,6},{1,9},{3,11}... | collective-permute-start | bytes 393224 | tf_op jit(solution)/shard_map/ppermute | solution.py:330
  14.7 8.4 %collective-permute-start.3 = (bf16[128,512]{1,0:T(8,128)(2,1)S(1)}, bf16[128,512]{1,0:T(8,128)(2,1)S(1)}, u32[]{:S(2)}, u32[]{:S(2)}) collective-permute-start(bf16[128,512]{1,0:T(8,128)(2,1)S(1)} %add_convert_fusion.refs_0_), channel_id=1, source_target_pairs={{0,6},{2,4},{4,2},{6,0},{8,14},{10,12},{12,10},{14,8},{1,7},{3,5},... | collective-permute-start | bytes 393224 | tf_op jit(solution)/shard_map/ppermute | solution.py:330
  17.5 8.2 %collective-permute-start.2 = (bf16[128,512]{1,0:T(8,128)(2,1)S(1)}, bf16[128,512]{1,0:T(8,128)(2,1)S(1)}, u32[]{:S(2)}, u32[]{:S(2)}) collective-permute-start(bf16[128,512]{1,0:T(8,128)(2,1)S(1)} %add_convert_fusion.refs_0_), channel_id=1, source_target_pairs={{0,4},{2,6},{4,0},{6,2},{8,12},{10,14},{12,8},{14,10},{1,5},{3,7},... | collective-permute-start | bytes 393224 | tf_op jit(solution)/shard_map/ppermute | solution.py:330
  17.9 7.8 %collective-permute-start.1 = (bf16[128,512]{1,0:T(8,128)(2,1)S(1)}, bf16[128,512]{1,0:T(8,128)(2,1)S(1)}, u32[]{:S(2)}, u32[]{:S(2)}) collective-permute-start(bf16[128,512]{1,0:T(8,128)(2,1)S(1)} %add_convert_fusion.refs_0_), channel_id=1, source_target_pairs={{0,2},{2,0},{4,6},{6,4},{8,10},{10,8},{12,14},{14,12},{1,3},{3,1},... | collective-permute-start | bytes 393224 | tf_op jit(solution)/shard_map/ppermute | solution.py:330
  20.5 8.1 %collective-permute-start.7 = (bf16[128,512]{1,0:T(8,128)(2,1)S(1)}, bf16[128,512]{1,0:T(8,128)(2,1)S(1)}, u32[]{:S(2)}, u32[]{:S(2)}) collective-permute-start(bf16[128,512]{1,0:T(8,128)(2,1)S(1)} %collective-permute-done.4.refs_4_), channel_id=1, source_target_pairs={{0,6},{2,4},{4,2},{6,0},{8,14},{10,12},{12,10},{14,8},{1,7},{3,5},... | collective-permute-start | bytes 393224 | tf_op jit(solution)/shard_map/ppermute | solution.py:330
  22.2 7.9 %collective-permute-start.6 = (bf16[128,512]{1,0:T(8,128)(2,1)S(1)}, bf16[128,512]{1,0:T(8,128)(2,1)S(1)}, u32[]{:S(2)}, u32[]{:S(2)}) collective-permute-start(bf16[128,512]{1,0:T(8,128)(2,1)S(1)} %collective-permute-done.4.refs_4_), channel_id=1, source_target_pairs={{0,4},{2,6},{4,0},{6,2},{8,12},{10,14},{12,8},{14,10},{1,5},{3,7},... | collective-permute-start | bytes 393224 | tf_op jit(solution)/shard_map/ppermute | solution.py:330
  23.1 7.0 %collective-permute-start.5 = (bf16[128,512]{1,0:T(8,128)(2,1)S(1)}, bf16[128,512]{1,0:T(8,128)(2,1)S(1)}, u32[]{:S(2)}, u32[]{:S(2)}) collective-permute-start(bf16[128,512]{1,0:T(8,128)(2,1)S(1)} %collective-permute-done.4.refs_4_), channel_id=1, source_target_pairs={{0,2},{2,0},{4,6},{6,4},{8,10},{10,8},{12,14},{14,12},{1,3},{3,1},... | collective-permute-start | bytes 393224 | tf_op jit(solution)/shard_map/ppermute | solution.py:330
  25.7 4.9 %collective-permute-start.8 = (bf16[128,512]{1,0:T(8,128)(2,1)S(1)}, bf16[128,512]{1,0:T(8,128)(2,1)S(1)}, u32[]{:S(2)}, u32[]{:S(2)}) collective-permute-start(bf16[128,512]{1,0:T(8,128)(2,1)S(1)} %add_convert_fusion.refs_0_), channel_id=1, source_target_pairs={{0,1},{1,0},{2,3},{3,2},{4,5},{5,4},{6,7},{7,6},{8,9},{9,8},{10,11... | collective-permute-start | bytes 393224 | tf_op jit(solution)/shard_map/ppermute | solution.py:341
  25.7 4.9 %collective-permute-start.12 = (bf16[128,512]{1,0:T(8,128)(2,1)S(1)}, bf16[128,512]{1,0:T(8,128)(2,1)S(1)}, u32[]{:S(2)}, u32[]{:S(2)}) collective-permute-start(bf16[128,512]{1,0:T(8,128)(2,1)S(1)} %collective-permute-done.4.refs_4_), channel_id=1, source_target_pairs={{0,1},{1,0},{2,3},{3,2},{4,5},{5,4},{6,7},{7,6},{8,9},{9,8},{10,11... | collective-permute-start | bytes 393224 | tf_op jit(solution)/shard_map/ppermute | solution.py:341
  28.6 2.5 %collective-permute-start.15 = (bf16[128,512]{1,0:T(8,128)(2,1)S(1)}, bf16[128,512]{1,0:T(8,128)(2,1)S(1)}, u32[]{:S(2)}, u32[]{:S(2)}) collective-permute-start(bf16[128,512]{1,0:T(8,128)(2,1)S(1)} %collective-permute-done.7.refs_7_), channel_id=1, source_target_pairs={{0,1},{1,0},{2,3},{3,2},{4,5},{5,4},{6,7},{7,6},{8,9},{9,8},{10,11... | collective-permute-start | bytes 393224 | tf_op jit(solution)/shard_map/ppermute | solution.py:341
  30.1 1.3 %collective-permute-start.9 = (bf16[128,512]{1,0:T(8,128)(2,1)S(1)}, bf16[128,512]{1,0:T(8,128)(2,1)S(1)}, u32[]{:S(2)}, u32[]{:S(2)}) collective-permute-start(bf16[128,512]{1,0:T(8,128)(2,1)S(1)} %collective-permute-done.1.refs_1_), channel_id=1, source_target_pairs={{0,1},{1,0},{2,3},{3,2},{4,5},{5,4},{6,7},{7,6},{8,9},{9,8},{10,11... | collective-permute-start | bytes 393224 | tf_op jit(solution)/shard_map/ppermute | solution.py:341
  30.1 1.5 %collective-permute-start.10 = (bf16[128,512]{1,0:T(8,128)(2,1)S(1)}, bf16[128,512]{1,0:T(8,128)(2,1)S(1)}, u32[]{:S(2)}, u32[]{:S(2)}) collective-permute-start(bf16[128,512]{1,0:T(8,128)(2,1)S(1)} %collective-permute-done.2.refs_2_), channel_id=1, source_target_pairs={{0,1},{1,0},{2,3},{3,2},{4,5},{5,4},{6,7},{7,6},{8,9},{9,8},{10,11... | collective-permute-start | bytes 393224 | tf_op jit(solution)/shard_map/ppermute | solution.py:341
  30.6 1.3 %collective-permute-start.11 = (bf16[128,512]{1,0:T(8,128)(2,1)S(1)}, bf16[128,512]{1,0:T(8,128)(2,1)S(1)}, u32[]{:S(2)}, u32[]{:S(2)}) collective-permute-start(bf16[128,512]{1,0:T(8,128)(2,1)S(1)} %collective-permute-done.3.refs_3_), channel_id=1, source_target_pairs={{0,1},{1,0},{2,3},{3,2},{4,5},{5,4},{6,7},{7,6},{8,9},{9,8},{10,11... | collective-permute-start | bytes 393224 | tf_op jit(solution)/shard_map/ppermute | solution.py:341
  30.6 1.5 %collective-permute-start.13 = (bf16[128,512]{1,0:T(8,128)(2,1)S(1)}, bf16[128,512]{1,0:T(8,128)(2,1)S(1)}, u32[]{:S(2)}, u32[]{:S(2)}) collective-permute-start(bf16[128,512]{1,0:T(8,128)(2,1)S(1)} %collective-permute-done.5.refs_5_), channel_id=1, source_target_pairs={{0,1},{1,0},{2,3},{3,2},{4,5},{5,4},{6,7},{7,6},{8,9},{9,8},{10,11... | collective-permute-start | bytes 393224 | tf_op jit(solution)/shard_map/ppermute | solution.py:341
  31.2 1.3 %collective-permute-start.14 = (bf16[128,512]{1,0:T(8,128)(2,1)S(1)}, bf16[128,512]{1,0:T(8,128)(2,1)S(1)}, u32[]{:S(2)}, u32[]{:S(2)}) collective-permute-start(bf16[128,512]{1,0:T(8,128)(2,1)S(1)} %collective-permute-done.6.refs_6_), channel_id=1, source_target_pairs={{0,1},{1,0},{2,3},{3,2},{4,5},{5,4},{6,7},{7,6},{8,9},{9,8},{10,11... | collective-permute-start | bytes 393224 | tf_op jit(solution)/shard_map/ppermute | solution.py:341

commit v6 on v5

--- a/solution.py
+++ b/solution.py
@@ -334,8 +334,13 @@
     own = own.astype(BF16)
     crossed = peer(own, inner // 2, 0)
     near = [(dv, dc) for dv in range(inner // 2) for dc in range(chans)]
-    mine = [own] + [peer(own, dv, dc) for dv, dc in near[1:]]
-    mine += [crossed] + [peer(crossed, dv, dc) for dv, dc in near[1:]]
+    first, second = {}, {}
+    for i in reversed(range(1, len(near))):
+        first[i] = peer(own, *near[i])
+    for i in reversed(range(1, len(near))):
+        second[i] = peer(crossed, *near[i])
+    rest = range(1, len(near))
+    mine = [own] + [first[i] for i in rest] + [crossed] + [second[i] for i in rest]
 
     def to_other(x):
         return lax.ppermute(x, "frm", [(f, f ^ 1) for f in range(frms)])

time: 38 us -> 38.2 us (level); the launches traced: 38.1 us -> 37.8 us
  waiting for transfers between devices: 12.4 us -> 12 us
  transfers between devices with their start and end apart: 16 -> 16, of which waited for: 10 -> 11; matrix products, arithmetic and copies ran while one was open for 0% -> 0% of each run, Pallas kernels for 0% -> 0%
where the time goes in v6:
time: 38.2 us; the launch traced here: 37.8 us
  starting transfers between devices  15.2 us (40%)
  waiting for transfers between devices  12 us (31%)
  Pallas kernels  9.85 us (26%)
  between operations  0.69 us (2%)
    ppermute x8, starting transfers between devices, peer(): return lax.ppermute(x, ('vox', 'chan'), pairs)  13.6 us
    ppermute x8, waiting for transfers between devices, peer(): return lax.ppermute(x, ('vox', 'chan'), pairs)  10.7 us
    pallas_call x1, Pallas kernels, shards(): pl.pallas_call(functools.partial(filter_kernel, fresh=fresh, inner=inner,...  5.61 us
    pallas_call x1, Pallas kernels, shards(): pl.pallas_call(functools.partial(das_kernel, chans=chans, lat=lat, vox_to...  4.24 us
    ppermute x8, starting transfers between devices, to_other(): return lax.ppermute(x, 'frm', [(f, f ^ 1) for f in range(frms)])  1.6 us
    ppermute x8, waiting for transfers between devices, to_other(): return lax.ppermute(x, 'frm', [(f, f ^ 1) for f in range(frms)])  1.28 us
  transfers between devices with their start and end apart: 16, of which 11 were waited for; matrix products, arithmetic and copies ran while one was open for 0% of the time, Pallas kernels for 0%

profile of v6, /device:TPU:0, one launch (start us, length us, event | category | flops | bytes accessed | tf_op | source)
XLA Modules:
  0.0 37.8 jit_solution(7024806377184598805)
XLA Ops:
  0.7 4.2 %shard_map.73 = (f32[128,512]{1,0:T(8,128)S(1)}, f32[1,128,512]{2,1,0:T(8,128)S(1)}, bf16[2,128,216]{2,1,0:T(8,128)(2,1)S(1)}) custom-call(s32[1,1]{1,0:T(1,128)S(6)} %copy.8.count, s32[64]{0:T(128)} %bitcast.9, s32[64]{0:T(128)} %bitcast.10, bf16[1024,2,256]{2,1,0:T(2,128)(2,1)} %bitcast.8, bf16[64,128,128]{2,1,0:T(8,128)(2,1)} %bitcast.7, ...), custom_call_target="tpu_custom_call" | custom-call | tf_op jit(solution)/shard_map/pallas_call | solution.py:296
  4.9 3.6 %collective-permute-start = (f16[128,512]{1,0:T(8,128)(2,1)S(1)}, f16[128,512]{1,0:T(8,128)(2,1)S(1)}, u32[]{:S(2)}, u32[]{:S(2)}) collective-permute-start(f16[128,512]{1,0:T(8,128)(2,1)S(1)} %convert_bitcast_fusion), channel_id=1, source_target_pairs={{0,2},{2,0},{4,6},{6,4},{8,10},{10,8},{12,14},{14,12},{1,3},{3,1},... | collective-permute-start | bytes 393224 | tf_op jit(solution)/shard_map/ppermute | solution.py:330
  8.5 3.5 %collective-permute-done = f16[128,512]{1,0:T(8,128)(2,1)S(1)} collective-permute-done((f16[128,512]{1,0:T(8,128)(2,1)S(1)}, f16[128,512]{1,0:T(8,128)(2,1)S(1)}, u32[]{:S(2)}, u32[]{:S(2)}) %collective-permute-start) | collective-permute-done | bytes 131104 | tf_op jit(solution)/shard_map/ppermute | solution.py:330
  12.1 2.9 %collective-permute-start.4 = (bf16[128,512]{1,0:T(8,128)(2,1)S(1)}, bf16[128,512]{1,0:T(8,128)(2,1)S(1)}, u32[]{:S(2)}, u32[]{:S(2)}) collective-permute-start(bf16[128,512]{1,0:T(8,128)(2,1)S(1)} %add_convert_fusion.refs_0_), channel_id=1, source_target_pairs={{0,8},{2,10},{4,12},{6,14},{8,0},{10,2},{12,4},{14,6},{1,9},{3,11}... | collective-permute-start | bytes 393224 | tf_op jit(solution)/shard_map/ppermute | solution.py:330
  14.9 2.0 %collective-permute-start.3 = (bf16[128,512]{1,0:T(8,128)(2,1)S(1)}, bf16[128,512]{1,0:T(8,128)(2,1)S(1)}, u32[]{:S(2)}, u32[]{:S(2)}) collective-permute-start(bf16[128,512]{1,0:T(8,128)(2,1)S(1)} %add_convert_fusion.refs_0_), channel_id=1, source_target_pairs={{0,6},{2,4},{4,2},{6,0},{8,14},{10,12},{12,10},{14,8},{1,7},{3,5},... | collective-permute-start | bytes 393224 | tf_op jit(solution)/shard_map/ppermute | solution.py:330
  16.9 0.5 %collective-permute-start.2 = (bf16[128,512]{1,0:T(8,128)(2,1)S(1)}, bf16[128,512]{1,0:T(8,128)(2,1)S(1)}, u32[]{:S(2)}, u32[]{:S(2)}) collective-permute-start(bf16[128,512]{1,0:T(8,128)(2,1)S(1)} %add_convert_fusion.refs_0_), channel_id=1, source_target_pairs={{0,4},{2,6},{4,0},{6,2},{8,12},{10,14},{12,8},{14,10},{1,5},{3,7},... | collective-permute-start | bytes 393224 | tf_op jit(solution)/shard_map/ppermute | solution.py:330
  17.3 1.1 %collective-permute-start.1 = (bf16[128,512]{1,0:T(8,128)(2,1)S(1)}, bf16[128,512]{1,0:T(8,128)(2,1)S(1)}, u32[]{:S(2)}, u32[]{:S(2)}) collective-permute-start(bf16[128,512]{1,0:T(8,128)(2,1)S(1)} %add_convert_fusion.refs_0_), channel_id=1, source_target_pairs={{0,2},{2,0},{4,6},{6,4},{8,10},{10,8},{12,14},{14,12},{1,3},{3,1},... | collective-permute-start | bytes 393224 | tf_op jit(solution)/shard_map/ppermute | solution.py:330
  18.4 1.9 %collective-permute-done.4.refs_4_ = bf16[128,512]{1,0:T(8,128)(2,1)S(1)} collective-permute-done((bf16[128,512]{1,0:T(8,128)(2,1)S(1)}, bf16[128,512]{1,0:T(8,128)(2,1)S(1)}, u32[]{:S(2)}, u32[]{:S(2)}) %collective-permute-start.4) | collective-permute-done | bytes 131104 | tf_op jit(solution)/shard_map/ppermute | solution.py:330
  20.3 1.3 %collective-permute-start.7 = (bf16[128,512]{1,0:T(8,128)(2,1)S(1)}, bf16[128,512]{1,0:T(8,128)(2,1)S(1)}, u32[]{:S(2)}, u32[]{:S(2)}) collective-permute-start(bf16[128,512]{1,0:T(8,128)(2,1)S(1)} %collective-permute-done.4.refs_4_), channel_id=1, source_target_pairs={{0,6},{2,4},{4,2},{6,0},{8,14},{10,12},{12,10},{14,8},{1,7},{3,5},... | collective-permute-start | bytes 393224 | tf_op jit(solution)/shard_map/ppermute | solution.py:330
  21.6 1.8 %collective-permute-start.6 = (bf16[128,512]{1,0:T(8,128)(2,1)S(1)}, bf16[128,512]{1,0:T(8,128)(2,1)S(1)}, u32[]{:S(2)}, u32[]{:S(2)}) collective-permute-start(bf16[128,512]{1,0:T(8,128)(2,1)S(1)} %collective-permute-done.4.refs_4_), channel_id=1, source_target_pairs={{0,4},{2,6},{4,0},{6,2},{8,12},{10,14},{12,8},{14,10},{1,5},{3,7},... | collective-permute-start | bytes 393224 | tf_op jit(solution)/shard_map/ppermute | solution.py:330
  23.4 0.5 %collective-permute-start.5 = (bf16[128,512]{1,0:T(8,128)(2,1)S(1)}, bf16[128,512]{1,0:T(8,128)(2,1)S(1)}, u32[]{:S(2)}, u32[]{:S(2)}) collective-permute-start(bf16[128,512]{1,0:T(8,128)(2,1)S(1)} %collective-permute-done.4.refs_4_), channel_id=1, source_target_pairs={{0,2},{2,0},{4,6},{6,4},{8,10},{10,8},{12,14},{14,12},{1,3},{3,1},... | collective-permute-start | bytes 393224 | tf_op jit(solution)/shard_map/ppermute | solution.py:330
  24.0 0.9 %collective-permute-done.2.refs_2_ = bf16[128,512]{1,0:T(8,128)(2,1)S(1)} collective-permute-done((bf16[128,512]{1,0:T(8,128)(2,1)S(1)}, bf16[128,512]{1,0:T(8,128)(2,1)S(1)}, u32[]{:S(2)}, u32[]{:S(2)}) %collective-permute-start.2) | collective-permute-done | bytes 131104 | tf_op jit(solution)/shard_map/ppermute | solution.py:330
  24.9 0.5 %collective-permute-start.12 = (bf16[128,512]{1,0:T(8,128)(2,1)S(1)}, bf16[128,512]{1,0:T(8,128)(2,1)S(1)}, u32[]{:S(2)}, u32[]{:S(2)}) collective-permute-start(bf16[128,512]{1,0:T(8,128)(2,1)S(1)} %collective-permute-done.4.refs_4_), channel_id=1, source_target_pairs={{0,1},{1,0},{2,3},{3,2},{4,5},{5,4},{6,7},{7,6},{8,9},{9,8},{10,11... | collective-permute-start | bytes 393224 | tf_op jit(solution)/shard_map/ppermute | solution.py:346
  25.4 3.6 %collective-permute-done.7.refs_7_ = bf16[128,512]{1,0:T(8,128)(2,1)S(1)} collective-permute-done((bf16[128,512]{1,0:T(8,128)(2,1)S(1)}, bf16[128,512]{1,0:T(8,128)(2,1)S(1)}, u32[]{:S(2)}, u32[]{:S(2)}) %collective-permute-start.7) | collective-permute-done | bytes 131104 | tf_op jit(solution)/shard_map/ppermute | solution.py:330
  29.0 0.6 %collective-permute-done.6.refs_6_ = bf16[128,512]{1,0:T(8,128)(2,1)S(1)} collective-permute-done((bf16[128,512]{1,0:T(8,128)(2,1)S(1)}, bf16[128,512]{1,0:T(8,128)(2,1)S(1)}, u32[]{:S(2)}, u32[]{:S(2)}) %collective-permute-start.6) | collective-permute-done | bytes 131104 | tf_op jit(solution)/shard_map/ppermute | solution.py:330
  29.6 0.1 collective-permute-done.5.refs_5_
  29.8 0.5 %collective-permute-start.10 = (bf16[128,512]{1,0:T(8,128)(2,1)S(1)}, bf16[128,512]{1,0:T(8,128)(2,1)S(1)}, u32[]{:S(2)}, u32[]{:S(2)}) collective-permute-start(bf16[128,512]{1,0:T(8,128)(2,1)S(1)} %collective-permute-done.2.refs_2_), channel_id=1, source_target_pairs={{0,1},{1,0},{2,3},{3,2},{4,5},{5,4},{6,7},{7,6},{8,9},{9,8},{10,11... | collective-permute-start | bytes 393224 | tf_op jit(solution)/shard_map/ppermute | solution.py:346
  30.3 0.5 %collective-permute-start.13 = (bf16[128,512]{1,0:T(8,128)(2,1)S(1)}, bf16[128,512]{1,0:T(8,128)(2,1)S(1)}, u32[]{:S(2)}, u32[]{:S(2)}) collective-permute-start(bf16[128,512]{1,0:T(8,128)(2,1)S(1)} %collective-permute-done.5.refs_5_), channel_id=1, source_target_pairs={{0,1},{1,0},{2,3},{3,2},{4,5},{5,4},{6,7},{7,6},{8,9},{9,8},{10,11... | collective-permute-start | bytes 393224 | tf_op jit(solution)/shard_map/ppermute | solution.py:346
  30.9 0.2 collective-permute-done.9.refs_9_
  31.1 0.2 collective-permute-done.10.refs_10_
  31.3 0.3 collective-permute-done.11.refs_11_
  31.6 0.2 collective-permute-done.13.refs_13_
  31.8 0.3 collective-permute-done.14.refs_14_
  32.2 5.6 %shard_map.74 = f32[128,256]{1,0:T(8,128)} custom-call(bf16[2,128,216]{2,1,0:T(8,128)(2,1)S(1)} %get-tuple-element.13.mix, bf16[128,512]{1,0:T(8,128)(2,1)S(1)} %add_convert_fusion.refs_0_, bf16[128,512]{1,0:T(8,128)(2,1)S(1)} %collective-permute-done.1.refs_1_, bf16[128,512]{1,0:T(8,128)(2,1)S(1)} %collective-permute-done.2.refs_2_, ...), custom_call_target="tpu_custom_call" | custom-call | tf_op jit(solution)/shard_map/pallas_call | solution.py:379
  (12 shorter events, 0.1 us)
Async XLA Ops:
  4.9 7.1 %collective-permute-start = (f16[128,512]{1,0:T(8,128)(2,1)S(1)}, f16[128,512]{1,0:T(8,128)(2,1)S(1)}, u32[]{:S(2)}, u32[]{:S(2)}) collective-permute-start(f16[128,512]{1,0:T(8,128)(2,1)S(1)} %convert_bitcast_fusion), channel_id=1, source_target_pairs={{0,2},{2,0},{4,6},{6,4},{8,10},{10,8},{12,14},{14,12},{1,3},{3,1},... | collective-permute-start | bytes 393224 | tf_op jit(solution)/shard_map/ppermute | solution.py:330
  12.1 8.3 %collective-permute-start.4 = (bf16[128,512]{1,0:T(8,128)(2,1)S(1)}, bf16[128,512]{1,0:T(8,128)(2,1)S(1)}, u32[]{:S(2)}, u32[]{:S(2)}) collective-permute-start(bf16[128,512]{1,0:T(8,128)(2,1)S(1)} %add_convert_fusion.refs_0_), channel_id=1, source_target_pairs={{0,8},{2,10},{4,12},{6,14},{8,0},{10,2},{12,4},{14,6},{1,9},{3,11}... | collective-permute-start | bytes 393224 | tf_op jit(solution)/shard_map/ppermute | solution.py:330
  14.9 8.5 %collective-permute-start.3 = (bf16[128,512]{1,0:T(8,128)(2,1)S(1)}, bf16[128,512]{1,0:T(8,128)(2,1)S(1)}, u32[]{:S(2)}, u32[]{:S(2)}) collective-permute-start(bf16[128,512]{1,0:T(8,128)(2,1)S(1)} %add_convert_fusion.refs_0_), channel_id=1, source_target_pairs={{0,6},{2,4},{4,2},{6,0},{8,14},{10,12},{12,10},{14,8},{1,7},{3,5},... | collective-permute-start | bytes 393224 | tf_op jit(solution)/shard_map/ppermute | solution.py:330
  16.9 8.0 %collective-permute-start.2 = (bf16[128,512]{1,0:T(8,128)(2,1)S(1)}, bf16[128,512]{1,0:T(8,128)(2,1)S(1)}, u32[]{:S(2)}, u32[]{:S(2)}) collective-permute-start(bf16[128,512]{1,0:T(8,128)(2,1)S(1)} %add_convert_fusion.refs_0_), channel_id=1, source_target_pairs={{0,4},{2,6},{4,0},{6,2},{8,12},{10,14},{12,8},{14,10},{1,5},{3,7},... | collective-permute-start | bytes 393224 | tf_op jit(solution)/shard_map/ppermute | solution.py:330
  17.3 7.6 %collective-permute-start.1 = (bf16[128,512]{1,0:T(8,128)(2,1)S(1)}, bf16[128,512]{1,0:T(8,128)(2,1)S(1)}, u32[]{:S(2)}, u32[]{:S(2)}) collective-permute-start(bf16[128,512]{1,0:T(8,128)(2,1)S(1)} %add_convert_fusion.refs_0_), channel_id=1, source_target_pairs={{0,2},{2,0},{4,6},{6,4},{8,10},{10,8},{12,14},{14,12},{1,3},{3,1},... | collective-permute-start | bytes 393224 | tf_op jit(solution)/shard_map/ppermute | solution.py:330
  20.3 8.7 %collective-permute-start.7 = (bf16[128,512]{1,0:T(8,128)(2,1)S(1)}, bf16[128,512]{1,0:T(8,128)(2,1)S(1)}, u32[]{:S(2)}, u32[]{:S(2)}) collective-permute-start(bf16[128,512]{1,0:T(8,128)(2,1)S(1)} %collective-permute-done.4.refs_4_), channel_id=1, source_target_pairs={{0,6},{2,4},{4,2},{6,0},{8,14},{10,12},{12,10},{14,8},{1,7},{3,5},... | collective-permute-start | bytes 393224 | tf_op jit(solution)/shard_map/ppermute | solution.py:330
  21.6 8.0 %collective-permute-start.6 = (bf16[128,512]{1,0:T(8,128)(2,1)S(1)}, bf16[128,512]{1,0:T(8,128)(2,1)S(1)}, u32[]{:S(2)}, u32[]{:S(2)}) collective-permute-start(bf16[128,512]{1,0:T(8,128)(2,1)S(1)} %collective-permute-done.4.refs_4_), channel_id=1, source_target_pairs={{0,4},{2,6},{4,0},{6,2},{8,12},{10,14},{12,8},{14,10},{1,5},{3,7},... | collective-permute-start | bytes 393224 | tf_op jit(solution)/shard_map/ppermute | solution.py:330
  23.4 6.4 %collective-permute-start.5 = (bf16[128,512]{1,0:T(8,128)(2,1)S(1)}, bf16[128,512]{1,0:T(8,128)(2,1)S(1)}, u32[]{:S(2)}, u32[]{:S(2)}) collective-permute-start(bf16[128,512]{1,0:T(8,128)(2,1)S(1)} %collective-permute-done.4.refs_4_), channel_id=1, source_target_pairs={{0,2},{2,0},{4,6},{6,4},{8,10},{10,8},{12,14},{14,12},{1,3},{3,1},... | collective-permute-start | bytes 393224 | tf_op jit(solution)/shard_map/ppermute | solution.py:330
  24.9 5.4 %collective-permute-start.8 = (bf16[128,512]{1,0:T(8,128)(2,1)S(1)}, bf16[128,512]{1,0:T(8,128)(2,1)S(1)}, u32[]{:S(2)}, u32[]{:S(2)}) collective-permute-start(bf16[128,512]{1,0:T(8,128)(2,1)S(1)} %add_convert_fusion.refs_0_), channel_id=1, source_target_pairs={{0,1},{1,0},{2,3},{3,2},{4,5},{5,4},{6,7},{7,6},{8,9},{9,8},{10,11... | collective-permute-start | bytes 393224 | tf_op jit(solution)/shard_map/ppermute | solution.py:346
  24.9 5.4 %collective-permute-start.12 = (bf16[128,512]{1,0:T(8,128)(2,1)S(1)}, bf16[128,512]{1,0:T(8,128)(2,1)S(1)}, u32[]{:S(2)}, u32[]{:S(2)}) collective-permute-start(bf16[128,512]{1,0:T(8,128)(2,1)S(1)} %collective-permute-done.4.refs_4_), channel_id=1, source_target_pairs={{0,1},{1,0},{2,3},{3,2},{4,5},{5,4},{6,7},{7,6},{8,9},{9,8},{10,11... | collective-permute-start | bytes 393224 | tf_op jit(solution)/shard_map/ppermute | solution.py:346
  29.0 1.8 %collective-permute-start.15 = (bf16[128,512]{1,0:T(8,128)(2,1)S(1)}, bf16[128,512]{1,0:T(8,128)(2,1)S(1)}, u32[]{:S(2)}, u32[]{:S(2)}) collective-permute-start(bf16[128,512]{1,0:T(8,128)(2,1)S(1)} %collective-permute-done.7.refs_7_), channel_id=1, source_target_pairs={{0,1},{1,0},{2,3},{3,2},{4,5},{5,4},{6,7},{7,6},{8,9},{9,8},{10,11... | collective-permute-start | bytes 393224 | tf_op jit(solution)/shard_map/ppermute | solution.py:346
  29.8 1.3 %collective-permute-start.9 = (bf16[128,512]{1,0:T(8,128)(2,1)S(1)}, bf16[128,512]{1,0:T(8,128)(2,1)S(1)}, u32[]{:S(2)}, u32[]{:S(2)}) collective-permute-start(bf16[128,512]{1,0:T(8,128)(2,1)S(1)} %collective-permute-done.1.refs_1_), channel_id=1, source_target_pairs={{0,1},{1,0},{2,3},{3,2},{4,5},{5,4},{6,7},{7,6},{8,9},{9,8},{10,11... | collective-permute-start | bytes 393224 | tf_op jit(solution)/shard_map/ppermute | solution.py:346
  29.8 1.5 %collective-permute-start.10 = (bf16[128,512]{1,0:T(8,128)(2,1)S(1)}, bf16[128,512]{1,0:T(8,128)(2,1)S(1)}, u32[]{:S(2)}, u32[]{:S(2)}) collective-permute-start(bf16[128,512]{1,0:T(8,128)(2,1)S(1)} %collective-permute-done.2.refs_2_), channel_id=1, source_target_pairs={{0,1},{1,0},{2,3},{3,2},{4,5},{5,4},{6,7},{7,6},{8,9},{9,8},{10,11... | collective-permute-start | bytes 393224 | tf_op jit(solution)/shard_map/ppermute | solution.py:346
  30.3 1.3 %collective-permute-start.11 = (bf16[128,512]{1,0:T(8,128)(2,1)S(1)}, bf16[128,512]{1,0:T(8,128)(2,1)S(1)}, u32[]{:S(2)}, u32[]{:S(2)}) collective-permute-start(bf16[128,512]{1,0:T(8,128)(2,1)S(1)} %collective-permute-done.3.refs_3_), channel_id=1, source_target_pairs={{0,1},{1,0},{2,3},{3,2},{4,5},{5,4},{6,7},{7,6},{8,9},{9,8},{10,11... | collective-permute-start | bytes 393224 | tf_op jit(solution)/shard_map/ppermute | solution.py:346
  30.3 1.5 %collective-permute-start.13 = (bf16[128,512]{1,0:T(8,128)(2,1)S(1)}, bf16[128,512]{1,0:T(8,128)(2,1)S(1)}, u32[]{:S(2)}, u32[]{:S(2)}) collective-permute-start(bf16[128,512]{1,0:T(8,128)(2,1)S(1)} %collective-permute-done.5.refs_5_), channel_id=1, source_target_pairs={{0,1},{1,0},{2,3},{3,2},{4,5},{5,4},{6,7},{7,6},{8,9},{9,8},{10,11... | collective-permute-start | bytes 393224 | tf_op jit(solution)/shard_map/ppermute | solution.py:346
  30.8 1.3 %collective-permute-start.14 = (bf16[128,512]{1,0:T(8,128)(2,1)S(1)}, bf16[128,512]{1,0:T(8,128)(2,1)S(1)}, u32[]{:S(2)}, u32[]{:S(2)}) collective-permute-start(bf16[128,512]{1,0:T(8,128)(2,1)S(1)} %collective-permute-done.6.refs_6_), channel_id=1, source_target_pairs={{0,1},{1,0},{2,3},{3,2},{4,5},{5,4},{6,7},{7,6},{8,9},{9,8},{10,11... | collective-permute-start | bytes 393224 | tf_op jit(solution)/shard_map/ppermute | solution.py:346
